TPU v7x, 32 devices: a whole 2x2x4 slice. The times are simulated.
32 devices in a mesh: chain: 4 (over y, x), gx: 2 (over core), gy: 4 (over z).
Axes of the slice: x: 2, y: 2, z: 4, core: 2. Of those that a mesh axis runs over, the one named last changes fastest.
Arguments:
- initial_path: float32 [8, 64, 96, 256], P('chain', 'gx', 'gy'), may hold values from -3 to 3, as said below
Outputs:
- relaxed_path: float32 [8, 64, 96, 256], P('chain', 'gx', 'gy')
Inputs may be any that keep to these rules, and one draw needn't show every extreme that they name: `initial_path`: each image lies near a point of a path between the two end states, with image-to-image noise.
All inputs are finite; a program needn't handle non-finite values.
Results may differ from a plain program's by a relative error of at most 0.00013.
Values sent between devices are 32-bit elements; how exact they have to be, the bound alone decides.
No kernel may reach another device: no remote copies, remote signals or barrier semaphores. Data moves between devices by JAX's collectives and lax.ppermute only.
A program may use at most 64 MiB of HBM per device.

v0:
```python
import jax
import jax.numpy as jnp
from jax import lax
from jax.sharding import PartitionSpec as P

RELAX = 3


spacing = 0.7853981633974483
undercool = -0.25
time_step = 0.00025
step_size = 0.002
stiffness = 0.5
epsilon = 1e-06


def padded_2(block, sides, width):
    for axis, dim in sides:
        count = lax.axis_size(axis)
        forward = [(i, i + 1) for i in range(count - 1)]
        forward.append((count - 1, 0))
        backward = [(target, source) for source, target in forward]
        low = lax.ppermute(
            lax.slice_in_dim(block, block.shape[dim] - width, None, axis=dim), axis, forward
        )
        high = lax.ppermute(lax.slice_in_dim(block, 0, width, axis=dim), axis, backward)
        block = jnp.concatenate([low, block, high], axis=dim)
    return block


def shifted(block, axis, distance):
    devices = range(lax.axis_size(axis))
    route = [(i - distance, i) for i in devices if i - distance in devices]
    return lax.ppermute(block, axis, route)


def inner_lap(padded):
    centre = padded[:, 1:-1, 1:-1]
    total = padded[:, 2:, 1:-1] + padded[:, :-2, 1:-1] + padded[:, 1:-1, 2:] + padded[:, 1:-1, :-2]
    total = total + jnp.roll(centre, -1, 3) + jnp.roll(centre, 1, 3)
    return (total - 6.0 * centre) / (spacing * spacing)


def deep_potential(field):
    padded = padded_2(field, (("gx", 1), ("gy", 2)), 3)
    first_lap = inner_lap(padded)
    second_lap = inner_lap(first_lap)
    centre = padded[:, 2:-2, 2:-2]
    return (
        (1.0 + undercool) * centre
        + 2.0 * first_lap[:, 1:-1, 1:-1]
        + second_lap
        + centre * centre * centre
    )


def relax_once(field):
    return field + time_step * inner_lap(deep_potential(field))


def chemical_of(field):
    return deep_potential(field)[:, 1:-1, 1:-1]


def per_device(initial_path):
    count = initial_path.shape[0]
    cells = (
        initial_path.shape[1]
        * lax.axis_size("gx")
        * initial_path.shape[2]
        * lax.axis_size("gy")
        * initial_path.shape[3]
    )
    images = count * lax.axis_size("chain")
    global_index = lax.axis_index("chain") * count + jnp.arange(count, dtype=jnp.int32)
    keeping = jnp.logical_or(global_index == 0, global_index == images - 1)
    field = initial_path
    for relax_turn in range(RELAX):
        field = relax_once(field)
    chemical = chemical_of(field)
    from_lower = shifted(field[-1:], "chain", 1)
    from_upper = shifted(field[:1], "chain", -1)
    extended = jnp.concatenate([from_lower, field, from_upper], axis=0)
    before = extended[:-2]
    after = extended[2:]
    tangent = after - before
    forward = after - field
    backward = field - before
    tangent_part = jnp.sum(tangent * tangent, axis=(1, 2, 3))
    forward_part = jnp.sum(forward * forward, axis=(1, 2, 3))
    backward_part = jnp.sum(backward * backward, axis=(1, 2, 3))
    tangent_sq, forward_sq, backward_sq = lax.psum(
        (tangent_part, forward_part, backward_part), ("gx", "gy")
    )
    scale = 1.0 / jnp.sqrt(tangent_sq / cells + epsilon)
    unit = tangent * scale[:, None, None, None]
    along = lax.psum(jnp.sum(chemical * unit, axis=(1, 2, 3)), ("gx", "gy")) / cells
    spring = stiffness * (
        jnp.sqrt(forward_sq / cells + epsilon) - jnp.sqrt(backward_sq / cells + epsilon)
    )
    moved = (
        field
        + step_size * (along[:, None, None, None] * unit - chemical)
        + spring[:, None, None, None] * unit
    )
    field = jnp.where(keeping[:, None, None, None], field, moved)
    return field


def solution(mesh):
    return jax.shard_map(
        per_device,
        mesh=mesh,
        in_specs=(P("chain", "gx", "gy", None),),
        out_specs=P("chain", "gx", "gy", None),
        check_vma=False,
    )
```

profile of v0, /device:TPU:5, one launch (start us, length us, event | category | flops | bytes accessed | tf_op | source)
XLA Modules:
  0.0 167.3 jit_solution(4694701738445298914)
XLA Ops:
  0.0 1.9 %copy.5 = f32[2,32,24,256]{3,1,2,0:T(8,128)S(1)} copy(f32[2,32,24,256]{3,2,1,0:T(8,128)} %param.1) | data formatting | bytes 3145728 | tf_op args[0]
  2.8 1.0 collective-permute-done
  4.2 1.3 collective-permute-start.2
  5.6 2.1 %collective-permute-start.3 = (f32[2,38,3,256]{3,1,2,0:T(8,128)S(1)}, f32[2,38,3,256]{3,1,2,0:T(8,128)S(1)}, u32[]{:S(2)}, u32[]{:S(2)}) collective-permute-start(f32[2,38,3,256]{3,1,2,0:T(8,128)S(1)} %get-tuple-element.65), channel_id=1, source_target_pairs={{1,0},{2,1},{3,2},{0,3},{5,4},{6,5},{7,6},{4,7},{9,8},{10,9},{11,1... | collective-permute-start | bytes 700424 | tf_op jit(solution)/shard_map/ppermute | solution.py:26
  7.7 5.9 %collective-permute-done.2 = f32[2,38,3,256]{3,1,2,0:T(8,128)S(1)} collective-permute-done((f32[2,38,3,256]{3,1,2,0:T(8,128)S(1)}, f32[2,38,3,256]{3,1,2,0:T(8,128)S(1)}, u32[]{:S(2)}, u32[]{:S(2)}) %collective-permute-start.2) | collective-permute-done | bytes 233504 | tf_op jit(solution)/shard_map/ppermute | solution.py:23
  13.5 4.6 %collective-permute-done.3 = f32[2,38,3,256]{3,1,2,0:T(8,128)S(1)} collective-permute-done((f32[2,38,3,256]{3,1,2,0:T(8,128)S(1)}, f32[2,38,3,256]{3,1,2,0:T(8,128)S(1)}, u32[]{:S(2)}, u32[]{:S(2)}) %collective-permute-start.3) | collective-permute-done | bytes 233504 | tf_op jit(solution)/shard_map/ppermute | solution.py:26
  18.4 0.8 fusion.71
  19.7 2.3 %fusion.13 = f32[2,36,28,256]{3,1,2,0:T(8,128)S(1)} fusion(f32[2,38,30,256]{3,1,2,0:T(8,128)S(1)} %pad_maximum_fusion, f32[2,36,28,1]{3,1,2,0:T(8,128)S(1)} %get-tuple-element.25, f32[2,36,28,255]{3,1,2,0:T(8,128)S(1)} %get-tuple-element.27, f32[2,36,28,255]{3,1,2,0:T(8,128)S(1)} %get-tuple-element.26, f32[2,36,28,1]{3,1,2,0:T(8,128)S(1)} %get-tuple-element.24), kind=kLoop, calls=%fused_computation.34 | loop fusion | flops 5160960 | bytes 16515072 | tf_op jit(solution)/shard_map/div | solution.py:41
  23.1 2.7 %fusion.16 = f32[2,34,26,256]{3,1,2,0:T(8,128)S(1)} fusion(f32[2,36,28,256]{3,1,2,0:T(8,128)S(1)} %fusion.13, f32[2,34,26,1]{3,1,2,0:T(8,128)S(1)} %get-tuple-element.43, f32[2,34,26,255]{3,1,2,0:T(8,128)S(1)} %get-tuple-element.45, f32[2,34,26,255]{3,1,2,0:T(8,128)S(1)} %get-tuple-element.44, f32[2,34,26,1]{3,1,2,0:T(8,128)S(1)} %get-tuple-element.42, ...), kind=kLoop, calls=%fused_computation.40 | loop fusion | flops 7694336 | bytes 16293888 | tf_op jit(solution)/shard_map/add | solution.py:50
  26.8 1.1 copy-done
  27.9 1.4 fusion.60
  29.3 1.1 collective-permute-start.4
  30.5 1.0 collective-permute-done.4
  32.0 0.9 collective-permute-start.6
  32.9 2.4 %collective-permute-start.7 = (f32[2,38,3,256]{3,1,2,0:T(8,128)S(1)}, f32[2,38,3,256]{3,1,2,0:T(8,128)S(1)}, u32[]{:S(2)}, u32[]{:S(2)}) collective-permute-start(f32[2,38,3,256]{3,1,2,0:T(8,128)S(1)} %get-tuple-element.63), channel_id=1, source_target_pairs={{1,0},{2,1},{3,2},{0,3},{5,4},{6,5},{7,6},{4,7},{9,8},{10,9},{11,1... | collective-permute-start | bytes 700424 | tf_op jit(solution)/shard_map/ppermute | solution.py:26
  35.3 5.9 %collective-permute-done.6 = f32[2,38,3,256]{3,1,2,0:T(8,128)S(1)} collective-permute-done((f32[2,38,3,256]{3,1,2,0:T(8,128)S(1)}, f32[2,38,3,256]{3,1,2,0:T(8,128)S(1)}, u32[]{:S(2)}, u32[]{:S(2)}) %collective-permute-start.6) | collective-permute-done | bytes 233504 | tf_op jit(solution)/shard_map/ppermute | solution.py:23
  41.1 4.0 %collective-permute-done.7 = f32[2,38,3,256]{3,1,2,0:T(8,128)S(1)} collective-permute-done((f32[2,38,3,256]{3,1,2,0:T(8,128)S(1)}, f32[2,38,3,256]{3,1,2,0:T(8,128)S(1)}, u32[]{:S(2)}, u32[]{:S(2)}) %collective-permute-start.7) | collective-permute-done | bytes 233504 | tf_op jit(solution)/shard_map/ppermute | solution.py:26
  45.4 0.8 fusion.69
  46.7 2.3 %fusion.9 = f32[2,36,28,256]{3,1,2,0:T(8,128)S(1)} fusion(f32[2,38,30,256]{3,1,2,0:T(8,128)S(1)} %pad_maximum_fusion.1, f32[2,36,28,1]{3,1,2,0:T(8,128)S(1)} %get-tuple-element.21, f32[2,36,28,255]{3,1,2,0:T(8,128)S(1)} %get-tuple-element.23, f32[2,36,28,255]{3,1,2,0:T(8,128)S(1)} %get-tuple-element.22, f32[2,36,28,1]{3,1,2,0:T(8,128)S(1)} %get-tuple-element.20), kind=kLoop, calls=%fused_computation.26 | loop fusion | flops 5160960 | bytes 16515072 | tf_op jit(solution)/shard_map/div | solution.py:41
  50.1 2.7 %fusion.17 = f32[2,34,26,256]{3,1,2,0:T(8,128)S(1)} fusion(f32[2,36,28,256]{3,1,2,0:T(8,128)S(1)} %fusion.9, f32[2,34,26,1]{3,1,2,0:T(8,128)S(1)} %get-tuple-element.39, f32[2,34,26,255]{3,1,2,0:T(8,128)S(1)} %get-tuple-element.41, f32[2,34,26,255]{3,1,2,0:T(8,128)S(1)} %get-tuple-element.40, f32[2,34,26,1]{3,1,2,0:T(8,128)S(1)} %get-tuple-element.38, ...), kind=kLoop, calls=%fused_computation.41 | loop fusion | flops 7694336 | bytes 16293888 | tf_op jit(solution)/shard_map/add | solution.py:50
  53.8 1.0 fusion.55
  54.9 1.5 collective-permute-start.8
  56.4 1.0 collective-permute-done.8
  58.4 2.8 %collective-permute-start.11 = (f32[2,38,3,256]{3,1,2,0:T(8,128)S(1)}, f32[2,38,3,256]{3,1,2,0:T(8,128)S(1)}, u32[]{:S(2)}, u32[]{:S(2)}) collective-permute-start(f32[2,38,3,256]{3,1,2,0:T(8,128)S(1)} %get-tuple-element.61), channel_id=1, source_target_pairs={{1,0},{2,1},{3,2},{0,3},{5,4},{6,5},{7,6},{4,7},{9,8},{10,9},{11,1... | collective-permute-start | bytes 700424 | tf_op jit(solution)/shard_map/ppermute | solution.py:26
  61.2 5.9 %collective-permute-done.10 = f32[2,38,3,256]{3,1,2,0:T(8,128)S(1)} collective-permute-done((f32[2,38,3,256]{3,1,2,0:T(8,128)S(1)}, f32[2,38,3,256]{3,1,2,0:T(8,128)S(1)}, u32[]{:S(2)}, u32[]{:S(2)}) %collective-permute-start.10) | collective-permute-done | bytes 233504 | tf_op jit(solution)/shard_map/ppermute | solution.py:23
  67.0 3.6 %collective-permute-done.11 = f32[2,38,3,256]{3,1,2,0:T(8,128)S(1)} collective-permute-done((f32[2,38,3,256]{3,1,2,0:T(8,128)S(1)}, f32[2,38,3,256]{3,1,2,0:T(8,128)S(1)}, u32[]{:S(2)}, u32[]{:S(2)}) %collective-permute-start.11) | collective-permute-done | bytes 233504 | tf_op jit(solution)/shard_map/ppermute | solution.py:26
  70.9 0.8 fusion.67
  72.2 2.3 %fusion.5 = f32[2,36,28,256]{3,1,2,0:T(8,128)S(1)} fusion(f32[2,38,30,256]{3,1,2,0:T(8,128)S(1)} %pad_maximum_fusion.2, f32[2,36,28,1]{3,1,2,0:T(8,128)S(1)} %get-tuple-element.17, f32[2,36,28,255]{3,1,2,0:T(8,128)S(1)} %get-tuple-element.19, f32[2,36,28,255]{3,1,2,0:T(8,128)S(1)} %get-tuple-element.18, f32[2,36,28,1]{3,1,2,0:T(8,128)S(1)} %get-tuple-element.16), kind=kLoop, calls=%fused_computation.18 | loop fusion | flops 5160960 | bytes 16515072 | tf_op jit(solution)/shard_map/div | solution.py:41
  75.6 2.7 %fusion.18 = f32[2,34,26,256]{3,1,2,0:T(8,128)S(1)} fusion(f32[2,36,28,256]{3,1,2,0:T(8,128)S(1)} %fusion.5, f32[2,34,26,1]{3,1,2,0:T(8,128)S(1)} %get-tuple-element.35, f32[2,34,26,255]{3,1,2,0:T(8,128)S(1)} %get-tuple-element.37, f32[2,34,26,255]{3,1,2,0:T(8,128)S(1)} %get-tuple-element.36, f32[2,34,26,1]{3,1,2,0:T(8,128)S(1)} %get-tuple-element.34, ...), kind=kLoop, calls=%fused_computation.42 | loop fusion | flops 7694336 | bytes 16293888 | tf_op jit(solution)/shard_map/add | solution.py:50
  79.3 1.0 fusion.50
  80.4 1.5 collective-permute-start.12
  81.9 1.0 collective-permute-done.12
  83.3 1.2 collective-permute-start.14
  84.5 2.2 %collective-permute-start.15 = (f32[2,38,3,256]{3,1,2,0:T(8,128)S(1)}, f32[2,38,3,256]{3,1,2,0:T(8,128)S(1)}, u32[]{:S(2)}, u32[]{:S(2)}) collective-permute-start(f32[2,38,3,256]{3,1,2,0:T(8,128)S(1)} %get-tuple-element.59), channel_id=1, source_target_pairs={{1,0},{2,1},{3,2},{0,3},{5,4},{6,5},{7,6},{4,7},{9,8},{10,9},{11,1... | collective-permute-start | bytes 700424 | tf_op jit(solution)/shard_map/ppermute | solution.py:26
  86.8 3.1 %collective-permute-start.16 = (f32[1,32,24,256]{3,1,2,0:T(8,128)S(1)}, f32[1,32,24,256]{3,1,2,0:T(8,128)S(1)}, u32[]{:S(2)}, u32[]{:S(2)}) collective-permute-start(f32[1,32,24,256]{3,1,2,0:T(8,128)S(1)} %get-tuple-element.68), channel_id=1, source_target_pairs={{8,0},{16,8},{24,16},{9,1},{17,9},{25,17},{10,2},{18,10},{26,18},{... | collective-permute-start | bytes 2359304 | tf_op jit(solution)/shard_map/ppermute | solution.py:34
  89.9 2.5 %collective-permute-start.17 = (f32[1,32,24,256]{3,1,2,0:T(8,128)S(1)}, f32[1,32,24,256]{3,1,2,0:T(8,128)S(1)}, u32[]{:S(2)}, u32[]{:S(2)}) collective-permute-start(f32[1,32,24,256]{3,1,2,0:T(8,128)S(1)} %get-tuple-element.69), channel_id=1, source_target_pairs={{0,8},{8,16},{16,24},{1,9},{9,17},{17,25},{2,10},{10,18},{18,26},{... | collective-permute-start | bytes 2359304 | tf_op jit(solution)/shard_map/ppermute | solution.py:34
  92.5 4.4 %collective-permute-done.15 = f32[2,38,3,256]{3,1,2,0:T(8,128)S(1)} collective-permute-done((f32[2,38,3,256]{3,1,2,0:T(8,128)S(1)}, f32[2,38,3,256]{3,1,2,0:T(8,128)S(1)}, u32[]{:S(2)}, u32[]{:S(2)}) %collective-permute-start.15) | collective-permute-done | bytes 233504 | tf_op jit(solution)/shard_map/ppermute | solution.py:26
  98.5 2.1 %fusion.1 = f32[2,36,28,256]{3,1,2,0:T(8,128)S(1)} fusion(f32[2,38,30,256]{3,1,2,0:T(8,128)S(1)} %pad_maximum_fusion.3, f32[2,36,28,1]{3,1,2,0:T(8,128)S(1)} %get-tuple-element.13, f32[2,36,28,255]{3,1,2,0:T(8,128)S(1)} %get-tuple-element.15, f32[2,36,28,255]{3,1,2,0:T(8,128)S(1)} %get-tuple-element.14, f32[2,36,28,1]{3,1,2,0:T(8,128)S(1)} %get-tuple-element.12), kind=kLoop, calls=%fused_computation.10 | loop fusion | flops 5160960 | bytes 16515072 | tf_op jit(solution)/shard_map/div | solution.py:41
  100.7 1.8 %fusion.74 = (f32[2,34,26,1]{3,1,2,0:T(8,128)}, f32[2,34,26,1]{3,1,2,0:T(8,128)}) fusion(f32[2,36,28,256]{3,1,2,0:T(8,128)S(1)} %fusion.1), kind=kLoop, calls=%fused_computation.145 | loop fusion | bytes 28288 | tf_op jit(solution)/shard_map/jit(_roll_static)/slice | solution.py:40
  102.4 2.5 %fusion.72 = (f32[2,34,26,256]{3,1,2,0:T(8,128)}, f32[2,34,26,256]{3,1,2,0:T(8,128)}) fusion(f32[2,36,28,256]{3,1,2,0:T(8,128)S(1)} %fusion.1), kind=kLoop, calls=%fused_computation.143 | loop fusion | flops 1357824 | bytes 12673024 | tf_op jit(solution)/shard_map/slice | solution.py:51
  105.0 2.7 %fusion.73 = (f32[2,34,26,255]{3,1,2,0:T(8,128)}, f32[2,34,26,255]{3,1,2,0:T(8,128)}) fusion(f32[2,36,28,256]{3,1,2,0:T(8,128)S(1)} %fusion.1), kind=kLoop, calls=%fused_computation.144 | loop fusion | bytes 7213440 | tf_op jit(solution)/shard_map/jit(_roll_static)/slice | solution.py:40
  107.7 16.0 %collective-permute-done.17 = f32[1,32,24,256]{3,1,2,0:T(8,128)S(1)} collective-permute-done((f32[1,32,24,256]{3,1,2,0:T(8,128)S(1)}, f32[1,32,24,256]{3,1,2,0:T(8,128)S(1)}, u32[]{:S(2)}, u32[]{:S(2)}) %collective-permute-start.17) | collective-permute-done | bytes 786464 | tf_op jit(solution)/shard_map/ppermute | solution.py:34
  124.2 1.5 slice.650
  125.7 15.3 %psum.28 = f32[2]{0:T(128)S(1)} all-reduce(f32[2]{0:T(128)S(1)} %multiply_reduce_fusion.1), channel_id=1, replica_groups=mesh['chain'=4,'gx'=2,'gy'=4] {'gx','gy'}, use_global_device_ids=true, to_apply=%region_1.2 | all-reduce | flops 2 | bytes 16 | tf_op jit(solution)/shard_map/psum | solution.py:92
  141.0 6.6 %multiply_reduce_fusion = (f32[2]{0:T(128)S(1)}, f32[2]{0:T(128)S(1)}, f32[2]{0:T(128)S(1)}, f32[2,32,24,256]{3,1,2,0:T(8,128)}) fusion(f32[2]{0:T(128)S(1)} %add_rsqrt_fusion, f32[2,32,24,256]{3,1,2,0:T(8,128)S(1)} %fusion.50, f32[1,32,24,256]{3,1,2,0:T(8,128)S(1)} %collective-permute-done.17, f32[1,32,24,256]{3,1,2,0:T(8,128)S(1)} %collective-permute-done.16, ...), kind=kLoop, calls=%fused_computation.117 | loop fusion | flops 10223610 | bytes 13058080 | tf_op jit(solution)/shard_map/reduce_sum | solution.py:97
  147.6 15.7 %all-reduce = (f32[2]{0:T(128)S(1)}, f32[2]{0:T(128)S(1)}, f32[2]{0:T(128)S(1)}) all-reduce(f32[2]{0:T(128)S(1)} %get-tuple-element.6, f32[2]{0:T(128)S(1)} %get-tuple-element.7, f32[2]{0:T(128)S(1)} %get-tuple-element.5), channel_id=1, replica_groups=mesh['chain'=4,'gx'=2,'gy'=4] {'gx','gy'}, use_global_device_ids=true, to_apply=%region_7.8 | all-reduce | flops 6 | bytes 48 | tf_op jit(solution)/shard_map/psum | solution.py:92
  163.2 2.0 %add_select_fusion = f32[2,32,24,256]{3,1,2,0:T(8,128)S(1)} fusion(f32[2,32,24,256]{3,1,2,0:T(8,128)S(1)} %fusion.50, f32[2,32,24,256]{3,1,2,0:T(8,128)} %get-tuple-element.11, f32[2]{0:T(128)S(1)} %get-tuple-element.76, f32[2]{0:T(128)S(1)} %get-tuple-element.77, f32[2]{0:T(128)S(1)} %add_rsqrt_fusion, pred[2]{0:T(512)(128)(4,1)S(1)} %compare_or_fusion, ...), kind=kLoop, calls=%fused_computation.116 | loop fusion | flops 4325376 | bytes 6291482 | tf_op jit(solution)/shard_map/jit(_where)/select_n | solution.py:106
  165.3 2.1 %copy.6 = f32[2,32,24,256]{3,2,1,0:T(8,128)} copy(f32[2,32,24,256]{3,1,2,0:T(8,128)S(1)} %add_select_fusion) | data formatting | bytes 3145728 | tf_op jit(solution)/shard_map/jit(_where)/select_n | solution.py:106
  (47 shorter events, 14.3 us)
Async XLA Ops:
  2.0 1.8 %collective-permute-start = (f32[2,3,24,256]{3,1,2,0:T(4,128)S(1)}, f32[2,3,24,256]{3,1,2,0:T(4,128)S(1)}, u32[]{:S(2)}, u32[]{:S(2)}) collective-permute-start(f32[2,3,24,256]{3,1,2,0:T(4,128)S(1)} %get-tuple-element.74), channel_id=1, source_target_pairs={{0,4},{4,0},{1,5},{5,1},{2,6},{6,2},{3,7},{7,3},{8,12},{12,8},{9,1... | collective-permute-start | bytes 442376 | tf_op jit(solution)/shard_map/ppermute | solution.py:23
  2.7 1.4 collective-permute-start.1
  4.2 9.3 %collective-permute-start.2 = (f32[2,38,3,256]{3,1,2,0:T(8,128)S(1)}, f32[2,38,3,256]{3,1,2,0:T(8,128)S(1)}, u32[]{:S(2)}, u32[]{:S(2)}) collective-permute-start(f32[2,38,3,256]{3,1,2,0:T(8,128)S(1)} %get-tuple-element.64), channel_id=1, source_target_pairs={{0,1},{1,2},{2,3},{3,0},{4,5},{5,6},{6,7},{7,4},{8,9},{9,10},{10,1... | collective-permute-start | bytes 700424 | tf_op jit(solution)/shard_map/ppermute | solution.py:23
  5.6 12.6 %collective-permute-start.3 = (f32[2,38,3,256]{3,1,2,0:T(8,128)S(1)}, f32[2,38,3,256]{3,1,2,0:T(8,128)S(1)}, u32[]{:S(2)}, u32[]{:S(2)}) collective-permute-start(f32[2,38,3,256]{3,1,2,0:T(8,128)S(1)} %get-tuple-element.65), channel_id=1, source_target_pairs={{1,0},{2,1},{3,2},{0,3},{5,4},{6,5},{7,6},{4,7},{9,8},{10,9},{11,1... | collective-permute-start | bytes 700424 | tf_op jit(solution)/shard_map/ppermute | solution.py:26
  26.5 1.4 copy-start
  29.3 2.2 %collective-permute-start.4 = (f32[2,3,24,256]{3,1,2,0:T(4,128)S(1)}, f32[2,3,24,256]{3,1,2,0:T(4,128)S(1)}, u32[]{:S(2)}, u32[]{:S(2)}) collective-permute-start(f32[2,3,24,256]{3,1,2,0:T(4,128)S(1)} %get-tuple-element.72), channel_id=1, source_target_pairs={{0,4},{4,0},{1,5},{5,1},{2,6},{6,2},{3,7},{7,3},{8,12},{12,8},{9,1... | collective-permute-start | bytes 442376 | tf_op jit(solution)/shard_map/ppermute | solution.py:23
  30.5 1.4 collective-permute-start.5
  32.0 9.2 %collective-permute-start.6 = (f32[2,38,3,256]{3,1,2,0:T(8,128)S(1)}, f32[2,38,3,256]{3,1,2,0:T(8,128)S(1)}, u32[]{:S(2)}, u32[]{:S(2)}) collective-permute-start(f32[2,38,3,256]{3,1,2,0:T(8,128)S(1)} %get-tuple-element.62), channel_id=1, source_target_pairs={{0,1},{1,2},{2,3},{3,0},{4,5},{5,6},{6,7},{7,4},{8,9},{9,10},{10,1... | collective-permute-start | bytes 700424 | tf_op jit(solution)/shard_map/ppermute | solution.py:23
  32.9 12.2 %collective-permute-start.7 = (f32[2,38,3,256]{3,1,2,0:T(8,128)S(1)}, f32[2,38,3,256]{3,1,2,0:T(8,128)S(1)}, u32[]{:S(2)}, u32[]{:S(2)}) collective-permute-start(f32[2,38,3,256]{3,1,2,0:T(8,128)S(1)} %get-tuple-element.63), channel_id=1, source_target_pairs={{1,0},{2,1},{3,2},{0,3},{5,4},{6,5},{7,6},{4,7},{9,8},{10,9},{11,1... | collective-permute-start | bytes 700424 | tf_op jit(solution)/shard_map/ppermute | solution.py:26
  54.9 2.5 %collective-permute-start.8 = (f32[2,3,24,256]{3,1,2,0:T(4,128)S(1)}, f32[2,3,24,256]{3,1,2,0:T(4,128)S(1)}, u32[]{:S(2)}, u32[]{:S(2)}) collective-permute-start(f32[2,3,24,256]{3,1,2,0:T(4,128)S(1)} %get-tuple-element.70), channel_id=1, source_target_pairs={{0,4},{4,0},{1,5},{5,1},{2,6},{6,2},{3,7},{7,3},{8,12},{12,8},{9,1... | collective-permute-start | bytes 442376 | tf_op jit(solution)/shard_map/ppermute | solution.py:23
  56.3 1.4 collective-permute-start.9
  57.9 9.2 %collective-permute-start.10 = (f32[2,38,3,256]{3,1,2,0:T(8,128)S(1)}, f32[2,38,3,256]{3,1,2,0:T(8,128)S(1)}, u32[]{:S(2)}, u32[]{:S(2)}) collective-permute-start(f32[2,38,3,256]{3,1,2,0:T(8,128)S(1)} %get-tuple-element.60), channel_id=1, source_target_pairs={{0,1},{1,2},{2,3},{3,0},{4,5},{5,6},{6,7},{7,4},{8,9},{9,10},{10,1... | collective-permute-start | bytes 700424 | tf_op jit(solution)/shard_map/ppermute | solution.py:23
  58.4 12.2 %collective-permute-start.11 = (f32[2,38,3,256]{3,1,2,0:T(8,128)S(1)}, f32[2,38,3,256]{3,1,2,0:T(8,128)S(1)}, u32[]{:S(2)}, u32[]{:S(2)}) collective-permute-start(f32[2,38,3,256]{3,1,2,0:T(8,128)S(1)} %get-tuple-element.61), channel_id=1, source_target_pairs={{1,0},{2,1},{3,2},{0,3},{5,4},{6,5},{7,6},{4,7},{9,8},{10,9},{11,1... | collective-permute-start | bytes 700424 | tf_op jit(solution)/shard_map/ppermute | solution.py:26
  80.4 2.6 %collective-permute-start.12 = (f32[2,3,24,256]{3,1,2,0:T(4,128)S(1)}, f32[2,3,24,256]{3,1,2,0:T(4,128)S(1)}, u32[]{:S(2)}, u32[]{:S(2)}) collective-permute-start(f32[2,3,24,256]{3,1,2,0:T(4,128)S(1)} %get-tuple-element.66), channel_id=1, source_target_pairs={{0,4},{4,0},{1,5},{5,1},{2,6},{6,2},{3,7},{7,3},{8,12},{12,8},{9,1... | collective-permute-start | bytes 442376 | tf_op jit(solution)/shard_map/ppermute | solution.py:23
  81.8 1.4 collective-permute-start.13
  83.3 9.2 %collective-permute-start.14 = (f32[2,38,3,256]{3,1,2,0:T(8,128)S(1)}, f32[2,38,3,256]{3,1,2,0:T(8,128)S(1)}, u32[]{:S(2)}, u32[]{:S(2)}) collective-permute-start(f32[2,38,3,256]{3,1,2,0:T(8,128)S(1)} %get-tuple-element.58), channel_id=1, source_target_pairs={{0,1},{1,2},{2,3},{3,0},{4,5},{5,6},{6,7},{7,4},{8,9},{9,10},{10,1... | collective-permute-start | bytes 700424 | tf_op jit(solution)/shard_map/ppermute | solution.py:23
  84.5 12.4 %collective-permute-start.15 = (f32[2,38,3,256]{3,1,2,0:T(8,128)S(1)}, f32[2,38,3,256]{3,1,2,0:T(8,128)S(1)}, u32[]{:S(2)}, u32[]{:S(2)}) collective-permute-start(f32[2,38,3,256]{3,1,2,0:T(8,128)S(1)} %get-tuple-element.59), channel_id=1, source_target_pairs={{1,0},{2,1},{3,2},{0,3},{5,4},{6,5},{7,6},{4,7},{9,8},{10,9},{11,1... | collective-permute-start | bytes 700424 | tf_op jit(solution)/shard_map/ppermute | solution.py:26
  86.8 20.9 %collective-permute-start.16 = (f32[1,32,24,256]{3,1,2,0:T(8,128)S(1)}, f32[1,32,24,256]{3,1,2,0:T(8,128)S(1)}, u32[]{:S(2)}, u32[]{:S(2)}) collective-permute-start(f32[1,32,24,256]{3,1,2,0:T(8,128)S(1)} %get-tuple-element.68), channel_id=1, source_target_pairs={{8,0},{16,8},{24,16},{9,1},{17,9},{25,17},{10,2},{18,10},{26,18},{... | collective-permute-start | bytes 2359304 | tf_op jit(solution)/shard_map/ppermute | solution.py:34
  89.9 33.8 %collective-permute-start.17 = (f32[1,32,24,256]{3,1,2,0:T(8,128)S(1)}, f32[1,32,24,256]{3,1,2,0:T(8,128)S(1)}, u32[]{:S(2)}, u32[]{:S(2)}) collective-permute-start(f32[1,32,24,256]{3,1,2,0:T(8,128)S(1)} %get-tuple-element.69), channel_id=1, source_target_pairs={{0,8},{8,16},{16,24},{1,9},{9,17},{17,25},{2,10},{10,18},{18,26},{... | collective-permute-start | bytes 2359304 | tf_op jit(solution)/shard_map/ppermute | solution.py:34
where the time goes:
time: 168 us; the launch traced here: 167 us
  waiting for transfers between devices  55.7 us (33%)
  other arithmetic  33.6 us (20%)
  blocking collectives  30.9 us (18%)
  starting transfers between devices  24.1 us (14%)
  local copies, waits for them, and re-layouts  22.5 us (13%)
    psum x2, blocking collectives, per_device(): lax.psum((tangent_part, forward_part, backward_part), ('gx', 'gy'))  30.9 us
    ppermute x8, waiting for transfers between devices, padded_2(): lax.ppermute(lax.slice_in_dim(block, block.shape[dim] - width, None, axis...  21.7 us
    ppermute x8, waiting for transfers between devices, padded_2(): lax.ppermute(lax.slice_in_dim(block, 0, width, axis=dim), axis, backward)  18 us
    ppermute x2, waiting for transfers between devices, shifted(): return lax.ppermute(block, axis, route)  16 us
    slice x22, local copies, waits for them, and re-layouts, inner_lap(): total = total + jnp.roll(centre, -1, 3) + jnp.roll(centre, 1, 3)  15.6 us
    ppermute x8, starting transfers between devices, padded_2(): lax.ppermute(lax.slice_in_dim(block, 0, width, axis=dim), axis, backward)  9.79 us
    div x4, other arithmetic, inner_lap(): return (total - 6.0 * centre) / (spacing * spacing)  9.01 us
    ppermute x8, starting transfers between devices, padded_2(): lax.ppermute(lax.slice_in_dim(block, block.shape[dim] - width, None, axis...  8.74 us
  transfers between devices with their start and end apart: 18, of which 17 were waited for; matrix products, arithmetic and copies ran while one was open for 6% of the time, Pallas kernels for 0%

commit v1 on v0

v1 whole, which is shorter than its diff:
```python
import functools

import jax
import jax.numpy as jnp
from jax import lax
from jax.experimental import pallas as pl
from jax.experimental.pallas import tpu as pltpu
from jax.sharding import PartitionSpec as P

RELAX = 3

spacing = 0.7853981633974483
undercool = -0.25
time_step = 0.00025
step_size = 0.002
stiffness = 0.5
epsilon = 1e-06

SUB = 8
LANES = 128
LAPS = 3
FIELD = LAPS * RELAX
REACH = FIELD + 2
CHUNKS = (11,)

VMEM = pl.BlockSpec(memory_space=pltpu.VMEM)
PARAMS = pltpu.CompilerParams(vmem_limit_bytes=32 << 20)


def neighbours(ref, i):
    c = ref[i]
    up = jnp.concatenate([c[1:], pltpu.roll(c[:1], SUB - 1, 1)], axis=0)
    down = jnp.concatenate([pltpu.roll(c[-1:], 1, 1), c[:-1]], axis=0)
    nz = c.shape[-1]
    side = pltpu.roll(c, 1, 2) + pltpu.roll(c, nz - 1, 2)
    return (ref[i - 1] + ref[i + 1]) + (up + down) + side - 6.0 * c


def potential_row(v, w, d):
    h2 = spacing * spacing
    return v * ((1.0 + undercool) + v * v) + (2.0 / h2) * w + (1.0 / (h2 * h2)) * d


def context(m):
    return LAPS if m % LAPS == 0 else 2


def level_row(levels, m, y):
    below, off = levels[m - 1]
    d = neighbours(below, y + off)
    kind = m % LAPS
    if kind == 1:
        return d
    w = below[y + off]
    ref, off = levels[m - 2 if kind == 2 else m - LAPS]
    v = ref[y + off]
    if kind == 2:
        return potential_row(v, w, d)
    return v + (time_step / (spacing * spacing)) * d


def rows_of(levels, m, start, stop, into):
    count = stop[0] - start[0]

    def body(i, carry):
        for side in range(2):
            ref, off = into[side]
            y = start[side] + i
            ref[y + off] = level_row(levels[side], m, y)
        return carry

    lax.fori_loop(0, count, body, 0)


def first_kernel(rows, sends, who_ref, whole_ref, recv_ref, *refs):
    slab, pieces = refs[0], refs[1:-2]
    halves, sems = refs[-2:]
    _, tiles, half, _, lanes = halves.shape
    planes = 2 * half // SUB
    copies = []
    for i, src in enumerate((whole_ref.at[who_ref[0]], recv_ref)):
        for z in range(tiles):
            part = src.at[:, :, pl.ds(z * lanes, lanes)]
            copies.append(pltpu.make_async_copy(part, halves.at[i, z], sems.at[i, z]))
    for copy in copies:
        copy.start()
    for copy in copies:
        copy.wait()
    flat = halves.reshape(2, tiles, half * rows, lanes)
    h = SUB // 2

    def body(y, carry):
        for r in range(planes):
            where = pl.ds(r * rows + y, h, stride=planes * rows)
            for i in range(2):
                for z in range(tiles):
                    slab[y, r, i * h : i * h + h, z * lanes : (z + 1) * lanes] = flat[i, z, where, :]
        return carry

    lax.fori_loop(0, rows, body, 0)
    for piece, (start, count) in zip(pieces, sends):
        def copy(i, carry, piece=piece, start=start):
            piece[i] = slab[start + i]
            return carry

        lax.fori_loop(0, count, copy, 0)


def inner_kernel(rows, slab_ref, *outs):
    levels = [(slab_ref, 0)] + [(ref, -m) for m, ref in enumerate(outs, 1)]
    for m in range(1, FIELD + 1):
        count = (rows - 2 * m) // 2
        start, stop = (m, m + count), (m + count, rows - m)
        rows_of((levels, levels), m, start, stop, (levels[m], levels[m]))


def edge_kernel(rows, before, after, low_ref, high_ref, *refs):
    count = after - before
    past, levels = refs[:FIELD], refs[-FIELD:]
    fields = refs[FIELD:-FIELD]
    sides = ([], [])
    for m, (old, new) in enumerate(zip(past, levels)):
        c = context(m)
        total = count + c
        for i in range(c):
            new[count + i] = old[i]
            new[total + i] = old[old.shape[0] - c + i]
        sides[0].append((new, after - m))
        sides[1].append((new, total + c - (rows - m + before)))

    def fill(i, carry):
        levels[0][i] = low_ref[i]
        levels[0][count + 2 * context(0) + i] = high_ref[i]
        return carry

    lax.fori_loop(0, count, fill, 0)
    for m in range(1, FIELD):
        start = (m - after, rows - m + before)
        stop = (m - before, rows - m + after)
        rows_of(sides, m, start, stop, (sides[0][m], sides[1][m]))
    beyond = max(0, after - FIELD)
    kept = count - beyond
    if kept:
        low = FIELD - after + beyond
        high = rows - FIELD + before
        into = ((fields[0], -low), (fields[0], kept - high))
        rows_of(sides, FIELD, (low, high), (low + kept, high + kept), into)
    if beyond:
        into = ((fields[-1], beyond), (fields[-1], beyond - rows))
        rows_of(sides, FIELD, (-beyond, rows), (0, rows + beyond), into)


def end_kernel(rows, segments, keep_ref, halo_ref, *refs):
    n = len(segments)
    pieces, partners, chains = refs[:n], refs[n : 2 * n], refs[2 * n : 3 * n]
    mine_ref, send_ref, sums_ref, field_ref, w_ref = refs[3 * n :]
    keep = keep_ref[0] != 0
    planes, nz = field_ref.shape[1], field_ref.shape[3]
    lanes = mine_ref.shape[-1]
    for i in range(2):
        field_ref[i] = halo_ref[i]
        field_ref[rows + 2 + i] = halo_ref[2 + i]
    for parts, piece in zip(segments, pieces):
        for start, count, first in parts:
            def copy(i, carry, start=start, first=first, piece=piece):
                field_ref[2 + start + i] = piece[first + i]
                return carry

            lax.fori_loop(0, count, copy, 0)

    def lap(i, carry):
        w_ref[i] = neighbours(field_ref, i + 1)
        return carry

    lax.fori_loop(0, rows + 2, lap, 0)
    sums_ref[...] = jnp.zeros_like(sums_ref)

    def fold(a):
        return sum(a[r, :, z : z + 128] for r in range(planes) for z in range(0, nz, lanes))

    def row(y, i, partner, chain):
        f = field_ref[y + 2]
        chem = potential_row(f, w_ref[y + 1], neighbours(w_ref, y + 1))
        a, b = partner[i], chain[i]
        t = a - b
        fr = pltpu.roll(f, SUB // 2, 1)
        da, db = a - fr, b - fr
        cr = pltpu.roll(chem, SUB // 2, 1)
        sums_ref[0] += fold(t * t)
        sums_ref[1] += fold(da * da)
        sums_ref[2] += fold(db * db)
        sums_ref[3] += fold(cr * t)
        g = jnp.where(keep, f, f - step_size * chem)
        h = SUB // 2
        for r in range(planes):
            where = pl.ds(r * rows + y, h, stride=planes * rows)
            for z in range(nz // lanes):
                at = slice(z * lanes, (z + 1) * lanes)
                mine_ref[0, z, where, :] = g[r, :h, at]
                send_ref[0, z, where, :] = g[r, h:, at]
                mine_ref[1, z, where, :] = t[r, h:, at]
                send_ref[1, z, where, :] = t[r, :h, at]

    for parts, partner, chain in zip(segments, partners, chains):
        for start, count, first in parts:
            def body(i, carry, start=start, first=first, partner=partner, chain=chain):
                row(start + i, first + i, partner, chain)
                return carry

            lax.fori_loop(0, count, body, 0)


def last_kernel(cells, keep_ref, who_ref, sums_ref, mine_ref, recv_ref, out_ref):
    def factor(i):
        def total(q):
            return jnp.sum(sums_ref[i, q], keepdims=True) / cells

        scale = lax.rsqrt(total(0) + epsilon)
        spring = stiffness * (jnp.sqrt(total(1) + epsilon) - jnp.sqrt(total(2) + epsilon))
        k = step_size * total(3) * scale * scale + spring * scale
        return jnp.where(keep_ref[i] != 0, jnp.zeros_like(k), k)

    _, half, rows, _ = out_ref.shape
    _, tiles, _, lanes = mine_ref.shape
    for i, ref in enumerate((mine_ref, recv_ref)):
        k = factor(i)
        image = who_ref[0] if i == 0 else 1 - who_ref[0]
        for z in range(tiles):
            value = ref[0, z] + k * ref[1, z]
            out_ref[image, :, :, z * lanes : (z + 1) * lanes] = value.reshape(half, rows, lanes)


def ring(axis, distance):
    n = lax.axis_size(axis)
    return [(i, (i + distance) % n) for i in range(n)]


def total_over(value, axis):
    n = lax.axis_size(axis)
    if n & (n - 1):
        return value + sum(lax.ppermute(value, axis, ring(axis, d)) for d in range(1, n))
    d = 1
    while d < n:
        value = value + lax.ppermute(value, axis, [(i, i ^ d) for i in range(n)])
        d *= 2
    return value


def per_device(initial_path):
    count, half, rows, nz = initial_path.shape
    assert count == lax.axis_size("gx") == 2
    assert rows % 2 == 0 and rows >= 2 * REACH and half % SUB == 0 and nz % LANES == 0
    planes = 2 * half // SUB
    cells = 2 * half * rows * lax.axis_size("gy") * nz
    chains = lax.axis_size("chain")
    gx = lax.axis_index("gx")
    chain = lax.axis_index("chain")
    swap = [(0, 1), (1, 0)]
    tiles = nz // LANES
    smem = pl.BlockSpec(memory_space=pltpu.SMEM)

    def slab(n):
        return jax.ShapeDtypeStruct((n, planes, SUB, nz), jnp.float32)

    who = gx.astype(jnp.int32)[None]
    other = lax.dynamic_index_in_dim(initial_path, 1 - gx, 0, keepdims=False)
    recv = lax.ppermute(other, "gx", swap)
    known = [0]
    for n in CHUNKS:
        known.append(known[-1] + n)
    sends = []
    for a, b in zip(known, known[1:]):
        sends += [(a, b - a), (rows - b, b - a)]
    first = pl.pallas_call(
        functools.partial(first_kernel, rows, sends),
        out_shape=[slab(rows)] + [slab(n) for _, n in sends],
        in_specs=[smem, pl.BlockSpec(memory_space=pl.ANY), pl.BlockSpec(memory_space=pl.ANY)],
        out_specs=[VMEM] * (1 + len(sends)),
        scratch_shapes=[
            pltpu.VMEM((2, tiles, half, rows, LANES), jnp.float32),
            pltpu.SemaphoreType.DMA((2, tiles)),
        ],
        compiler_params=PARAMS,
        name="first",
    )(who, initial_path, recv)
    halos = []
    for j in range(len(CHUNKS)):
        low, high = first[1 + 2 * j], first[2 + 2 * j]
        halos.append((
            lax.ppermute(high, "gy", ring("gy", 1)),
            lax.ppermute(low, "gy", ring("gy", -1)),
        ))

    inner = pl.pallas_call(
        functools.partial(inner_kernel, rows),
        out_shape=[slab(rows - 2 * m) for m in range(1, FIELD + 1)],
        in_specs=[VMEM],
        out_specs=[VMEM] * FIELD,
        compiler_params=PARAMS,
        name="inner",
    )(first[0])
    levels = [first[0]] + list(inner[:-1])
    pieces = [inner[-1]]
    segments = [[(FIELD, rows - 2 * FIELD, 0)]]
    for (low, high), a, b in zip(halos, known, known[1:]):
        beyond = max(0, b - FIELD)
        kept = b - a - beyond
        fields = [slab(2 * n) for n in (kept, beyond) if n]
        buffers = [(2 * (b - a + context(m)), planes, SUB, nz) for m in range(FIELD)]
        last = b == REACH
        outs = fields if last else fields + [slab(shape[0]) for shape in buffers]
        done = pl.pallas_call(
            functools.partial(edge_kernel, rows, a, b),
            out_shape=outs,
            in_specs=[VMEM] * (FIELD + 2),
            out_specs=[VMEM] * len(outs),
            scratch_shapes=[pltpu.VMEM(shape, jnp.float32) for shape in buffers] if last else [],
            compiler_params=PARAMS,
            name="edge",
        )(low, high, *levels)
        if kept:
            pieces.append(done[0])
            segments.append([(FIELD - a - kept, kept, 0), (rows - FIELD + a, kept, kept)])
        levels = list(done[len(fields) :])
        halo = done[len(fields) - 1]

    along_chain = []
    for c in range(chains - 1):
        along_chain += [(2 * c + 1, 2 * c + 2), (2 * c + 2, 2 * c + 1)]
    from_partner = [lax.ppermute(p, "gx", swap) for p in pieces]
    from_chain = [lax.ppermute(p, ("chain", "gx"), along_chain) for p in pieces]

    def keeping(image):
        return jnp.logical_or(image == 0, image == 2 * chains - 1).astype(jnp.int32)

    keep = jnp.stack([keeping(2 * chain + gx), keeping(2 * chain + 1 - gx)])
    part = jax.ShapeDtypeStruct((2, tiles, half * rows, LANES), jnp.float32)
    mine, send, sums = pl.pallas_call(
        functools.partial(end_kernel, rows, segments),
        out_shape=[part, part, jax.ShapeDtypeStruct((4, SUB, LANES), jnp.float32)],
        in_specs=[smem] + [VMEM] * (1 + 3 * len(pieces)),
        out_specs=[VMEM] * 3,
        scratch_shapes=[
            pltpu.VMEM((rows + 4, planes, SUB, nz), jnp.float32),
            pltpu.VMEM((rows + 2, planes, SUB, nz), jnp.float32),
        ],
        compiler_params=PARAMS,
        name="end",
    )(keep, halo, *pieces, *from_partner, *from_chain)
    halfway = lax.ppermute(send, "gx", swap)
    total = total_over(sums, "gy")
    totals = jnp.stack([total, lax.ppermute(total, "gx", swap)])
    return pl.pallas_call(
        functools.partial(last_kernel, cells),
        out_shape=jax.ShapeDtypeStruct(initial_path.shape, jnp.float32),
        in_specs=[smem, smem] + [VMEM] * 3,
        out_specs=VMEM,
        compiler_params=PARAMS,
        name="last",
    )(keep, who, totals, mine, halfway)


def solution(mesh):
    return jax.shard_map(
        per_device,
        mesh=mesh,
        in_specs=(P("chain", "gx", "gy", None),),
        out_specs=P("chain", "gx", "gy", None),
        check_vma=False,
    )
```

time: 168 us -> 116 us (0.69)
  Pallas kernels: 0 us -> 36.3 us
  other arithmetic: 33.6 us -> 0.09 us
  blocking collectives: 30.9 us -> 0 us
  local copies, waits for them, and re-layouts: 22.5 us -> 2.96 us
  starting transfers between devices: 24.1 us -> 18.1 us
  waiting for transfers between devices: 55.7 us -> 57.9 us
    pallas_call x0 -> x5, Pallas kernels: none -> 36.3 us  [the longest x1 14.7 us: per_device(): pl.pallas_call(functools.partial(edge_kernel, rows, a, b), out_shape=outs...]
    psum x2 -> x0, blocking collectives: 30.9 us -> none  [per_device(): lax.psum((tangent_part, forward_part, backward_part), ('gx', 'gy'))]
    slice x28 -> x0, local copies, waits for them, and re-layouts: 17.5 us -> none  [the longest x22 15.6 us: inner_lap(): total = total + jnp.roll(centre, -1, 3) + jnp.roll(centre, 1, 3)]
    add x6 -> x2, other arithmetic: 11.4 us -> 0.01 us  [total_over(): value = value + lax.ppermute(value, axis, [(i, i ^ d) for i in range(n)])]
    div x4 -> x0, other arithmetic: 9.01 us -> none  [inner_lap(): return (total - 6.0 * centre) / (spacing * spacing)]
    reduce_sum x2 -> x0, other arithmetic: 7.08 us -> none  [the longest x1 6.61 us: per_device(): jnp.sum(chemical * unit, axis=(1, 2, 3))]
    ppermute x18 -> x11, starting transfers between devices: 24.1 us -> 18.1 us  [the longest x2 5.98 us: per_device(): from_chain = [lax.ppermute(p, ('chain', 'gx'), along_chain) for p in pieces]]
    slice x5 -> x0, other arithmetic: 2.79 us -> none  [the longest x1 2.54 us: deep_potential(): first_lap[:, 1:-1, 1:-1]]
  transfers between devices with their start and end apart: 18 -> 11, of which waited for: 17 -> 7; matrix products, arithmetic and copies ran while one was open for 6% -> 0% of each run, Pallas kernels for 0% -> 9%
where the time goes in v1:
time: 116 us; the launch traced here: 115 us
  waiting for transfers between devices  57.9 us (50%)
  Pallas kernels  36.3 us (31%)
  starting transfers between devices  18.1 us (16%)
  local copies, waits for them, and re-layouts  2.96 us (3%)
    ppermute x2, waiting for transfers between devices, per_device(): from_chain = [lax.ppermute(p, ('chain', 'gx'), along_chain) for p in pieces]  30.2 us
    ppermute x1, waiting for transfers between devices, per_device(): lax.ppermute(low, 'gy', ring('gy', -1))  14.9 us
    pallas_call x1, Pallas kernels, per_device(): pl.pallas_call(functools.partial(edge_kernel, rows, a, b), out_shape=outs...  14.7 us
    pallas_call x1, Pallas kernels, per_device(): pl.pallas_call(functools.partial(inner_kernel, rows), out_shape=[slab(row...  9.91 us
    pallas_call x1, Pallas kernels, per_device(): pl.pallas_call(functools.partial(end_kernel, rows, segments), out_shape=[...  8.12 us
    ppermute x1, waiting for transfers between devices, per_device(): lax.ppermute(high, 'gy', ring('gy', 1))  6.02 us
    ppermute x2, starting transfers between devices, per_device(): from_chain = [lax.ppermute(p, ('chain', 'gx'), along_chain) for p in pieces]  5.98 us
    ppermute x2, waiting for transfers between devices, total_over(): value = value + lax.ppermute(value, axis, [(i, i ^ d) for i in range(n)])  4.07 us
  transfers between devices with their start and end apart: 11, of which 7 were waited for; matrix products, arithmetic and copies ran while one was open for 0% of the time, Pallas kernels for 9%

profile of v1, /device:TPU:5, one launch (start us, length us, event | category | flops | bytes accessed | tf_op | source)
XLA Modules:
  0.0 115.4 jit_solution(15896216223845872800)
XLA Ops:
  0.0 0.0 copy-start
  0.0 1.3 %dynamic-slice_bitcast_fusion = f32[32,24,256]{2,1,0:T(8,128)S(1)} fusion(f32[2,32,24,256]{3,2,1,0:T(8,128)} %whole_ref.1, s32[]{:T(128)S(6)} %select_n.4), kind=kLoop, calls=%fused_computation | loop fusion | bytes 1572868 | tf_op jit(solution)/shard_map/jit(dynamic_index_in_dim)/squeeze | solution.py:266
  1.3 0.7 collective-permute-start
  2.0 1.9 %collective-permute-done.recv_ref = f32[32,24,256]{2,1,0:T(8,128)S(1)} collective-permute-done((f32[32,24,256]{2,1,0:T(8,128)S(1)}, f32[32,24,256]{2,1,0:T(8,128)S(1)}, u32[]{:S(2)}, u32[]{:S(2)}) %collective-permute-start) | collective-permute-done | bytes 786464 | tf_op jit(solution)/shard_map/ppermute | solution.py:267
  4.0 0.0 copy-done
  4.0 1.4 %first.1 = (f32[24,8,8,256]{3,2,1,0:T(8,128)S(1)}, f32[11,8,8,256]{3,2,1,0:T(8,128)S(1)}, f32[11,8,8,256]{3,2,1,0:T(8,128)S(1)}) custom-call(s32[1]{0:T(128)} %bitcast.2.who_ref, f32[2,32,24,256]{3,2,1,0:T(8,128)S(1)} %copy-done, f32[32,24,256]{2,1,0:T(8,128)S(1)} %collective-permute-done.recv_ref), custom_call_target="tpu_custom_call" | custom-call | tf_op jit(solution)/shard_map/first/pallas_call | solution.py:274
  5.4 1.3 %collective-permute-start.1 = (f32[11,8,8,256]{3,2,1,0:T(8,128)S(1)}, f32[11,8,8,256]{3,2,1,0:T(8,128)S(1)}, u32[]{:S(2)}, u32[]{:S(2)}) collective-permute-start(f32[11,8,8,256]{3,2,1,0:T(8,128)S(1)} %get-tuple-element.22), channel_id=1, source_target_pairs={{0,1},{1,2},{2,3},{3,0},{4,5},{5,6},{6,7},{7,4},{8,9},{9,10},{10,1... | collective-permute-start | bytes 2162696 | tf_op jit(solution)/shard_map/ppermute | solution.py:290
  6.8 2.1 %collective-permute-start.2 = (f32[11,8,8,256]{3,2,1,0:T(8,128)S(1)}, f32[11,8,8,256]{3,2,1,0:T(8,128)S(1)}, u32[]{:S(2)}, u32[]{:S(2)}) collective-permute-start(f32[11,8,8,256]{3,2,1,0:T(8,128)S(1)} %get-tuple-element.23), channel_id=1, source_target_pairs={{0,3},{1,0},{2,1},{3,2},{4,7},{5,4},{6,5},{7,6},{8,11},{9,8},{10,9... | collective-permute-start | bytes 2162696 | tf_op jit(solution)/shard_map/ppermute | solution.py:291
  8.9 9.9 %inner.1 = (f32[22,8,8,256]{3,2,1,0:T(8,128)S(1)}, f32[20,8,8,256]{3,2,1,0:T(8,128)S(1)}, f32[18,8,8,256]{3,2,1,0:T(8,128)S(1)}, f32[16,8,8,256]{3,2,1,0:T(8,128...) custom-call(f32[24,8,8,256]{3,2,1,0:T(8,128)S(1)} %get-tuple-element, ...), custom_call_target="tpu_custom_call" | custom-call | tf_op jit(solution)/shard_map/inner/pallas_call | solution.py:294
  18.8 6.0 %collective-permute-done.1.low_ref = f32[11,8,8,256]{3,2,1,0:T(8,128)S(1)} collective-permute-done((f32[11,8,8,256]{3,2,1,0:T(8,128)S(1)}, f32[11,8,8,256]{3,2,1,0:T(8,128)S(1)}, u32[]{:S(2)}, u32[]{:S(2)}) %collective-permute-start.1) | collective-permute-done | bytes 720928 | tf_op jit(solution)/shard_map/ppermute | solution.py:290
  24.8 14.9 %collective-permute-done.2.high_ref = f32[11,8,8,256]{3,2,1,0:T(8,128)S(1)} collective-permute-done((f32[11,8,8,256]{3,2,1,0:T(8,128)S(1)}, f32[11,8,8,256]{3,2,1,0:T(8,128)S(1)}, u32[]{:S(2)}, u32[]{:S(2)}) %collective-permute-start.2) | collective-permute-done | bytes 720928 | tf_op jit(solution)/shard_map/ppermute | solution.py:291
  39.7 14.7 %edge.1 = (f32[18,8,8,256]{3,2,1,0:T(8,128)S(1)}, f32[4,8,8,256]{3,2,1,0:T(8,128)S(1)}) custom-call(f32[11,8,8,256]{3,2,1,0:T(8,128)S(1)} %collective-permute-done.1.low_ref, f32[11,8,8,256]{3,2,1,0:T(8,128)S(1)} %collective-permute-done.2.high_ref, f32[24,8,8,256]{3,2,1,0:T(8,128)S(1)} %get-tuple-element.24.slab_ref.refs_0_, ...), custom_call_target="tpu_custom_call" | custom-call | tf_op jit(solution)/shard_map/edge/pallas_call | solution.py:312
  54.4 0.0 copy-start.1
  54.4 0.7 copy-done.1
  55.2 4.1 %collective-permute-start.6 = (f32[18,8,8,256]{3,2,1,0:T(8,128)S(1)}, f32[18,8,8,256]{3,2,1,0:T(8,128)S(1)}, u32[]{:S(2)}, u32[]{:S(2)}) collective-permute-start(f32[18,8,8,256]{3,2,1,0:T(8,128)S(1)} %get-tuple-element.35.refs_1_), channel_id=1, source_target_pairs={{4,8},{8,4},{12,16},{16,12},{20,24},{24,20},{5,9},{9,5},{13,17},{1... | collective-permute-start | bytes 3538952 | tf_op jit(solution)/shard_map/ppermute | solution.py:331
  59.2 0.1 collective-permute-start.4
  59.3 1.9 %collective-permute-start.5 = (f32[6,8,8,256]{3,2,1,0:T(8,128)}, f32[6,8,8,256]{3,2,1,0:T(8,128)}, u32[]{:S(2)}, u32[]{:S(2)}) collective-permute-start(f32[6,8,8,256]{3,2,1,0:T(8,128)} %get-tuple-element.34.refs_0_), channel_id=1, source_target_pairs={{4,8},{8,4},{12,16},{16,12},{20,24},{24,20},{5,9},{9,5},{13,17},{1... | collective-permute-start | bytes 1179656 | tf_op jit(solution)/shard_map/ppermute | solution.py:331
  61.2 1.6 %collective-permute-start.3 = (f32[6,8,8,256]{3,2,1,0:T(8,128)}, f32[6,8,8,256]{3,2,1,0:T(8,128)}, u32[]{:S(2)}, u32[]{:S(2)}) collective-permute-start(f32[6,8,8,256]{3,2,1,0:T(8,128)} %get-tuple-element.34.refs_0_), channel_id=1, source_target_pairs={{0,4},{4,0},{1,5},{5,1},{2,6},{6,2},{3,7},{7,3},{8,12},{12,8},{9,1... | collective-permute-start | bytes 1179656 | tf_op jit(solution)/shard_map/ppermute | solution.py:330
  62.8 0.1 add_convert_fusion.keep_ref
  62.9 30.2 %collective-permute-done.5.refs_4_ = f32[6,8,8,256]{3,2,1,0:T(8,128)} collective-permute-done((f32[6,8,8,256]{3,2,1,0:T(8,128)}, f32[6,8,8,256]{3,2,1,0:T(8,128)}, u32[]{:S(2)}, u32[]{:S(2)}) %collective-permute-start.5) | collective-permute-done | bytes 393248 | tf_op jit(solution)/shard_map/ppermute | solution.py:331
  93.1 0.0 collective-permute-done.3.refs_2_
  93.1 0.0 collective-permute-done.6.refs_5_
  93.1 0.0 collective-permute-done.4.refs_3_
  93.1 0.0 copy-start.2
  93.1 0.9 copy-done.2
  94.1 8.1 %end.1 = (f32[2,2,768,128]{3,2,1,0:T(8,128)S(1)}, f32[2,2,768,128]{3,2,1,0:T(8,128)S(1)}, f32[4,8,128]{2,1,0:T(8,128)S(1)}) custom-call(s32[2]{0:T(128)S(1)} %add_convert_fusion.keep_ref, f32[4,8,8,256]{3,2,1,0:T(8,128)S(1)} %copy-done.2, f32[6,8,8,256]{3,2,1,0:T(8,128)} %get-tuple-element.34.refs_0_, f32[18,8,8,256]{3,2,1,0:T(8,128)S(1)} %get-tuple-element.35.refs_1_, ...), custom_call_target="tpu_custom_call" | custom-call | tf_op jit(solution)/shard_map/end/pallas_call | solution.py:338
  102.2 1.9 %collective-permute-start.10 = (f32[2,2,768,128]{3,2,1,0:T(8,128)S(1)}, f32[2,2,768,128]{3,2,1,0:T(8,128)S(1)}, u32[]{:S(2)}, u32[]{:S(2)}) collective-permute-start(f32[2,2,768,128]{3,2,1,0:T(8,128)S(1)} %get-tuple-element.38), channel_id=1, source_target_pairs={{0,4},{4,0},{1,5},{5,1},{2,6},{6,2},{3,7},{7,3},{8,12},{12,8},{9,1... | collective-permute-start | bytes 4718600 | tf_op jit(solution)/shard_map/ppermute | solution.py:350
  104.1 1.0 collective-permute-start.7
  105.1 1.6 %collective-permute-done.7 = f32[4,8,128]{2,1,0:T(8,128)S(1)} collective-permute-done((f32[4,8,128]{2,1,0:T(8,128)S(1)}, f32[4,8,128]{2,1,0:T(8,128)S(1)}, u32[]{:S(2)}, u32[]{:S(2)}) %collective-permute-start.7) | collective-permute-done | bytes 16416 | tf_op jit(solution)/shard_map/ppermute | solution.py:244
  106.7 1.0 collective-permute-start.8
  107.7 2.5 %collective-permute-done.8 = f32[4,8,128]{2,1,0:T(8,128)S(1)} collective-permute-done((f32[4,8,128]{2,1,0:T(8,128)S(1)}, f32[4,8,128]{2,1,0:T(8,128)S(1)}, u32[]{:S(2)}, u32[]{:S(2)}) %collective-permute-start.8) | collective-permute-done | bytes 16416 | tf_op jit(solution)/shard_map/ppermute | solution.py:244
  110.2 2.4 %collective-permute-start.9 = (f32[4,8,128]{2,1,0:T(8,128)S(1)}, f32[4,8,128]{2,1,0:T(8,128)S(1)}, u32[]{:S(2)}, u32[]{:S(2)}) collective-permute-start(f32[4,8,128]{2,1,0:T(8,128)S(1)} %add.21), channel_id=1, source_target_pairs={{0,4},{4,0},{1,5},{5,1},{2,6},{6,2},{3,7},{7,3},{8,12},{12,8},{9,1... | collective-permute-start | bytes 49160 | tf_op jit(solution)/shard_map/ppermute | solution.py:352
  112.5 0.8 collective-permute-done.9
  113.4 0.0 collective-permute-done.10.recv_ref
  113.4 2.1 %last.1 = f32[2,32,24,256]{3,2,1,0:T(8,128)} custom-call(s32[2]{0:T(128)S(1)} %add_convert_fusion.keep_ref, s32[1]{0:T(128)} %bitcast.2.who_ref, f32[2,4,8,128]{3,2,1,0:T(8,128)S(1)} %pad_maximum_fusion.sums_ref, f32[2,2,768,128]{3,2,1,0:T(8,128)S(1)} %get-tuple-element.37.mine_ref, f32[2,2,768,128]{3,2,1,0:T(8,128)S(1)} %collective-permute-done.10.recv_ref), custom_call_target="tpu_custom_call" | custom-call | tf_op jit(solution)/shard_map/last/pallas_call | solution.py:353
  (3 shorter events, 0.0 us)
Async XLA Ops:
  0.0 4.0 %copy-start = (f32[2,32,24,256]{3,2,1,0:T(8,128)S(1)}, f32[2,32,24,256]{3,2,1,0:T(8,128)}, u32[]{:S(2)}) copy-start(f32[2,32,24,256]{3,2,1,0:T(8,128)} %whole_ref.1) | copy-start | bytes 4718596
  1.3 2.7 %collective-permute-start = (f32[32,24,256]{2,1,0:T(8,128)S(1)}, f32[32,24,256]{2,1,0:T(8,128)S(1)}, u32[]{:S(2)}, u32[]{:S(2)}) collective-permute-start(f32[32,24,256]{2,1,0:T(8,128)S(1)} %dynamic-slice_bitcast_fusion), channel_id=1, source_target_pairs={{0,4},{4,0},{1,5},{5,1},{2,6},{6,2},{3,7},{7,3},{8,12},{12,8},{9,1... | collective-permute-start | bytes 2359304 | tf_op jit(solution)/shard_map/ppermute | solution.py:267
  5.4 19.4 %collective-permute-start.1 = (f32[11,8,8,256]{3,2,1,0:T(8,128)S(1)}, f32[11,8,8,256]{3,2,1,0:T(8,128)S(1)}, u32[]{:S(2)}, u32[]{:S(2)}) collective-permute-start(f32[11,8,8,256]{3,2,1,0:T(8,128)S(1)} %get-tuple-element.22), channel_id=1, source_target_pairs={{0,1},{1,2},{2,3},{3,0},{4,5},{5,6},{6,7},{7,4},{8,9},{9,10},{10,1... | collective-permute-start | bytes 2162696 | tf_op jit(solution)/shard_map/ppermute | solution.py:290
  6.8 32.9 %collective-permute-start.2 = (f32[11,8,8,256]{3,2,1,0:T(8,128)S(1)}, f32[11,8,8,256]{3,2,1,0:T(8,128)S(1)}, u32[]{:S(2)}, u32[]{:S(2)}) collective-permute-start(f32[11,8,8,256]{3,2,1,0:T(8,128)S(1)} %get-tuple-element.23), channel_id=1, source_target_pairs={{0,3},{1,0},{2,1},{3,2},{4,7},{5,4},{6,5},{7,6},{8,11},{9,8},{10,9... | collective-permute-start | bytes 2162696 | tf_op jit(solution)/shard_map/ppermute | solution.py:291
  54.4 0.7 copy-start.1
  55.2 37.9 %collective-permute-start.6 = (f32[18,8,8,256]{3,2,1,0:T(8,128)S(1)}, f32[18,8,8,256]{3,2,1,0:T(8,128)S(1)}, u32[]{:S(2)}, u32[]{:S(2)}) collective-permute-start(f32[18,8,8,256]{3,2,1,0:T(8,128)S(1)} %get-tuple-element.35.refs_1_), channel_id=1, source_target_pairs={{4,8},{8,4},{12,16},{16,12},{20,24},{24,20},{5,9},{9,5},{13,17},{1... | collective-permute-start | bytes 3538952 | tf_op jit(solution)/shard_map/ppermute | solution.py:331
  59.2 33.9 %collective-permute-start.4 = (f32[18,8,8,256]{3,2,1,0:T(8,128)S(1)}, f32[18,8,8,256]{3,2,1,0:T(8,128)S(1)}, u32[]{:S(2)}, u32[]{:S(2)}) collective-permute-start(f32[18,8,8,256]{3,2,1,0:T(8,128)S(1)} %get-tuple-element.35.refs_1_), channel_id=1, source_target_pairs={{0,4},{4,0},{1,5},{5,1},{2,6},{6,2},{3,7},{7,3},{8,12},{12,8},{9,1... | collective-permute-start | bytes 3538952 | tf_op jit(solution)/shard_map/ppermute | solution.py:330
  59.3 33.8 %collective-permute-start.5 = (f32[6,8,8,256]{3,2,1,0:T(8,128)}, f32[6,8,8,256]{3,2,1,0:T(8,128)}, u32[]{:S(2)}, u32[]{:S(2)}) collective-permute-start(f32[6,8,8,256]{3,2,1,0:T(8,128)} %get-tuple-element.34.refs_0_), channel_id=1, source_target_pairs={{4,8},{8,4},{12,16},{16,12},{20,24},{24,20},{5,9},{9,5},{13,17},{1... | collective-permute-start | bytes 1179656 | tf_op jit(solution)/shard_map/ppermute | solution.py:331
  61.2 31.9 %collective-permute-start.3 = (f32[6,8,8,256]{3,2,1,0:T(8,128)}, f32[6,8,8,256]{3,2,1,0:T(8,128)}, u32[]{:S(2)}, u32[]{:S(2)}) collective-permute-start(f32[6,8,8,256]{3,2,1,0:T(8,128)} %get-tuple-element.34.refs_0_), channel_id=1, source_target_pairs={{0,4},{4,0},{1,5},{5,1},{2,6},{6,2},{3,7},{7,3},{8,12},{12,8},{9,1... | collective-permute-start | bytes 1179656 | tf_op jit(solution)/shard_map/ppermute | solution.py:330
  93.1 1.0 copy-start.2
  102.2 11.2 %collective-permute-start.10 = (f32[2,2,768,128]{3,2,1,0:T(8,128)S(1)}, f32[2,2,768,128]{3,2,1,0:T(8,128)S(1)}, u32[]{:S(2)}, u32[]{:S(2)}) collective-permute-start(f32[2,2,768,128]{3,2,1,0:T(8,128)S(1)} %get-tuple-element.38), channel_id=1, source_target_pairs={{0,4},{4,0},{1,5},{5,1},{2,6},{6,2},{3,7},{7,3},{8,12},{12,8},{9,1... | collective-permute-start | bytes 4718600 | tf_op jit(solution)/shard_map/ppermute | solution.py:350
  104.1 2.6 %collective-permute-start.7 = (f32[4,8,128]{2,1,0:T(8,128)S(1)}, f32[4,8,128]{2,1,0:T(8,128)S(1)}, u32[]{:S(2)}, u32[]{:S(2)}) collective-permute-start(f32[4,8,128]{2,1,0:T(8,128)S(1)} %get-tuple-element.36), channel_id=1, source_target_pairs={{0,1},{1,0},{2,3},{3,2},{4,5},{5,4},{6,7},{7,6},{8,9},{9,8},{10,11... | collective-permute-start | bytes 49160 | tf_op jit(solution)/shard_map/ppermute | solution.py:244
  106.7 3.5 %collective-permute-start.8 = (f32[4,8,128]{2,1,0:T(8,128)S(1)}, f32[4,8,128]{2,1,0:T(8,128)S(1)}, u32[]{:S(2)}, u32[]{:S(2)}) collective-permute-start(f32[4,8,128]{2,1,0:T(8,128)S(1)} %add.20), channel_id=1, source_target_pairs={{0,2},{1,3},{2,0},{3,1},{4,6},{5,7},{6,4},{7,5},{8,10},{9,11},{10,... | collective-permute-start | bytes 49160 | tf_op jit(solution)/shard_map/ppermute | solution.py:244
  110.2 3.2 %collective-permute-start.9 = (f32[4,8,128]{2,1,0:T(8,128)S(1)}, f32[4,8,128]{2,1,0:T(8,128)S(1)}, u32[]{:S(2)}, u32[]{:S(2)}) collective-permute-start(f32[4,8,128]{2,1,0:T(8,128)S(1)} %add.21), channel_id=1, source_target_pairs={{0,4},{4,0},{1,5},{5,1},{2,6},{6,2},{3,7},{7,3},{8,12},{12,8},{9,1... | collective-permute-start | bytes 49160 | tf_op jit(solution)/shard_map/ppermute | solution.py:352

commit v2 on v1

--- a/solution.py
+++ b/solution.py
@@ -21,10 +21,10 @@
 LAPS = 3
 FIELD = LAPS * RELAX
 REACH = FIELD + 2
-CHUNKS = (11,)
+CHUNKS = (5, 4, 2)
 
 VMEM = pl.BlockSpec(memory_space=pltpu.VMEM)
-PARAMS = pltpu.CompilerParams(vmem_limit_bytes=32 << 20)
+PARAMS = pltpu.CompilerParams(vmem_limit_bytes=8 << 20)
 
 
 def neighbours(ref, i):
@@ -60,16 +60,11 @@
 
 
 def rows_of(levels, m, start, stop, into):
-    count = stop[0] - start[0]
-
-    def body(i, carry):
+    for i in range(stop[0] - start[0]):
         for side in range(2):
             ref, off = into[side]
             y = start[side] + i
             ref[y + off] = level_row(levels[side], m, y)
-        return carry
-
-    lax.fori_loop(0, count, body, 0)
 
 
 def first_kernel(rows, sends, who_ref, whole_ref, recv_ref, *refs):
@@ -150,67 +145,66 @@
         rows_of(sides, FIELD, (-beyond, rows), (0, rows + beyond), into)
 
 
-def end_kernel(rows, segments, keep_ref, halo_ref, *refs):
+def chemical_kernel(rows, segments, halo_ref, *refs):
     n = len(segments)
-    pieces, partners, chains = refs[:n], refs[n : 2 * n], refs[2 * n : 3 * n]
-    mine_ref, send_ref, sums_ref, field_ref, w_ref = refs[3 * n :]
-    keep = keep_ref[0] != 0
-    planes, nz = field_ref.shape[1], field_ref.shape[3]
-    lanes = mine_ref.shape[-1]
+    pieces, outs = refs[:n], refs[n : 2 * n]
+    field_ref, w_ref = refs[2 * n :]
     for i in range(2):
         field_ref[i] = halo_ref[i]
         field_ref[rows + 2 + i] = halo_ref[2 + i]
     for parts, piece in zip(segments, pieces):
         for start, count, first in parts:
-            def copy(i, carry, start=start, first=first, piece=piece):
+            for i in range(count):
                 field_ref[2 + start + i] = piece[first + i]
-                return carry
-
-            lax.fori_loop(0, count, copy, 0)
-
-    def lap(i, carry):
+    for i in range(rows + 2):
         w_ref[i] = neighbours(field_ref, i + 1)
-        return carry
-
-    lax.fori_loop(0, rows + 2, lap, 0)
-    sums_ref[...] = jnp.zeros_like(sums_ref)
+    for parts, out in zip(segments, outs):
+        for start, count, first in parts:
+            for i in range(count):
+                y = start + i
+                out[first + i] = potential_row(field_ref[y + 2], w_ref[y + 1], neighbours(w_ref, y + 1))
+
+
+def sums_kernel(n, lanes, keep_ref, *refs):
+    sums_ref, outs = refs[4 * n], refs[4 * n + 1 :]
+    keep = keep_ref[0] != 0
+    planes, nz = refs[0].shape[1], refs[0].shape[3]
 
     def fold(a):
-        return sum(a[r, :, z : z + 128] for r in range(planes) for z in range(0, nz, lanes))
-
-    def row(y, i, partner, chain):
-        f = field_ref[y + 2]
-        chem = potential_row(f, w_ref[y + 1], neighbours(w_ref, y + 1))
-        a, b = partner[i], chain[i]
-        t = a - b
-        fr = pltpu.roll(f, SUB // 2, 1)
-        da, db = a - fr, b - fr
-        cr = pltpu.roll(chem, SUB // 2, 1)
-        sums_ref[0] += fold(t * t)
-        sums_ref[1] += fold(da * da)
-        sums_ref[2] += fold(db * db)
-        sums_ref[3] += fold(cr * t)
-        g = jnp.where(keep, f, f - step_size * chem)
-        h = SUB // 2
-        for r in range(planes):
-            where = pl.ds(r * rows + y, h, stride=planes * rows)
-            for z in range(nz // lanes):
-                at = slice(z * lanes, (z + 1) * lanes)
-                mine_ref[0, z, where, :] = g[r, :h, at]
-                send_ref[0, z, where, :] = g[r, h:, at]
-                mine_ref[1, z, where, :] = t[r, h:, at]
-                send_ref[1, z, where, :] = t[r, :h, at]
-
-    for parts, partner, chain in zip(segments, partners, chains):
-        for start, count, first in parts:
-            def body(i, carry, start=start, first=first, partner=partner, chain=chain):
-                row(start + i, first + i, partner, chain)
-                return carry
-
-            lax.fori_loop(0, count, body, 0)
-
-
-def last_kernel(cells, keep_ref, who_ref, sums_ref, mine_ref, recv_ref, out_ref):
+        return sum(a[r, :, z : z + lanes] for r in range(planes) for z in range(0, nz, lanes))
+
+    low = lax.broadcasted_iota(jnp.int32, (planes, SUB, nz), 1) < SUB // 2
+    totals = [jnp.zeros((SUB, lanes), jnp.float32)] * 4
+    for j in range(n):
+        piece, partner, chain, chemical = refs[j : 4 * n : n]
+        mine, send = outs[2 * j], outs[2 * j + 1]
+
+        def body(i, totals, piece=piece, partner=partner, chain=chain, chemical=chemical, mine=mine, send=send):
+            f, a, b, chem = piece[i], partner[i], chain[i], chemical[i]
+            t = a - b
+            fr = pltpu.roll(f, SUB // 2, 1)
+            cr = pltpu.roll(chem, SUB // 2, 1)
+            da, db = a - fr, b - fr
+            g = jnp.where(keep, f, f - step_size * chem)
+            mine[i] = jnp.where(low, g, t)
+            send[i] = jnp.where(low, t, g)
+            parts = (fold(t * t), fold(da * da), fold(db * db), fold(cr * t))
+            return tuple(total + part for total, part in zip(totals, parts))
+
+        totals = lax.fori_loop(0, piece.shape[0], body, tuple(totals))
+    for q in range(4):
+        sums_ref[q] = totals[q]
+
+
+def last_kernel(cells, segments, keep_ref, who_ref, sums_ref, *refs):
+    n = len(segments)
+    out_ref, natural, sems = refs[2 * n :]
+    _, half, rows, _ = out_ref.shape
+    _, tiles, _, _, lanes = natural.shape
+    flat = natural.reshape(2, tiles, half * rows, lanes)
+    planes = 2 * half // SUB
+    h = SUB // 2
+
     def factor(i):
         def total(q):
             return jnp.sum(sums_ref[i, q], keepdims=True) / cells
@@ -220,14 +214,29 @@
         k = step_size * total(3) * scale * scale + spring * scale
         return jnp.where(keep_ref[i] != 0, jnp.zeros_like(k), k)
 
-    _, half, rows, _ = out_ref.shape
-    _, tiles, _, lanes = mine_ref.shape
-    for i, ref in enumerate((mine_ref, recv_ref)):
+    copies = []
+    for i in range(2):
         k = factor(i)
         image = who_ref[0] if i == 0 else 1 - who_ref[0]
+        for parts, ref in zip(segments, refs[i * n : (i + 1) * n]):
+            for start, count, first in parts:
+                def body(j, carry, start=start, first=first, ref=ref, i=i, k=k):
+                    for r in range(planes):
+                        for z in range(tiles):
+                            at = slice(z * lanes, (z + 1) * lanes)
+                            v = ref[first + j, r, :, at]
+                            v = v + k * pltpu.roll(v, h, 0)
+                            where = pl.ds(r * rows + start + j, h, stride=planes * rows)
+                            flat[i, z, where, :] = v[i * h : i * h + h]
+                    return carry
+
+                lax.fori_loop(0, count, body, 0)
         for z in range(tiles):
-            value = ref[0, z] + k * ref[1, z]
-            out_ref[image, :, :, z * lanes : (z + 1) * lanes] = value.reshape(half, rows, lanes)
+            part = out_ref.at[image, :, :, pl.ds(z * lanes, lanes)]
+            copies.append(pltpu.make_async_copy(natural.at[i, z], part, sems.at[i, z]))
+            copies[-1].start()
+    for copy in copies:
+        copy.wait()
 
 
 def ring(axis, distance):
@@ -334,30 +343,47 @@
         return jnp.logical_or(image == 0, image == 2 * chains - 1).astype(jnp.int32)
 
     keep = jnp.stack([keeping(2 * chain + gx), keeping(2 * chain + 1 - gx)])
-    part = jax.ShapeDtypeStruct((2, tiles, half * rows, LANES), jnp.float32)
-    mine, send, sums = pl.pallas_call(
-        functools.partial(end_kernel, rows, segments),
-        out_shape=[part, part, jax.ShapeDtypeStruct((4, SUB, LANES), jnp.float32)],
-        in_specs=[smem] + [VMEM] * (1 + 3 * len(pieces)),
-        out_specs=[VMEM] * 3,
+    chemical = pl.pallas_call(
+        functools.partial(chemical_kernel, rows, segments),
+        out_shape=[slab(p.shape[0]) for p in pieces],
+        in_specs=[VMEM] * (1 + len(pieces)),
+        out_specs=[VMEM] * len(pieces),
         scratch_shapes=[
             pltpu.VMEM((rows + 4, planes, SUB, nz), jnp.float32),
             pltpu.VMEM((rows + 2, planes, SUB, nz), jnp.float32),
         ],
         compiler_params=PARAMS,
-        name="end",
-    )(keep, halo, *pieces, *from_partner, *from_chain)
-    halfway = lax.ppermute(send, "gx", swap)
-    total = total_over(sums, "gy")
+        name="chemical",
+    )(halo, *pieces)
+    mine, halfway, total = [], [], 0.0
+    for some in (slice(0, -1), slice(-1, None)):
+        n = len(pieces[some])
+        sums, *outs = pl.pallas_call(
+            functools.partial(sums_kernel, n, LANES),
+            out_shape=[jax.ShapeDtypeStruct((4, SUB, LANES), jnp.float32)]
+            + [slab(p.shape[0]) for p in pieces[some] for _ in range(2)],
+            in_specs=[smem] + [VMEM] * (4 * n),
+            out_specs=[VMEM] * (1 + 2 * n),
+            compiler_params=PARAMS,
+            name="sums",
+        )(keep, *pieces[some], *from_partner[some], *from_chain[some], *chemical[some])
+        total = total + sums
+        mine += outs[::2]
+        halfway += [lax.ppermute(send, "gx", swap) for send in outs[1::2]]
+    total = total_over(total, "gy")
     totals = jnp.stack([total, lax.ppermute(total, "gx", swap)])
     return pl.pallas_call(
-        functools.partial(last_kernel, cells),
+        functools.partial(last_kernel, cells, segments),
         out_shape=jax.ShapeDtypeStruct(initial_path.shape, jnp.float32),
-        in_specs=[smem, smem] + [VMEM] * 3,
-        out_specs=VMEM,
+        in_specs=[smem, smem] + [VMEM] * (1 + 2 * len(pieces)),
+        out_specs=pl.BlockSpec(memory_space=pl.ANY),
+        scratch_shapes=[
+            pltpu.VMEM((2, tiles, half, rows, LANES), jnp.float32),
+            pltpu.SemaphoreType.DMA((2, tiles)),
+        ],
         compiler_params=PARAMS,
         name="last",
-    )(keep, who, totals, mine, halfway)
+    )(keep, who, totals, *mine, *halfway)
 
 
 def solution(mesh):

time: 116 us -> 82.9 us (0.71)
  waiting for transfers between devices: 57.9 us -> 12.3 us
  local copies, waits for them, and re-layouts: 2.96 us -> 17.9 us
  Pallas kernels: 36.3 us -> 23 us
  starting transfers between devices: 18.1 us -> 28.2 us
    ppermute x2 -> x3, waiting for transfers between devices: 30.2 us -> 0.01 us  [per_device(): from_chain = [lax.ppermute(p, ('chain', 'gx'), along_chain) for p in pieces]]
    unnamed x6 -> x38, local copies, waits for them, and re-layouts: 1.66 us -> 16.6 us
    ppermute x1 -> x3, waiting for transfers between devices: 14.9 us -> 3.48 us  [per_device(): lax.ppermute(low, 'gy', ring('gy', -1))]
    ppermute x2 -> x3, starting transfers between devices: 5.98 us -> 13.5 us  [per_device(): from_chain = [lax.ppermute(p, ('chain', 'gx'), along_chain) for p in pieces]]
    pallas_call x1 -> x3, Pallas kernels: 14.7 us -> 8.26 us  [per_device(): pl.pallas_call(functools.partial(edge_kernel, rows, a, b), out_shape=outs...]
    ppermute x1 -> x3, waiting for transfers between devices: 6.02 us -> 0.01 us  [per_device(): lax.ppermute(high, 'gy', ring('gy', 1))]
    pallas_call x1, Pallas kernels: 9.91 us -> 4.6 us  [per_device(): pl.pallas_call(functools.partial(inner_kernel, rows), out_shape=[slab(row...]
    ppermute x1 -> x3, starting transfers between devices: 2.09 us -> 7.08 us  [per_device(): lax.ppermute(low, 'gy', ring('gy', -1))]
  transfers between devices with their start and end apart: 11 -> 19, of which waited for: 7 -> 6; matrix products, arithmetic and copies ran while one was open for 0% -> 0% of each run, Pallas kernels for 9% -> 23%
where the time goes in v2:
time: 82.9 us; the launch traced here: 81.9 us
  starting transfers between devices  28.2 us (34%)
  Pallas kernels  23 us (28%)
  local copies, waits for them, and re-layouts  17.9 us (22%)
  waiting for transfers between devices  12.3 us (15%)
    unnamed x38, local copies, waits for them, and re-layouts  16.6 us
    ppermute x3, starting transfers between devices, per_device(): from_chain = [lax.ppermute(p, ('chain', 'gx'), along_chain) for p in pieces]  13.5 us
    pallas_call x3, Pallas kernels, per_device(): pl.pallas_call(functools.partial(edge_kernel, rows, a, b), out_shape=outs...  8.26 us
    ppermute x3, starting transfers between devices, per_device(): lax.ppermute(low, 'gy', ring('gy', -1))  7.08 us
    ppermute x2, waiting for transfers between devices, total_over(): value = value + lax.ppermute(value, axis, [(i, i ^ d) for i in range(n)])  6.08 us
    pallas_call x1, Pallas kernels, per_device(): pl.pallas_call(functools.partial(inner_kernel, rows), out_shape=[slab(row...  4.6 us
    pallas_call x2, Pallas kernels, per_device(): pl.pallas_call(functools.partial(sums_kernel, n, LANES), out_shape=[jax.S...  3.69 us
    ppermute x3, waiting for transfers between devices, per_device(): lax.ppermute(low, 'gy', ring('gy', -1))  3.48 us
  transfers between devices with their start and end apart: 19, of which 6 were waited for; matrix products, arithmetic and copies ran while one was open for 0% of the time, Pallas kernels for 23%

profile of v2, /device:TPU:5, one launch (start us, length us, event | category | flops | bytes accessed | tf_op | source)
XLA Modules:
  0.0 81.9 jit_solution(2642410648640950019)
XLA Ops:
  0.0 1.3 %dynamic-slice_bitcast_fusion = f32[32,24,256]{2,1,0:T(8,128)S(1)} fusion(f32[2,32,24,256]{3,2,1,0:T(8,128)} %whole_ref.1, s32[]{:T(128)S(6)} %select_n.4), kind=kLoop, calls=%fused_computation | loop fusion | bytes 1572868 | tf_op jit(solution)/shard_map/jit(dynamic_index_in_dim)/squeeze | solution.py:275
  1.3 0.7 collective-permute-start
  2.0 1.9 %collective-permute-done.recv_ref = f32[32,24,256]{2,1,0:T(8,128)S(1)} collective-permute-done((f32[32,24,256]{2,1,0:T(8,128)S(1)}, f32[32,24,256]{2,1,0:T(8,128)S(1)}, u32[]{:S(2)}, u32[]{:S(2)}) %collective-permute-start) | collective-permute-done | bytes 786464 | tf_op jit(solution)/shard_map/ppermute | solution.py:276
  4.0 1.4 %first.1 = (f32[24,8,8,256]{3,2,1,0:T(8,128)S(1)}, f32[5,8,8,256]{3,2,1,0:T(8,128)S(1)}, f32[5,8,8,256]{3,2,1,0:T(8,128)S(1)}, f32[4,8,8,256]{3,2,1,0:T(8,128)S(...) custom-call(s32[1]{0:T(128)} %bitcast.2.who_ref, ...), custom_call_target="tpu_custom_call" | custom-call | tf_op jit(solution)/shard_map/first/pallas_call | solution.py:283
  5.4 1.3 %collective-permute-start.1 = (f32[5,8,8,256]{3,2,1,0:T(8,128)S(1)}, f32[5,8,8,256]{3,2,1,0:T(8,128)S(1)}, u32[]{:S(2)}, u32[]{:S(2)}) collective-permute-start(f32[5,8,8,256]{3,2,1,0:T(8,128)S(1)} %get-tuple-element.54), channel_id=1, source_target_pairs={{0,1},{1,2},{2,3},{3,0},{4,5},{5,6},{6,7},{7,4},{8,9},{9,10},{10,1... | collective-permute-start | bytes 983048 | tf_op jit(solution)/shard_map/ppermute | solution.py:299
  6.8 2.1 %collective-permute-start.2 = (f32[5,8,8,256]{3,2,1,0:T(8,128)S(1)}, f32[5,8,8,256]{3,2,1,0:T(8,128)S(1)}, u32[]{:S(2)}, u32[]{:S(2)}) collective-permute-start(f32[5,8,8,256]{3,2,1,0:T(8,128)S(1)} %get-tuple-element.55), channel_id=1, source_target_pairs={{0,3},{1,0},{2,1},{3,2},{4,7},{5,4},{6,5},{7,6},{8,11},{9,8},{10,9... | collective-permute-start | bytes 983048 | tf_op jit(solution)/shard_map/ppermute | solution.py:300
  8.9 3.3 %collective-permute-start.10 = (f32[4,8,8,256]{3,2,1,0:T(8,128)S(1)}, f32[4,8,8,256]{3,2,1,0:T(8,128)S(1)}, u32[]{:S(2)}, u32[]{:S(2)}) collective-permute-start(f32[4,8,8,256]{3,2,1,0:T(8,128)S(1)} %get-tuple-element.68), channel_id=1, source_target_pairs={{0,3},{1,0},{2,1},{3,2},{4,7},{5,4},{6,5},{7,6},{8,11},{9,8},{10,9... | collective-permute-start | bytes 786440 | tf_op jit(solution)/shard_map/ppermute | solution.py:300
  12.1 4.6 %inner.1 = (f32[22,8,8,256]{3,2,1,0:T(8,128)S(1)}, f32[20,8,8,256]{3,2,1,0:T(8,128)S(1)}, f32[18,8,8,256]{3,2,1,0:T(8,128)S(1)}, f32[16,8,8,256]{3,2,1,0:T(8,128...) custom-call(f32[24,8,8,256]{3,2,1,0:T(8,128)S(1)} %get-tuple-element, ...), custom_call_target="tpu_custom_call" | custom-call | tf_op jit(solution)/shard_map/inner/pallas_call | solution.py:303
  16.7 4.4 %collective-permute-start.5 = (f32[6,8,8,256]{3,2,1,0:T(8,128)S(1)}, f32[6,8,8,256]{3,2,1,0:T(8,128)S(1)}, u32[]{:S(2)}, u32[]{:S(2)}) collective-permute-start(f32[6,8,8,256]{3,2,1,0:T(8,128)S(1)} %get-tuple-element.53.refs_0_), channel_id=1, source_target_pairs={{4,8},{8,4},{12,16},{16,12},{20,24},{24,20},{5,9},{9,5},{13,17},{1... | collective-permute-start | bytes 1179656 | tf_op jit(solution)/shard_map/ppermute | solution.py:340
  21.1 1.7 %collective-permute-done.2.high_ref = f32[5,8,8,256]{3,2,1,0:T(8,128)S(1)} collective-permute-done((f32[5,8,8,256]{3,2,1,0:T(8,128)S(1)}, f32[5,8,8,256]{3,2,1,0:T(8,128)S(1)}, u32[]{:S(2)}, u32[]{:S(2)}) %collective-permute-start.2) | collective-permute-done | bytes 327712 | tf_op jit(solution)/shard_map/ppermute | solution.py:300
  22.8 3.6 %edge.3 = (f32[10,8,8,256]{3,2,1,0:T(8,128)S(1)}, f32[16,8,8,256]{3,2,1,0:T(8,128)S(1)}, f32[14,8,8,256]{3,2,1,0:T(8,128)S(1)}, f32[14,8,8,256]{3,2,1,0:T(8,128)...) custom-call(f32[5,8,8,256]{3,2,1,0:T(8,128)S(1)} %collective-permute, ...), custom_call_target="tpu_custom_call" | custom-call | tf_op jit(solution)/shard_map/edge/pallas_call | solution.py:321
  26.4 5.5 %collective-permute-start.6 = (f32[10,8,8,256]{3,2,1,0:T(8,128)S(1)}, f32[10,8,8,256]{3,2,1,0:T(8,128)}, u32[]{:S(2)}, u32[]{:S(2)}) collective-permute-start(f32[10,8,8,256]{3,2,1,0:T(8,128)S(1)} %get-tuple-element.64.refs_1_), channel_id=1, source_target_pairs={{4,8},{8,4},{12,16},{16,12},{20,24},{24,20},{5,9},{9,5},{13,17},{1... | collective-permute-start | bytes 1966088 | tf_op jit(solution)/shard_map/ppermute | solution.py:340
  32.0 0.3 collective-permute-start.7
  32.3 1.8 %collective-permute-done.10.high_ref = f32[4,8,8,256]{3,2,1,0:T(8,128)S(1)} collective-permute-done((f32[4,8,8,256]{3,2,1,0:T(8,128)S(1)}, f32[4,8,8,256]{3,2,1,0:T(8,128)S(1)}, u32[]{:S(2)}, u32[]{:S(2)}) %collective-permute-start.10) | collective-permute-done | bytes 262176 | tf_op jit(solution)/shard_map/ppermute | solution.py:300
  34.1 1.7 %collective-permute-start.8 = (f32[2,8,8,256]{3,2,1,0:T(8,128)S(1)}, f32[2,8,8,256]{3,2,1,0:T(8,128)S(1)}, u32[]{:S(2)}, u32[]{:S(2)}) collective-permute-start(f32[2,8,8,256]{3,2,1,0:T(8,128)S(1)} %get-tuple-element.66), channel_id=1, source_target_pairs={{0,3},{1,0},{2,1},{3,2},{4,7},{5,4},{6,5},{7,6},{8,11},{9,8},{10,9... | collective-permute-start | bytes 393224 | tf_op jit(solution)/shard_map/ppermute | solution.py:300
  35.8 2.9 %edge.4 = (f32[8,8,8,256]{3,2,1,0:T(8,128)S(1)}, f32[14,8,8,256]{3,2,1,0:T(8,128)S(1)}, f32[12,8,8,256]{3,2,1,0:T(8,128)S(1)}, f32[12,8,8,256]{3,2,1,0:T(8,128)S...) custom-call(f32[4,8,8,256]{3,2,1,0:T(8,128)S(1)} %collective-permute, ...), custom_call_target="tpu_custom_call" | custom-call | tf_op jit(solution)/shard_map/edge/pallas_call | solution.py:321
  38.7 0.9 %copy-done.1 = f32[14,8,8,256]{3,2,1,0:T(8,128)} copy-done((f32[14,8,8,256]{3,2,1,0:T(8,128)}, f32[14,8,8,256]{3,2,1,0:T(8,128)S(1)}, u32[]{:S(2)}) %copy-start.1) | copy-done | bytes 917528
  39.6 0.9 %copy-done.3 = f32[12,8,8,256]{3,2,1,0:T(8,128)} copy-done((f32[12,8,8,256]{3,2,1,0:T(8,128)}, f32[12,8,8,256]{3,2,1,0:T(8,128)S(1)}, u32[]{:S(2)}) %copy-start.3) | copy-done | bytes 786456
  40.5 0.9 %copy-done.5 = f32[12,8,8,256]{3,2,1,0:T(8,128)} copy-done((f32[12,8,8,256]{3,2,1,0:T(8,128)}, f32[12,8,8,256]{3,2,1,0:T(8,128)S(1)}, u32[]{:S(2)}) %copy-start.5) | copy-done | bytes 786456
  41.4 0.9 %copy-done.7 = f32[12,8,8,256]{3,2,1,0:T(8,128)} copy-done((f32[12,8,8,256]{3,2,1,0:T(8,128)}, f32[12,8,8,256]{3,2,1,0:T(8,128)S(1)}, u32[]{:S(2)}) %copy-start.7) | copy-done | bytes 786456
  42.3 0.9 %copy-done.9 = f32[12,8,8,256]{3,2,1,0:T(8,128)} copy-done((f32[12,8,8,256]{3,2,1,0:T(8,128)}, f32[12,8,8,256]{3,2,1,0:T(8,128)S(1)}, u32[]{:S(2)}) %copy-start.9) | copy-done | bytes 786456
  43.2 0.9 %copy-done.11 = f32[12,8,8,256]{3,2,1,0:T(8,128)} copy-done((f32[12,8,8,256]{3,2,1,0:T(8,128)}, f32[12,8,8,256]{3,2,1,0:T(8,128)S(1)}, u32[]{:S(2)}) %copy-start.11) | copy-done | bytes 786456
  44.1 0.9 %copy-done.13 = f32[12,8,8,256]{3,2,1,0:T(8,128)} copy-done((f32[12,8,8,256]{3,2,1,0:T(8,128)}, f32[12,8,8,256]{3,2,1,0:T(8,128)S(1)}, u32[]{:S(2)}) %copy-start.13) | copy-done | bytes 786456
  45.0 1.7 %collective-permute-start.3 = (f32[6,8,8,256]{3,2,1,0:T(8,128)S(1)}, f32[6,8,8,256]{3,2,1,0:T(8,128)}, u32[]{:S(2)}, u32[]{:S(2)}) collective-permute-start(f32[6,8,8,256]{3,2,1,0:T(8,128)S(1)} %get-tuple-element.53.refs_0_), channel_id=1, source_target_pairs={{0,4},{4,0},{1,5},{5,1},{2,6},{6,2},{3,7},{7,3},{8,12},{12,8},{9,1... | collective-permute-start | bytes 1179656 | tf_op jit(solution)/shard_map/ppermute | solution.py:339
  46.6 0.7 copy-done.17
  47.3 3.6 %collective-permute-start.12 = (f32[8,8,8,256]{3,2,1,0:T(8,128)S(1)}, f32[8,8,8,256]{3,2,1,0:T(8,128)}, u32[]{:S(2)}, u32[]{:S(2)}) collective-permute-start(f32[8,8,8,256]{3,2,1,0:T(8,128)S(1)} %get-tuple-element.87.refs_2_.refs_0_), channel_id=1, source_target_pairs={{4,8},{8,4},{12,16},{16,12},{20,24},{24,20},{5,9},{9,5},{13,17},{1... | collective-permute-start | bytes 1572872 | tf_op jit(solution)/shard_map/ppermute | solution.py:340
  50.9 0.8 copy-done.15
  51.7 0.1 add_convert_fusion.keep_ref
  51.8 1.2 %copy-done.2 = f32[14,8,8,256]{3,2,1,0:T(8,128)S(1)} copy-done((f32[14,8,8,256]{3,2,1,0:T(8,128)S(1)}, f32[14,8,8,256]{3,2,1,0:T(8,128)}, u32[]{:S(2)}) %copy-start.2) | copy-done | bytes 917528
  53.0 1.1 %copy-done.4 = f32[12,8,8,256]{3,2,1,0:T(8,128)S(1)} copy-done((f32[12,8,8,256]{3,2,1,0:T(8,128)S(1)}, f32[12,8,8,256]{3,2,1,0:T(8,128)}, u32[]{:S(2)}) %copy-start.4) | copy-done | bytes 786456
  54.1 1.1 %copy-done.6 = f32[12,8,8,256]{3,2,1,0:T(8,128)S(1)} copy-done((f32[12,8,8,256]{3,2,1,0:T(8,128)S(1)}, f32[12,8,8,256]{3,2,1,0:T(8,128)}, u32[]{:S(2)}) %copy-start.6) | copy-done | bytes 786456
  55.3 1.1 %copy-done.8 = f32[12,8,8,256]{3,2,1,0:T(8,128)S(1)} copy-done((f32[12,8,8,256]{3,2,1,0:T(8,128)S(1)}, f32[12,8,8,256]{3,2,1,0:T(8,128)}, u32[]{:S(2)}) %copy-start.8) | copy-done | bytes 786456
  56.4 1.1 %copy-done.10 = f32[12,8,8,256]{3,2,1,0:T(8,128)S(1)} copy-done((f32[12,8,8,256]{3,2,1,0:T(8,128)S(1)}, f32[12,8,8,256]{3,2,1,0:T(8,128)}, u32[]{:S(2)}) %copy-start.10) | copy-done | bytes 786456
  57.5 1.1 %copy-done.12 = f32[12,8,8,256]{3,2,1,0:T(8,128)S(1)} copy-done((f32[12,8,8,256]{3,2,1,0:T(8,128)S(1)}, f32[12,8,8,256]{3,2,1,0:T(8,128)}, u32[]{:S(2)}) %copy-start.12) | copy-done | bytes 786456
  58.7 1.1 %copy-done.14 = f32[12,8,8,256]{3,2,1,0:T(8,128)S(1)} copy-done((f32[12,8,8,256]{3,2,1,0:T(8,128)S(1)}, f32[12,8,8,256]{3,2,1,0:T(8,128)}, u32[]{:S(2)}) %copy-start.14) | copy-done | bytes 786456
  59.8 0.9 %copy-done.18 = f32[2,8,8,256]{3,2,1,0:T(8,128)S(1)} copy-done((f32[2,8,8,256]{3,2,1,0:T(8,128)S(1)}, f32[2,8,8,256]{3,2,1,0:T(8,128)}, u32[]{:S(2)}) %copy-start.18) | copy-done | bytes 131096
  60.7 1.8 %edge.5.halo_ref = f32[4,8,8,256]{3,2,1,0:T(8,128)S(1)} custom-call(f32[2,8,8,256]{3,2,1,0:T(8,128)S(1)} %collective-permute-done.7.low_ref, f32[2,8,8,256]{3,2,1,0:T(8,128)S(1)} %copy-done.18, f32[14,8,8,256]{3,2,1,0:T(8,128)S(1)} %get-tuple-element.78.refs_0_, f32[12,8,8,256]{3,2,1,0:T(8,128)S(1)} %copy-done.4, f32[12,8,8,256]{3,2,1,0:T(8,128)S(1)} %copy-done.6, ...), custom_call_target="tpu_custom_call" | custom-call | tf_op jit(solution)/shard_map/edge/pallas_call | solution.py:321
  62.5 2.0 %chemical.1 = (f32[6,8,8,256]{3,2,1,0:T(8,128)S(1)}, f32[10,8,8,256]{3,2,1,0:T(8,128)S(1)}, f32[8,8,8,256]{3,2,1,0:T(8,128)S(1)}) custom-call(f32[4,8,8,256]{3,2,1,0:T(8,128)S(1)} %edge.5.halo_ref, f32[6,8,8,256]{3,2,1,0:T(8,128)S(1)} %get-tuple-element.53.refs_0_, f32[10,8,8,256]{3,2,1,0:T(8,128)S(1)} %get-tuple-element.64.refs_1_, ...), custom_call_target="tpu_custom_call" | custom-call | tf_op jit(solution)/shard_map/chemical/pallas_call | solution.py:346
  64.6 2.1 %sums.2 = (f32[4,8,128]{2,1,0:T(8,128)S(1)}, f32[6,8,8,256]{3,2,1,0:T(8,128)S(1)}, f32[6,8,8,256]{3,2,1,0:T(8,128)S(1)}, f32[10,8,8,256]{3,2,1,0:T(8,128)S(1)}, f32[10,8,8,256]{3,2,1,0:T(8,128)S(1)}) custom-call(s32[2]{0:T(128)S(1)} %add_convert_fusion.keep_ref, f32[6,8,8,256]{3,2,1,0:T(8,128)S(1)} %get-tuple-element.53.refs_0_, ...), custom_call_target="tpu_custom_call" | custom-call | tf_op jit(solution)/shard_map/sums/pallas_call | solution.py:361
  66.7 0.6 collective-permute-start.17
  67.3 1.6 %sums.3 = (f32[4,8,128]{2,1,0:T(8,128)S(1)}, f32[8,8,8,256]{3,2,1,0:T(8,128)S(1)}, f32[8,8,8,256]{3,2,1,0:T(8,128)S(1)}) custom-call(s32[2]{0:T(128)S(1)} %add_convert_fusion.keep_ref, f32[8,8,8,256]{3,2,1,0:T(8,128)S(1)} %get-tuple-element.87.refs_2_.refs_0_, f32[8,8,8,256]{3,2,1,0:T(8,128)} %collective-permute-done.11.refs_1_, ...), custom_call_target="tpu_custom_call" | custom-call | tf_op jit(solution)/shard_map/sums/pallas_call | solution.py:361
  68.9 0.1 collective-permute-start.18
  69.0 0.5 collective-permute-start.16
  69.4 2.6 %collective-permute-done.13 = f32[4,8,128]{2,1,0:T(8,128)S(1)} collective-permute-done((f32[4,8,128]{2,1,0:T(8,128)S(1)}, f32[4,8,128]{2,1,0:T(8,128)S(1)}, u32[]{:S(2)}, u32[]{:S(2)}) %collective-permute-start.13) | collective-permute-done | bytes 16416 | tf_op jit(solution)/shard_map/ppermute | solution.py:253
  72.1 3.5 %collective-permute-done.14 = f32[4,8,128]{2,1,0:T(8,128)S(1)} collective-permute-done((f32[4,8,128]{2,1,0:T(8,128)S(1)}, f32[4,8,128]{2,1,0:T(8,128)S(1)}, u32[]{:S(2)}, u32[]{:S(2)}) %collective-permute-start.14) | collective-permute-done | bytes 16416 | tf_op jit(solution)/shard_map/ppermute | solution.py:253
  75.5 2.4 %collective-permute-start.15 = (f32[4,8,128]{2,1,0:T(8,128)S(1)}, f32[4,8,128]{2,1,0:T(8,128)S(1)}, u32[]{:S(2)}, u32[]{:S(2)}) collective-permute-start(f32[4,8,128]{2,1,0:T(8,128)S(1)} %add.25), channel_id=1, source_target_pairs={{0,4},{4,0},{1,5},{5,1},{2,6},{6,2},{3,7},{7,3},{8,12},{12,8},{9,1... | collective-permute-start | bytes 49160 | tf_op jit(solution)/shard_map/ppermute | solution.py:374
  77.9 0.8 %collective-permute-done.15 = f32[4,8,128]{2,1,0:T(8,128)S(1)} collective-permute-done((f32[4,8,128]{2,1,0:T(8,128)S(1)}, f32[4,8,128]{2,1,0:T(8,128)S(1)}, u32[]{:S(2)}, u32[]{:S(2)}) %collective-permute-start.15) | collective-permute-done | bytes 16416 | tf_op jit(solution)/shard_map/ppermute | solution.py:374
  78.8 3.0 %last.1 = f32[2,32,24,256]{3,2,1,0:T(8,128)} custom-call(s32[2]{0:T(128)S(1)} %add_convert_fusion.keep_ref, s32[1]{0:T(128)} %bitcast.2.who_ref, f32[2,4,8,128]{3,2,1,0:T(8,128)S(1)} %pad_maximum_fusion.sums_ref, f32[6,8,8,256]{3,2,1,0:T(8,128)S(1)} %get-tuple-element.93.refs_0_, f32[10,8,8,256]{3,2,1,0:T(8,128)S(1)} %get-tuple-element.94.refs_1_, ...), custom_call_target="tpu_custom_call" | custom-call | tf_op jit(solution)/shard_map/last/pallas_call | solution.py:375
  (43 shorter events, 0.2 us)
Async XLA Ops:
  0.0 4.0 %copy-start = (f32[2,32,24,256]{3,2,1,0:T(8,128)S(1)}, f32[2,32,24,256]{3,2,1,0:T(8,128)}, u32[]{:S(2)}) copy-start(f32[2,32,24,256]{3,2,1,0:T(8,128)} %whole_ref.1) | copy-start | bytes 4718596
  1.3 2.7 %collective-permute-start = (f32[32,24,256]{2,1,0:T(8,128)S(1)}, f32[32,24,256]{2,1,0:T(8,128)S(1)}, u32[]{:S(2)}, u32[]{:S(2)}) collective-permute-start(f32[32,24,256]{2,1,0:T(8,128)S(1)} %dynamic-slice_bitcast_fusion), channel_id=1, source_target_pairs={{0,4},{4,0},{1,5},{5,1},{2,6},{6,2},{3,7},{7,3},{8,12},{12,8},{9,1... | collective-permute-start | bytes 2359304 | tf_op jit(solution)/shard_map/ppermute | solution.py:276
  5.4 15.7 %collective-permute-start.1 = (f32[5,8,8,256]{3,2,1,0:T(8,128)S(1)}, f32[5,8,8,256]{3,2,1,0:T(8,128)S(1)}, u32[]{:S(2)}, u32[]{:S(2)}) collective-permute-start(f32[5,8,8,256]{3,2,1,0:T(8,128)S(1)} %get-tuple-element.54), channel_id=1, source_target_pairs={{0,1},{1,2},{2,3},{3,0},{4,5},{5,6},{6,7},{7,4},{8,9},{9,10},{10,1... | collective-permute-start | bytes 983048 | tf_op jit(solution)/shard_map/ppermute | solution.py:299
  6.8 16.1 %collective-permute-start.2 = (f32[5,8,8,256]{3,2,1,0:T(8,128)S(1)}, f32[5,8,8,256]{3,2,1,0:T(8,128)S(1)}, u32[]{:S(2)}, u32[]{:S(2)}) collective-permute-start(f32[5,8,8,256]{3,2,1,0:T(8,128)S(1)} %get-tuple-element.55), channel_id=1, source_target_pairs={{0,3},{1,0},{2,1},{3,2},{4,7},{5,4},{6,5},{7,6},{8,11},{9,8},{10,9... | collective-permute-start | bytes 983048 | tf_op jit(solution)/shard_map/ppermute | solution.py:300
  8.9 23.1 %collective-permute-start.9 = (f32[4,8,8,256]{3,2,1,0:T(8,128)S(1)}, f32[4,8,8,256]{3,2,1,0:T(8,128)S(1)}, u32[]{:S(2)}, u32[]{:S(2)}) collective-permute-start(f32[4,8,8,256]{3,2,1,0:T(8,128)S(1)} %get-tuple-element.67), channel_id=1, source_target_pairs={{0,1},{1,2},{2,3},{3,0},{4,5},{5,6},{6,7},{7,4},{8,9},{9,10},{10,1... | collective-permute-start | bytes 786440 | tf_op jit(solution)/shard_map/ppermute | solution.py:299
  8.9 25.2 %collective-permute-start.10 = (f32[4,8,8,256]{3,2,1,0:T(8,128)S(1)}, f32[4,8,8,256]{3,2,1,0:T(8,128)S(1)}, u32[]{:S(2)}, u32[]{:S(2)}) collective-permute-start(f32[4,8,8,256]{3,2,1,0:T(8,128)S(1)} %get-tuple-element.68), channel_id=1, source_target_pairs={{0,3},{1,0},{2,1},{3,2},{4,7},{5,4},{6,5},{7,6},{8,11},{9,8},{10,9... | collective-permute-start | bytes 786440 | tf_op jit(solution)/shard_map/ppermute | solution.py:300
  16.7 34.2 %collective-permute-start.5 = (f32[6,8,8,256]{3,2,1,0:T(8,128)S(1)}, f32[6,8,8,256]{3,2,1,0:T(8,128)S(1)}, u32[]{:S(2)}, u32[]{:S(2)}) collective-permute-start(f32[6,8,8,256]{3,2,1,0:T(8,128)S(1)} %get-tuple-element.53.refs_0_), channel_id=1, source_target_pairs={{4,8},{8,4},{12,16},{16,12},{20,24},{24,20},{5,9},{9,5},{13,17},{1... | collective-permute-start | bytes 1179656 | tf_op jit(solution)/shard_map/ppermute | solution.py:340
  26.4 38.1 %collective-permute-start.6 = (f32[10,8,8,256]{3,2,1,0:T(8,128)S(1)}, f32[10,8,8,256]{3,2,1,0:T(8,128)}, u32[]{:S(2)}, u32[]{:S(2)}) collective-permute-start(f32[10,8,8,256]{3,2,1,0:T(8,128)S(1)} %get-tuple-element.64.refs_1_), channel_id=1, source_target_pairs={{4,8},{8,4},{12,16},{16,12},{20,24},{24,20},{5,9},{9,5},{13,17},{1... | collective-permute-start | bytes 1966088 | tf_op jit(solution)/shard_map/ppermute | solution.py:340
  31.9 32.7 %collective-permute-start.4 = (f32[10,8,8,256]{3,2,1,0:T(8,128)S(1)}, f32[10,8,8,256]{3,2,1,0:T(8,128)}, u32[]{:S(2)}, u32[]{:S(2)}) collective-permute-start(f32[10,8,8,256]{3,2,1,0:T(8,128)S(1)} %get-tuple-element.64.refs_1_), channel_id=1, source_target_pairs={{0,4},{4,0},{1,5},{5,1},{2,6},{6,2},{3,7},{7,3},{8,12},{12,8},{9,1... | collective-permute-start | bytes 1966088 | tf_op jit(solution)/shard_map/ppermute | solution.py:339
  32.0 13.0 %collective-permute-start.7 = (f32[2,8,8,256]{3,2,1,0:T(8,128)S(1)}, f32[2,8,8,256]{3,2,1,0:T(8,128)S(1)}, u32[]{:S(2)}, u32[]{:S(2)}) collective-permute-start(f32[2,8,8,256]{3,2,1,0:T(8,128)S(1)} %get-tuple-element.65), channel_id=1, source_target_pairs={{0,1},{1,2},{2,3},{3,0},{4,5},{5,6},{6,7},{7,4},{8,9},{9,10},{10,1... | collective-permute-start | bytes 393224 | tf_op jit(solution)/shard_map/ppermute | solution.py:299
  34.1 12.5 %collective-permute-start.8 = (f32[2,8,8,256]{3,2,1,0:T(8,128)S(1)}, f32[2,8,8,256]{3,2,1,0:T(8,128)S(1)}, u32[]{:S(2)}, u32[]{:S(2)}) collective-permute-start(f32[2,8,8,256]{3,2,1,0:T(8,128)S(1)} %get-tuple-element.66), channel_id=1, source_target_pairs={{0,3},{1,0},{2,1},{3,2},{4,7},{5,4},{6,5},{7,6},{8,11},{9,8},{10,9... | collective-permute-start | bytes 393224 | tf_op jit(solution)/shard_map/ppermute | solution.py:300
  38.7 0.9 %copy-start.1 = (f32[14,8,8,256]{3,2,1,0:T(8,128)}, f32[14,8,8,256]{3,2,1,0:T(8,128)S(1)}, u32[]{:S(2)}) copy-start(f32[14,8,8,256]{3,2,1,0:T(8,128)S(1)} %get-tuple-element.84.refs_6_) | copy-start | bytes 2752516
  39.6 0.9 %copy-start.3 = (f32[12,8,8,256]{3,2,1,0:T(8,128)}, f32[12,8,8,256]{3,2,1,0:T(8,128)S(1)}, u32[]{:S(2)}) copy-start(f32[12,8,8,256]{3,2,1,0:T(8,128)S(1)} %get-tuple-element.79.refs_1_) | copy-start | bytes 2359300
  40.5 0.9 %copy-start.5 = (f32[12,8,8,256]{3,2,1,0:T(8,128)}, f32[12,8,8,256]{3,2,1,0:T(8,128)S(1)}, u32[]{:S(2)}) copy-start(f32[12,8,8,256]{3,2,1,0:T(8,128)S(1)} %get-tuple-element.80.refs_2_) | copy-start | bytes 2359300
  41.4 0.9 %copy-start.7 = (f32[12,8,8,256]{3,2,1,0:T(8,128)}, f32[12,8,8,256]{3,2,1,0:T(8,128)S(1)}, u32[]{:S(2)}) copy-start(f32[12,8,8,256]{3,2,1,0:T(8,128)S(1)} %get-tuple-element.82.refs_4_) | copy-start | bytes 2359300
  42.3 0.9 %copy-start.9 = (f32[12,8,8,256]{3,2,1,0:T(8,128)}, f32[12,8,8,256]{3,2,1,0:T(8,128)S(1)}, u32[]{:S(2)}) copy-start(f32[12,8,8,256]{3,2,1,0:T(8,128)S(1)} %get-tuple-element.83.refs_5_) | copy-start | bytes 2359300
  43.2 0.9 %copy-start.11 = (f32[12,8,8,256]{3,2,1,0:T(8,128)}, f32[12,8,8,256]{3,2,1,0:T(8,128)S(1)}, u32[]{:S(2)}) copy-start(f32[12,8,8,256]{3,2,1,0:T(8,128)S(1)} %get-tuple-element.85.refs_7_) | copy-start | bytes 2359300
  44.1 0.9 %copy-start.13 = (f32[12,8,8,256]{3,2,1,0:T(8,128)}, f32[12,8,8,256]{3,2,1,0:T(8,128)S(1)}, u32[]{:S(2)}) copy-start(f32[12,8,8,256]{3,2,1,0:T(8,128)S(1)} %get-tuple-element.86.refs_8_) | copy-start | bytes 2359300
  45.0 19.6 %collective-permute-start.3 = (f32[6,8,8,256]{3,2,1,0:T(8,128)S(1)}, f32[6,8,8,256]{3,2,1,0:T(8,128)}, u32[]{:S(2)}, u32[]{:S(2)}) collective-permute-start(f32[6,8,8,256]{3,2,1,0:T(8,128)S(1)} %get-tuple-element.53.refs_0_), channel_id=1, source_target_pairs={{0,4},{4,0},{1,5},{5,1},{2,6},{6,2},{3,7},{7,3},{8,12},{12,8},{9,1... | collective-permute-start | bytes 1179656 | tf_op jit(solution)/shard_map/ppermute | solution.py:339
  46.6 0.7 copy-start.17
  47.3 20.0 %collective-permute-start.12 = (f32[8,8,8,256]{3,2,1,0:T(8,128)S(1)}, f32[8,8,8,256]{3,2,1,0:T(8,128)}, u32[]{:S(2)}, u32[]{:S(2)}) collective-permute-start(f32[8,8,8,256]{3,2,1,0:T(8,128)S(1)} %get-tuple-element.87.refs_2_.refs_0_), channel_id=1, source_target_pairs={{4,8},{8,4},{12,16},{16,12},{20,24},{24,20},{5,9},{9,5},{13,17},{1... | collective-permute-start | bytes 1572872 | tf_op jit(solution)/shard_map/ppermute | solution.py:340
  50.9 0.8 copy-start.15
  51.7 15.6 %collective-permute-start.11 = (f32[8,8,8,256]{3,2,1,0:T(8,128)S(1)}, f32[8,8,8,256]{3,2,1,0:T(8,128)}, u32[]{:S(2)}, u32[]{:S(2)}) collective-permute-start(f32[8,8,8,256]{3,2,1,0:T(8,128)S(1)} %get-tuple-element.87.refs_2_.refs_0_), channel_id=1, source_target_pairs={{0,4},{4,0},{1,5},{5,1},{2,6},{6,2},{3,7},{7,3},{8,12},{12,8},{9,1... | collective-permute-start | bytes 1572872 | tf_op jit(solution)/shard_map/ppermute | solution.py:339
  51.8 1.2 %copy-start.2 = (f32[14,8,8,256]{3,2,1,0:T(8,128)S(1)}, f32[14,8,8,256]{3,2,1,0:T(8,128)}, u32[]{:S(2)}) copy-start(f32[14,8,8,256]{3,2,1,0:T(8,128)} %copy-done.1) | copy-start | bytes 2752516
  53.0 1.1 %copy-start.4 = (f32[12,8,8,256]{3,2,1,0:T(8,128)S(1)}, f32[12,8,8,256]{3,2,1,0:T(8,128)}, u32[]{:S(2)}) copy-start(f32[12,8,8,256]{3,2,1,0:T(8,128)} %copy-done.3) | copy-start | bytes 2359300
  54.1 1.1 %copy-start.6 = (f32[12,8,8,256]{3,2,1,0:T(8,128)S(1)}, f32[12,8,8,256]{3,2,1,0:T(8,128)}, u32[]{:S(2)}) copy-start(f32[12,8,8,256]{3,2,1,0:T(8,128)} %copy-done.5) | copy-start | bytes 2359300
  55.2 1.1 %copy-start.8 = (f32[12,8,8,256]{3,2,1,0:T(8,128)S(1)}, f32[12,8,8,256]{3,2,1,0:T(8,128)}, u32[]{:S(2)}) copy-start(f32[12,8,8,256]{3,2,1,0:T(8,128)} %copy-done.7) | copy-start | bytes 2359300
  56.4 1.1 %copy-start.10 = (f32[12,8,8,256]{3,2,1,0:T(8,128)S(1)}, f32[12,8,8,256]{3,2,1,0:T(8,128)}, u32[]{:S(2)}) copy-start(f32[12,8,8,256]{3,2,1,0:T(8,128)} %copy-done.9) | copy-start | bytes 2359300
  57.5 1.1 %copy-start.12 = (f32[12,8,8,256]{3,2,1,0:T(8,128)S(1)}, f32[12,8,8,256]{3,2,1,0:T(8,128)}, u32[]{:S(2)}) copy-start(f32[12,8,8,256]{3,2,1,0:T(8,128)} %copy-done.11) | copy-start | bytes 2359300
  58.6 1.1 %copy-start.14 = (f32[12,8,8,256]{3,2,1,0:T(8,128)S(1)}, f32[12,8,8,256]{3,2,1,0:T(8,128)}, u32[]{:S(2)}) copy-start(f32[12,8,8,256]{3,2,1,0:T(8,128)} %copy-done.13) | copy-start | bytes 2359300
  59.8 0.9 %copy-start.18 = (f32[2,8,8,256]{3,2,1,0:T(8,128)S(1)}, f32[2,8,8,256]{3,2,1,0:T(8,128)}, u32[]{:S(2)}) copy-start(f32[2,8,8,256]{3,2,1,0:T(8,128)} %copy-done.17) | copy-start | bytes 393220
  62.5 2.1 %copy-start.16 = (f32[6,8,8,256]{3,2,1,0:T(8,128)S(1)}, f32[6,8,8,256]{3,2,1,0:T(8,128)}, u32[]{:S(2)}) copy-start(f32[6,8,8,256]{3,2,1,0:T(8,128)} %copy-done.15) | copy-start | bytes 1179652
  66.7 12.1 %collective-permute-start.17 = (f32[10,8,8,256]{3,2,1,0:T(8,128)S(1)}, f32[10,8,8,256]{3,2,1,0:T(8,128)S(1)}, u32[]{:S(2)}, u32[]{:S(2)}) collective-permute-start(f32[10,8,8,256]{3,2,1,0:T(8,128)S(1)} %get-tuple-element.97), channel_id=1, source_target_pairs={{0,4},{4,0},{1,5},{5,1},{2,6},{6,2},{3,7},{7,3},{8,12},{12,8},{9,1... | collective-permute-start | bytes 1966088 | tf_op jit(solution)/shard_map/ppermute | solution.py:372
  68.9 9.9 %collective-permute-start.18 = (f32[8,8,8,256]{3,2,1,0:T(8,128)S(1)}, f32[8,8,8,256]{3,2,1,0:T(8,128)S(1)}, u32[]{:S(2)}, u32[]{:S(2)}) collective-permute-start(f32[8,8,8,256]{3,2,1,0:T(8,128)S(1)} %get-tuple-element.98), channel_id=1, source_target_pairs={{0,4},{4,0},{1,5},{5,1},{2,6},{6,2},{3,7},{7,3},{8,12},{12,8},{9,1... | collective-permute-start | bytes 1572872 | tf_op jit(solution)/shard_map/ppermute | solution.py:372
  69.0 9.8 %collective-permute-start.16 = (f32[6,8,8,256]{3,2,1,0:T(8,128)S(1)}, f32[6,8,8,256]{3,2,1,0:T(8,128)S(1)}, u32[]{:S(2)}, u32[]{:S(2)}) collective-permute-start(f32[6,8,8,256]{3,2,1,0:T(8,128)S(1)} %get-tuple-element.96), channel_id=1, source_target_pairs={{0,4},{4,0},{1,5},{5,1},{2,6},{6,2},{3,7},{7,3},{8,12},{12,8},{9,1... | collective-permute-start | bytes 1179656 | tf_op jit(solution)/shard_map/ppermute | solution.py:372
  69.4 2.6 %collective-permute-start.13 = (f32[4,8,128]{2,1,0:T(8,128)S(1)}, f32[4,8,128]{2,1,0:T(8,128)S(1)}, u32[]{:S(2)}, u32[]{:S(2)}) collective-permute-start(f32[4,8,128]{2,1,0:T(8,128)S(1)} %add.23), channel_id=1, source_target_pairs={{0,1},{1,0},{2,3},{3,2},{4,5},{5,4},{6,7},{7,6},{8,9},{9,8},{10,11... | collective-permute-start | bytes 49160 | tf_op jit(solution)/shard_map/ppermute | solution.py:253
  72.1 3.5 %collective-permute-start.14 = (f32[4,8,128]{2,1,0:T(8,128)S(1)}, f32[4,8,128]{2,1,0:T(8,128)S(1)}, u32[]{:S(2)}, u32[]{:S(2)}) collective-permute-start(f32[4,8,128]{2,1,0:T(8,128)S(1)} %add.24), channel_id=1, source_target_pairs={{0,2},{1,3},{2,0},{3,1},{4,6},{5,7},{6,4},{7,5},{8,10},{9,11},{10,... | collective-permute-start | bytes 49160 | tf_op jit(solution)/shard_map/ppermute | solution.py:253
  75.5 3.2 %collective-permute-start.15 = (f32[4,8,128]{2,1,0:T(8,128)S(1)}, f32[4,8,128]{2,1,0:T(8,128)S(1)}, u32[]{:S(2)}, u32[]{:S(2)}) collective-permute-start(f32[4,8,128]{2,1,0:T(8,128)S(1)} %add.25), channel_id=1, source_target_pairs={{0,4},{4,0},{1,5},{5,1},{2,6},{6,2},{3,7},{7,3},{8,12},{12,8},{9,1... | collective-permute-start | bytes 49160 | tf_op jit(solution)/shard_map/ppermute | solution.py:374

commit v3 on v2

--- a/solution.py
+++ b/solution.py
@@ -67,38 +67,75 @@
             ref[y + off] = level_row(levels[side], m, y)
 
 
-def first_kernel(rows, sends, who_ref, whole_ref, recv_ref, *refs):
-    slab, pieces = refs[0], refs[1:-2]
-    halves, sems = refs[-2:]
-    _, tiles, half, _, lanes = halves.shape
-    planes = 2 * half // SUB
+def cut_kernel(whole_ref, half_ref, sems):
+    lanes = half_ref.shape[-1]
     copies = []
-    for i, src in enumerate((whole_ref.at[who_ref[0]], recv_ref)):
-        for z in range(tiles):
-            part = src.at[:, :, pl.ds(z * lanes, lanes)]
-            copies.append(pltpu.make_async_copy(part, halves.at[i, z], sems.at[i, z]))
-    for copy in copies:
-        copy.start()
+    for z in range(half_ref.shape[0]):
+        part = whole_ref.at[1 - lax.axis_index("gx"), :, :, pl.ds(z * lanes, lanes)]
+        copies.append(pltpu.make_async_copy(part, half_ref.at[z], sems.at[z]))
+        copies[-1].start()
     for copy in copies:
         copy.wait()
-    flat = halves.reshape(2, tiles, half * rows, lanes)
+
+
+def own_kernel(whole_ref, slab_ref, half_ref, sems):
+    tiles, half, rows, lanes = half_ref.shape
+    planes = slab_ref.shape[1]
+    copies = []
+    for z in range(tiles):
+        part = whole_ref.at[lax.axis_index("gx"), :, :, pl.ds(z * lanes, lanes)]
+        copies.append(pltpu.make_async_copy(part, half_ref.at[z], sems.at[z]))
+        copies[-1].start()
+    for copy in copies:
+        copy.wait()
+    flat = half_ref.reshape(tiles, half * rows, lanes)
     h = SUB // 2
 
     def body(y, carry):
         for r in range(planes):
             where = pl.ds(r * rows + y, h, stride=planes * rows)
-            for i in range(2):
-                for z in range(tiles):
-                    slab[y, r, i * h : i * h + h, z * lanes : (z + 1) * lanes] = flat[i, z, where, :]
+            for z in range(tiles):
+                slab_ref[y, r, :h, z * lanes : (z + 1) * lanes] = flat[z, where, :]
         return carry
 
     lax.fori_loop(0, rows, body, 0)
-    for piece, (start, count) in zip(pieces, sends):
-        def copy(i, carry, piece=piece, start=start):
-            piece[i] = slab[start + i]
+
+
+def first_kernel(rows, sends, own_ref, recv_ref, *refs):
+    slab_ref, pieces = refs[0], refs[1:]
+    tiles, half, _, lanes = recv_ref.shape
+    planes = slab_ref.shape[1]
+    flat = recv_ref.reshape(tiles, half * rows, lanes)
+    h = SUB // 2
+
+    def row(y):
+        for r in range(planes):
+            where = pl.ds(r * rows + y, h, stride=planes * rows)
+            for z in range(tiles):
+                at = slice(z * lanes, (z + 1) * lanes)
+                value = jnp.concatenate([own_ref[y, r, :h, at], flat[z, where, :]], axis=0)
+                slab_ref[y, r, :, at] = value
+                yield r, at, value
+
+    def plain(y, carry):
+        for _ in row(y):
+            pass
+        return carry
+
+    done = 0
+    for start, count, piece in sorted(((*send, piece) for send, piece in zip(sends, pieces)), key=lambda s: s[0]):
+        if start > done:
+            lax.fori_loop(done, start, plain, 0)
+
+        def body(i, carry, start=start, piece=piece):
+            for r, at, value in row(start + i):
+                piece[i, r, :, at] = value
             return carry
 
-        lax.fori_loop(0, count, copy, 0)
+        lax.fori_loop(0, count, body, 0)
+        done = start + count
+    if rows > done:
+        lax.fori_loop(done, rows, plain, 0)
 
 
 def inner_kernel(rows, slab_ref, *outs):
@@ -143,6 +180,11 @@
     if beyond:
         into = ((fields[-1], beyond), (fields[-1], beyond - rows))
         rows_of(sides, FIELD, (-beyond, rows), (0, rows + beyond), into)
+
+
+def keeping(gx):
+    image = 2 * lax.axis_index("chain") + gx
+    return jnp.logical_or(image == 0, image == 2 * lax.axis_size("chain") - 1)
 
 
 def chemical_kernel(rows, segments, halo_ref, *refs):
@@ -165,16 +207,16 @@
                 out[first + i] = potential_row(field_ref[y + 2], w_ref[y + 1], neighbours(w_ref, y + 1))
 
 
-def sums_kernel(n, lanes, keep_ref, *refs):
+def sums_kernel(n, lanes, before_ref, *refs):
     sums_ref, outs = refs[4 * n], refs[4 * n + 1 :]
-    keep = keep_ref[0] != 0
+    keep = keeping(lax.axis_index("gx"))
     planes, nz = refs[0].shape[1], refs[0].shape[3]
 
     def fold(a):
         return sum(a[r, :, z : z + lanes] for r in range(planes) for z in range(0, nz, lanes))
 
     low = lax.broadcasted_iota(jnp.int32, (planes, SUB, nz), 1) < SUB // 2
-    totals = [jnp.zeros((SUB, lanes), jnp.float32)] * 4
+    totals = [before_ref[q] for q in range(4)] if before_ref is not None else [jnp.zeros((SUB, lanes), jnp.float32)] * 4
     for j in range(n):
         piece, partner, chain, chemical = refs[j : 4 * n : n]
         mine, send = outs[2 * j], outs[2 * j + 1]
@@ -196,7 +238,7 @@
         sums_ref[q] = totals[q]
 
 
-def last_kernel(cells, segments, keep_ref, who_ref, sums_ref, *refs):
+def last_kernel(cells, segments, mine_sums, other_sums, *refs):
     n = len(segments)
     out_ref, natural, sems = refs[2 * n :]
     _, half, rows, _ = out_ref.shape
@@ -205,19 +247,24 @@
     planes = 2 * half // SUB
     h = SUB // 2
 
+    gx = lax.axis_index("gx")
+    images = (gx, 1 - gx)
+
     def factor(i):
+        sums_ref = (mine_sums, other_sums)[i]
+
         def total(q):
-            return jnp.sum(sums_ref[i, q], keepdims=True) / cells
+            return jnp.sum(sums_ref[q], keepdims=True) / cells
 
         scale = lax.rsqrt(total(0) + epsilon)
         spring = stiffness * (jnp.sqrt(total(1) + epsilon) - jnp.sqrt(total(2) + epsilon))
         k = step_size * total(3) * scale * scale + spring * scale
-        return jnp.where(keep_ref[i] != 0, jnp.zeros_like(k), k)
+        return jnp.where(keeping(images[i]), jnp.zeros_like(k), k)
 
     copies = []
     for i in range(2):
         k = factor(i)
-        image = who_ref[0] if i == 0 else 1 - who_ref[0]
+        image = images[i]
         for parts, ref in zip(segments, refs[i * n : (i + 1) * n]):
             for start, count, first in parts:
                 def body(j, carry, start=start, first=first, ref=ref, i=i, k=k):
@@ -244,13 +291,29 @@
     return [(i, (i + distance) % n) for i in range(n)]
 
 
+def add_kernel(a_ref, b_ref, out_ref):
+    out_ref[...] = a_ref[...] + b_ref[...]
+
+
+def add(a, b):
+    return pl.pallas_call(
+        add_kernel,
+        out_shape=jax.ShapeDtypeStruct(a.shape, a.dtype),
+        in_specs=[VMEM] * 2,
+        out_specs=VMEM,
+        compiler_params=PARAMS,
+        name="add",
+    )(a, b)
+
+
 def total_over(value, axis):
     n = lax.axis_size(axis)
     if n & (n - 1):
-        return value + sum(lax.ppermute(value, axis, ring(axis, d)) for d in range(1, n))
+        others = [lax.ppermute(value, axis, ring(axis, d)) for d in range(1, n)]
+        return functools.reduce(add, others, value)
     d = 1
     while d < n:
-        value = value + lax.ppermute(value, axis, [(i, i ^ d) for i in range(n)])
+        value = add(value, lax.ppermute(value, axis, [(i, i ^ d) for i in range(n)]))
         d *= 2
     return value
 
@@ -262,18 +325,33 @@
     planes = 2 * half // SUB
     cells = 2 * half * rows * lax.axis_size("gy") * nz
     chains = lax.axis_size("chain")
-    gx = lax.axis_index("gx")
-    chain = lax.axis_index("chain")
     swap = [(0, 1), (1, 0)]
     tiles = nz // LANES
-    smem = pl.BlockSpec(memory_space=pltpu.SMEM)
+    hbm = pl.BlockSpec(memory_space=pl.ANY)
 
     def slab(n):
         return jax.ShapeDtypeStruct((n, planes, SUB, nz), jnp.float32)
 
-    who = gx.astype(jnp.int32)[None]
-    other = lax.dynamic_index_in_dim(initial_path, 1 - gx, 0, keepdims=False)
+    part = (tiles, half, rows, LANES)
+    other = pl.pallas_call(
+        cut_kernel,
+        out_shape=jax.ShapeDtypeStruct(part, jnp.float32),
+        in_specs=[hbm],
+        out_specs=VMEM,
+        scratch_shapes=[pltpu.SemaphoreType.DMA((tiles,))],
+        compiler_params=PARAMS,
+        name="cut",
+    )(initial_path)
     recv = lax.ppermute(other, "gx", swap)
+    own = pl.pallas_call(
+        own_kernel,
+        out_shape=slab(rows),
+        in_specs=[hbm],
+        out_specs=VMEM,
+        scratch_shapes=[pltpu.VMEM(part, jnp.float32), pltpu.SemaphoreType.DMA((tiles,))],
+        compiler_params=PARAMS,
+        name="own",
+    )(initial_path)
     known = [0]
     for n in CHUNKS:
         known.append(known[-1] + n)
@@ -283,15 +361,11 @@
     first = pl.pallas_call(
         functools.partial(first_kernel, rows, sends),
         out_shape=[slab(rows)] + [slab(n) for _, n in sends],
-        in_specs=[smem, pl.BlockSpec(memory_space=pl.ANY), pl.BlockSpec(memory_space=pl.ANY)],
+        in_specs=[VMEM] * 2,
         out_specs=[VMEM] * (1 + len(sends)),
-        scratch_shapes=[
-            pltpu.VMEM((2, tiles, half, rows, LANES), jnp.float32),
-            pltpu.SemaphoreType.DMA((2, tiles)),
-        ],
         compiler_params=PARAMS,
         name="first",
-    )(who, initial_path, recv)
+    )(own, recv)
     halos = []
     for j in range(len(CHUNKS)):
         low, high = first[1 + 2 * j], first[2 + 2 * j]
@@ -339,10 +413,6 @@
     from_partner = [lax.ppermute(p, "gx", swap) for p in pieces]
     from_chain = [lax.ppermute(p, ("chain", "gx"), along_chain) for p in pieces]
 
-    def keeping(image):
-        return jnp.logical_or(image == 0, image == 2 * chains - 1).astype(jnp.int32)
-
-    keep = jnp.stack([keeping(2 * chain + gx), keeping(2 * chain + 1 - gx)])
     chemical = pl.pallas_call(
         functools.partial(chemical_kernel, rows, segments),
         out_shape=[slab(p.shape[0]) for p in pieces],
@@ -355,35 +425,36 @@
         compiler_params=PARAMS,
         name="chemical",
     )(halo, *pieces)
-    mine, halfway, total = [], [], 0.0
+    mine, halfway, total = [], [], None
     for some in (slice(0, -1), slice(-1, None)):
         n = len(pieces[some])
-        sums, *outs = pl.pallas_call(
-            functools.partial(sums_kernel, n, LANES),
+        before = [] if total is None else [total]
+        kernel = functools.partial(sums_kernel, n, LANES)
+        total, *outs = pl.pallas_call(
+            kernel if before else functools.partial(kernel, None),
             out_shape=[jax.ShapeDtypeStruct((4, SUB, LANES), jnp.float32)]
             + [slab(p.shape[0]) for p in pieces[some] for _ in range(2)],
-            in_specs=[smem] + [VMEM] * (4 * n),
+            in_specs=[VMEM] * (4 * n + len(before)),
             out_specs=[VMEM] * (1 + 2 * n),
             compiler_params=PARAMS,
             name="sums",
-        )(keep, *pieces[some], *from_partner[some], *from_chain[some], *chemical[some])
-        total = total + sums
+        )(*before, *pieces[some], *from_partner[some], *from_chain[some], *chemical[some])
         mine += outs[::2]
         halfway += [lax.ppermute(send, "gx", swap) for send in outs[1::2]]
     total = total_over(total, "gy")
-    totals = jnp.stack([total, lax.ppermute(total, "gx", swap)])
+    other = lax.ppermute(total, "gx", swap)
     return pl.pallas_call(
         functools.partial(last_kernel, cells, segments),
         out_shape=jax.ShapeDtypeStruct(initial_path.shape, jnp.float32),
-        in_specs=[smem, smem] + [VMEM] * (1 + 2 * len(pieces)),
-        out_specs=pl.BlockSpec(memory_space=pl.ANY),
+        in_specs=[VMEM] * (2 + 2 * len(pieces)),
+        out_specs=hbm,
         scratch_shapes=[
-            pltpu.VMEM((2, tiles, half, rows, LANES), jnp.float32),
+            pltpu.VMEM((2, *part), jnp.float32),
             pltpu.SemaphoreType.DMA((2, tiles)),
         ],
         compiler_params=PARAMS,
         name="last",
-    )(keep, who, totals, *mine, *halfway)
+    )(total, other, *mine, *halfway)
 
 
 def solution(mesh):

time: 82.9 us -> 71.6 us (0.86)
  local copies, waits for them, and re-layouts: 17.9 us -> 1.41 us
  starting transfers between devices: 28.2 us -> 33.1 us
  waiting for transfers between devices: 12.3 us -> 16.8 us
  Pallas kernels: 23 us -> 19.8 us
    unnamed x38 -> x2, local copies, waits for them, and re-layouts: 16.6 us -> 1.41 us
    ppermute x3, waiting for transfers between devices: 0.01 us -> 6.43 us  [per_device(): from_chain = [lax.ppermute(p, ('chain', 'gx'), along_chain) for p in pieces]]
    ppermute x3, starting transfers between devices: 2.37 us -> 4.6 us  [the longest x1 2.89 us: per_device(): other = lax.ppermute(total, 'gx', swap)]
    pallas_call x2 -> x6, Pallas kernels: 3.69 us -> 1.77 us  [the longest x2 1.04 us: per_device(): pl.pallas_call(kernel if before else functools.partial(kernel, None), out...]
    ppermute x3, starting transfers between devices: 1.73 us -> 3.53 us  [per_device(): from_partner = [lax.ppermute(p, 'gx', swap) for p in pieces]]
    ppermute x3, starting transfers between devices: 1.15 us -> 2.91 us  [per_device(): halfway += [lax.ppermute(send, 'gx', swap) for send in outs[1::2]]]
    ppermute x3, waiting for transfers between devices: 6.92 us -> 5.21 us  [the longest x2 4.37 us: total_over(): lax.ppermute(value, axis, [(i, i ^ d) for i in range(n)])]
    squeeze x1 -> x0, local copies, waits for them, and re-layouts: 1.3 us -> none  [per_device(): other = lax.dynamic_index_in_dim(initial_path, 1 - gx, 0, keepdims=False)]
  transfers between devices with their start and end apart: 19 -> 19, of which waited for: 6 -> 8; matrix products, arithmetic and copies ran while one was open for 0% -> 0% of each run, Pallas kernels for 23% -> 23%
where the time goes in v3:
time: 71.6 us; the launch traced here: 71.4 us
  starting transfers between devices  33.1 us (46%)
  Pallas kernels  19.8 us (28%)
  waiting for transfers between devices  16.8 us (23%)
  local copies, waits for them, and re-layouts  1.41 us (2%)
    ppermute x3, starting transfers between devices, per_device(): from_chain = [lax.ppermute(p, ('chain', 'gx'), along_chain) for p in pieces]  12.5 us
    pallas_call x3, Pallas kernels, per_device(): pl.pallas_call(functools.partial(edge_kernel, rows, a, b), out_shape=outs...  8.26 us
    ppermute x3, starting transfers between devices, per_device(): lax.ppermute(low, 'gy', ring('gy', -1))  7.08 us
    ppermute x3, waiting for transfers between devices, per_device(): from_chain = [lax.ppermute(p, ('chain', 'gx'), along_chain) for p in pieces]  6.43 us
    pallas_call x1, Pallas kernels, per_device(): pl.pallas_call(functools.partial(inner_kernel, rows), out_shape=[slab(row...  4.6 us
    ppermute x2, waiting for transfers between devices, total_over(): lax.ppermute(value, axis, [(i, i ^ d) for i in range(n)])  4.37 us
    ppermute x3, waiting for transfers between devices, per_device(): lax.ppermute(low, 'gy', ring('gy', -1))  3.9 us
    ppermute x3, starting transfers between devices, per_device(): from_partner = [lax.ppermute(p, 'gx', swap) for p in pieces]  3.53 us
  transfers between devices with their start and end apart: 19, of which 8 were waited for; matrix products, arithmetic and copies ran while one was open for 0% of the time, Pallas kernels for 23%

profile of v3, /device:TPU:5, one launch (start us, length us, event | category | flops | bytes accessed | tf_op | source)
XLA Modules:
  0.0 71.4 jit_solution(2567147023108993274)
XLA Ops:
  0.0 1.4 %copy-done = f32[2,32,24,256]{3,2,1,0:T(8,128)S(1)} copy-done((f32[2,32,24,256]{3,2,1,0:T(8,128)S(1)}, f32[2,32,24,256]{3,2,1,0:T(8,128)}, u32[]{:S(2)}) %copy-start) | copy-done | bytes 1572888
  1.4 0.1 cut.1
  1.5 0.7 %collective-permute-start = (f32[2,32,24,128]{3,2,1,0:T(8,128)S(1)}, f32[2,32,24,128]{3,2,1,0:T(8,128)S(1)}, u32[]{:S(2)}, u32[]{:S(2)}) collective-permute-start(f32[2,32,24,128]{3,2,1,0:T(8,128)S(1)} %cut.1), channel_id=1, source_target_pairs={{0,4},{4,0},{1,5},{5,1},{2,6},{6,2},{3,7},{7,3},{8,12},{12,8},{9,1... | collective-permute-start | bytes 2359304 | tf_op jit(solution)/shard_map/ppermute | solution.py:345
  2.2 0.7 own.1.own_ref
  2.9 1.3 %collective-permute-done.recv_ref = f32[2,32,24,128]{3,2,1,0:T(8,128)S(1)} collective-permute-done((f32[2,32,24,128]{3,2,1,0:T(8,128)S(1)}, f32[2,32,24,128]{3,2,1,0:T(8,128)S(1)}, u32[]{:S(2)}, u32[]{:S(2)}) %collective-permute-start) | collective-permute-done | bytes 786464 | tf_op jit(solution)/shard_map/ppermute | solution.py:345
  4.1 0.7 first.1
  4.9 1.3 %collective-permute-start.1 = (f32[5,8,8,256]{3,2,1,0:T(8,128)S(1)}, f32[5,8,8,256]{3,2,1,0:T(8,128)S(1)}, u32[]{:S(2)}, u32[]{:S(2)}) collective-permute-start(f32[5,8,8,256]{3,2,1,0:T(8,128)S(1)} %get-tuple-element.54), channel_id=1, source_target_pairs={{0,1},{1,2},{2,3},{3,0},{4,5},{5,6},{6,7},{7,4},{8,9},{9,10},{10,1... | collective-permute-start | bytes 983048 | tf_op jit(solution)/shard_map/ppermute | solution.py:373
  6.2 2.1 %collective-permute-start.2 = (f32[5,8,8,256]{3,2,1,0:T(8,128)S(1)}, f32[5,8,8,256]{3,2,1,0:T(8,128)S(1)}, u32[]{:S(2)}, u32[]{:S(2)}) collective-permute-start(f32[5,8,8,256]{3,2,1,0:T(8,128)S(1)} %get-tuple-element.55), channel_id=1, source_target_pairs={{0,3},{1,0},{2,1},{3,2},{4,7},{5,4},{6,5},{7,6},{8,11},{9,8},{10,9... | collective-permute-start | bytes 983048 | tf_op jit(solution)/shard_map/ppermute | solution.py:374
  8.3 0.0 collective-permute-start.9
  8.3 3.3 %collective-permute-start.10 = (f32[4,8,8,256]{3,2,1,0:T(8,128)S(1)}, f32[4,8,8,256]{3,2,1,0:T(8,128)S(1)}, u32[]{:S(2)}, u32[]{:S(2)}) collective-permute-start(f32[4,8,8,256]{3,2,1,0:T(8,128)S(1)} %get-tuple-element.68), channel_id=1, source_target_pairs={{0,3},{1,0},{2,1},{3,2},{4,7},{5,4},{6,5},{7,6},{8,11},{9,8},{10,9... | collective-permute-start | bytes 786440 | tf_op jit(solution)/shard_map/ppermute | solution.py:374
  11.6 4.6 %inner.1 = (f32[22,8,8,256]{3,2,1,0:T(8,128)S(1)}, f32[20,8,8,256]{3,2,1,0:T(8,128)S(1)}, f32[18,8,8,256]{3,2,1,0:T(8,128)S(1)}, f32[16,8,8,256]{3,2,1,0:T(8,128...) custom-call(f32[24,8,8,256]{3,2,1,0:T(8,128)S(1)} %get-tuple-element, ...), custom_call_target="tpu_custom_call" | custom-call | tf_op jit(solution)/shard_map/inner/pallas_call | solution.py:377
  16.2 4.4 %collective-permute-start.5 = (f32[6,8,8,256]{3,2,1,0:T(8,128)S(1)}, f32[6,8,8,256]{3,2,1,0:T(8,128)S(1)}, u32[]{:S(2)}, u32[]{:S(2)}) collective-permute-start(f32[6,8,8,256]{3,2,1,0:T(8,128)S(1)} %get-tuple-element.53.refs_0_), channel_id=1, source_target_pairs={{4,8},{8,4},{12,16},{16,12},{20,24},{24,20},{5,9},{9,5},{13,17},{1... | collective-permute-start | bytes 1179656 | tf_op jit(solution)/shard_map/ppermute | solution.py:414
  20.6 0.0 collective-permute-done.1.low_ref
  20.6 1.7 %collective-permute-done.2.high_ref = f32[5,8,8,256]{3,2,1,0:T(8,128)S(1)} collective-permute-done((f32[5,8,8,256]{3,2,1,0:T(8,128)S(1)}, f32[5,8,8,256]{3,2,1,0:T(8,128)S(1)}, u32[]{:S(2)}, u32[]{:S(2)}) %collective-permute-start.2) | collective-permute-done | bytes 327712 | tf_op jit(solution)/shard_map/ppermute | solution.py:374
  22.3 3.6 %edge.3 = (f32[10,8,8,256]{3,2,1,0:T(8,128)S(1)}, f32[16,8,8,256]{3,2,1,0:T(8,128)S(1)}, f32[14,8,8,256]{3,2,1,0:T(8,128)S(1)}, f32[14,8,8,256]{3,2,1,0:T(8,128)...) custom-call(f32[5,8,8,256]{3,2,1,0:T(8,128)S(1)} %collective-permute, ...), custom_call_target="tpu_custom_call" | custom-call | tf_op jit(solution)/shard_map/edge/pallas_call | solution.py:395
  25.9 5.5 %collective-permute-start.6 = (f32[10,8,8,256]{3,2,1,0:T(8,128)S(1)}, f32[10,8,8,256]{3,2,1,0:T(8,128)S(1)}, u32[]{:S(2)}, u32[]{:S(2)}) collective-permute-start(f32[10,8,8,256]{3,2,1,0:T(8,128)S(1)} %get-tuple-element.64.refs_1_), channel_id=1, source_target_pairs={{4,8},{8,4},{12,16},{16,12},{20,24},{24,20},{5,9},{9,5},{13,17},{1... | collective-permute-start | bytes 1966088 | tf_op jit(solution)/shard_map/ppermute | solution.py:414
  31.4 0.1 collective-permute-start.4
  31.4 0.0 collective-permute-done.9.low_ref
  31.4 0.3 collective-permute-start.7
  31.8 1.8 %collective-permute-done.10.high_ref = f32[4,8,8,256]{3,2,1,0:T(8,128)S(1)} collective-permute-done((f32[4,8,8,256]{3,2,1,0:T(8,128)S(1)}, f32[4,8,8,256]{3,2,1,0:T(8,128)S(1)}, u32[]{:S(2)}, u32[]{:S(2)}) %collective-permute-start.10) | collective-permute-done | bytes 262176 | tf_op jit(solution)/shard_map/ppermute | solution.py:374
  33.5 1.7 %collective-permute-start.8 = (f32[2,8,8,256]{3,2,1,0:T(8,128)S(1)}, f32[2,8,8,256]{3,2,1,0:T(8,128)S(1)}, u32[]{:S(2)}, u32[]{:S(2)}) collective-permute-start(f32[2,8,8,256]{3,2,1,0:T(8,128)S(1)} %get-tuple-element.66), channel_id=1, source_target_pairs={{0,3},{1,0},{2,1},{3,2},{4,7},{5,4},{6,5},{7,6},{8,11},{9,8},{10,9... | collective-permute-start | bytes 393224 | tf_op jit(solution)/shard_map/ppermute | solution.py:374
  35.2 2.9 %edge.4 = (f32[8,8,8,256]{3,2,1,0:T(8,128)S(1)}, f32[14,8,8,256]{3,2,1,0:T(8,128)S(1)}, f32[12,8,8,256]{3,2,1,0:T(8,128)S(1)}, f32[12,8,8,256]{3,2,1,0:T(8,128)S...) custom-call(f32[4,8,8,256]{3,2,1,0:T(8,128)S(1)} %collective-permute, ...), custom_call_target="tpu_custom_call" | custom-call | tf_op jit(solution)/shard_map/edge/pallas_call | solution.py:395
  38.1 0.0 collective-permute-done.7.low_ref
  38.2 2.6 %collective-permute-start.3 = (f32[6,8,8,256]{3,2,1,0:T(8,128)S(1)}, f32[6,8,8,256]{3,2,1,0:T(8,128)S(1)}, u32[]{:S(2)}, u32[]{:S(2)}) collective-permute-start(f32[6,8,8,256]{3,2,1,0:T(8,128)S(1)} %get-tuple-element.53.refs_0_), channel_id=1, source_target_pairs={{0,4},{4,0},{1,5},{5,1},{2,6},{6,2},{3,7},{7,3},{8,12},{12,8},{9,1... | collective-permute-start | bytes 1179656 | tf_op jit(solution)/shard_map/ppermute | solution.py:413
  40.8 0.4 collective-permute-done.8.high_ref
  41.2 2.7 %collective-permute-start.12 = (f32[8,8,8,256]{3,2,1,0:T(8,128)S(1)}, f32[8,8,8,256]{3,2,1,0:T(8,128)S(1)}, u32[]{:S(2)}, u32[]{:S(2)}) collective-permute-start(f32[8,8,8,256]{3,2,1,0:T(8,128)S(1)} %get-tuple-element.87.refs_2_.refs_0_), channel_id=1, source_target_pairs={{4,8},{8,4},{12,16},{16,12},{20,24},{24,20},{5,9},{9,5},{13,17},{1... | collective-permute-start | bytes 1572872 | tf_op jit(solution)/shard_map/ppermute | solution.py:414
  43.9 0.8 %collective-permute-start.11 = (f32[8,8,8,256]{3,2,1,0:T(8,128)S(1)}, f32[8,8,8,256]{3,2,1,0:T(8,128)S(1)}, u32[]{:S(2)}, u32[]{:S(2)}) collective-permute-start(f32[8,8,8,256]{3,2,1,0:T(8,128)S(1)} %get-tuple-element.87.refs_2_.refs_0_), channel_id=1, source_target_pairs={{0,4},{4,0},{1,5},{5,1},{2,6},{6,2},{3,7},{7,3},{8,12},{12,8},{9,1... | collective-permute-start | bytes 1572872 | tf_op jit(solution)/shard_map/ppermute | solution.py:413
  44.7 1.8 %edge.5.halo_ref = f32[4,8,8,256]{3,2,1,0:T(8,128)S(1)} custom-call(f32[2,8,8,256]{3,2,1,0:T(8,128)S(1)} %collective-permute-done.7.low_ref, f32[2,8,8,256]{3,2,1,0:T(8,128)S(1)} %collective-permute-done.8.high_ref, f32[14,8,8,256]{3,2,1,0:T(8,128)S(1)} %get-tuple-element.78.refs_0_, f32[12,8,8,256]{3,2,1,0:T(8,128)S(1)} %get-tuple-element.79.refs_1_, ...), custom_call_target="tpu_custom_call" | custom-call | tf_op jit(solution)/shard_map/edge/pallas_call | solution.py:395
  46.5 2.0 %chemical.1 = (f32[6,8,8,256]{3,2,1,0:T(8,128)S(1)}, f32[10,8,8,256]{3,2,1,0:T(8,128)S(1)}, f32[8,8,8,256]{3,2,1,0:T(8,128)S(1)}) custom-call(f32[4,8,8,256]{3,2,1,0:T(8,128)S(1)} %edge.5.halo_ref, f32[6,8,8,256]{3,2,1,0:T(8,128)S(1)} %get-tuple-element.53.refs_0_, f32[10,8,8,256]{3,2,1,0:T(8,128)S(1)} %get-tuple-element.64.refs_1_, ...), custom_call_target="tpu_custom_call" | custom-call | tf_op jit(solution)/shard_map/chemical/pallas_call | solution.py:416
  48.6 0.0 collective-permute-done.6.refs_5_
  48.6 0.0 collective-permute-done.4.refs_3_
  48.6 0.7 sums.2
  49.3 0.1 collective-permute-start.17
  49.4 6.4 %collective-permute-done.12.refs_2_ = f32[8,8,8,256]{3,2,1,0:T(8,128)S(1)} collective-permute-done((f32[8,8,8,256]{3,2,1,0:T(8,128)S(1)}, f32[8,8,8,256]{3,2,1,0:T(8,128)S(1)}, u32[]{:S(2)}, u32[]{:S(2)}) %collective-permute-start.12) | collective-permute-done | bytes 524320 | tf_op jit(solution)/shard_map/ppermute | solution.py:414
  55.8 0.0 collective-permute-done.11.refs_1_
  55.8 0.3 sums.3
  56.2 2.7 %collective-permute-start.18 = (f32[8,8,8,256]{3,2,1,0:T(8,128)S(1)}, f32[8,8,8,256]{3,2,1,0:T(8,128)S(1)}, u32[]{:S(2)}, u32[]{:S(2)}) collective-permute-start(f32[8,8,8,256]{3,2,1,0:T(8,128)S(1)} %get-tuple-element.98), channel_id=1, source_target_pairs={{0,4},{4,0},{1,5},{5,1},{2,6},{6,2},{3,7},{7,3},{8,12},{12,8},{9,1... | collective-permute-start | bytes 1572872 | tf_op jit(solution)/shard_map/ppermute | solution.py:443
  58.9 0.1 collective-permute-start.16
  59.0 0.3 collective-permute-start.13
  59.3 2.3 %collective-permute-done.13.b_ref = f32[4,8,128]{2,1,0:T(8,128)S(1)} collective-permute-done((f32[4,8,128]{2,1,0:T(8,128)S(1)}, f32[4,8,128]{2,1,0:T(8,128)S(1)}, u32[]{:S(2)}, u32[]{:S(2)}) %collective-permute-start.13) | collective-permute-done | bytes 16416 | tf_op jit(solution)/shard_map/ppermute | solution.py:316
  61.6 1.4 %collective-permute-start.14 = (f32[4,8,128]{2,1,0:T(8,128)S(1)}, f32[4,8,128]{2,1,0:T(8,128)S(1)}, u32[]{:S(2)}, u32[]{:S(2)}) collective-permute-start(f32[4,8,128]{2,1,0:T(8,128)S(1)} %add.2.a_ref), channel_id=1, source_target_pairs={{0,2},{1,3},{2,0},{3,1},{4,6},{5,7},{6,4},{7,5},{8,10},{9,11},{10,... | collective-permute-start | bytes 49160 | tf_op jit(solution)/shard_map/ppermute | solution.py:316
  63.0 2.1 %collective-permute-done.14.b_ref = f32[4,8,128]{2,1,0:T(8,128)S(1)} collective-permute-done((f32[4,8,128]{2,1,0:T(8,128)S(1)}, f32[4,8,128]{2,1,0:T(8,128)S(1)}, u32[]{:S(2)}, u32[]{:S(2)}) %collective-permute-start.14) | collective-permute-done | bytes 16416 | tf_op jit(solution)/shard_map/ppermute | solution.py:316
  65.1 2.9 %collective-permute-start.15 = (f32[4,8,128]{2,1,0:T(8,128)S(1)}, f32[4,8,128]{2,1,0:T(8,128)S(1)}, u32[]{:S(2)}, u32[]{:S(2)}) collective-permute-start(f32[4,8,128]{2,1,0:T(8,128)S(1)} %add.3.mine_sums), channel_id=1, source_target_pairs={{0,4},{4,0},{1,5},{5,1},{2,6},{6,2},{3,7},{7,3},{8,12},{12,8},{9,1... | collective-permute-start | bytes 49160 | tf_op jit(solution)/shard_map/ppermute | solution.py:445
  68.0 0.8 %collective-permute-done.15.other_sums = f32[4,8,128]{2,1,0:T(8,128)S(1)} collective-permute-done((f32[4,8,128]{2,1,0:T(8,128)S(1)}, f32[4,8,128]{2,1,0:T(8,128)S(1)}, u32[]{:S(2)}, u32[]{:S(2)}) %collective-permute-start.15) | collective-permute-done | bytes 16416 | tf_op jit(solution)/shard_map/ppermute | solution.py:445
  68.8 0.0 collective-permute-done.16.refs_3_
  68.8 0.0 collective-permute-done.18.refs_5_
  68.8 0.0 collective-permute-done.17.refs_4_
  68.8 2.4 %last.1 = f32[2,32,24,256]{3,2,1,0:T(8,128)} custom-call(f32[4,8,128]{2,1,0:T(8,128)S(1)} %add.3.mine_sums, f32[4,8,128]{2,1,0:T(8,128)S(1)} %collective-permute-done.15.other_sums, f32[6,8,8,256]{3,2,1,0:T(8,128)S(1)} %get-tuple-element.93.refs_0_, f32[10,8,8,256]{3,2,1,0:T(8,128)S(1)} %get-tuple-element.94.refs_1_, ...), custom_call_target="tpu_custom_call" | custom-call | tf_op jit(solution)/shard_map/last/pallas_call | solution.py:446
  (5 shorter events, 0.0 us)
Async XLA Ops:
  0.0 1.4 %copy-start = (f32[2,32,24,256]{3,2,1,0:T(8,128)S(1)}, f32[2,32,24,256]{3,2,1,0:T(8,128)}, u32[]{:S(2)}) copy-start(f32[2,32,24,256]{3,2,1,0:T(8,128)} %whole_ref.3) | copy-start | bytes 4718596
  1.5 2.7 %collective-permute-start = (f32[2,32,24,128]{3,2,1,0:T(8,128)S(1)}, f32[2,32,24,128]{3,2,1,0:T(8,128)S(1)}, u32[]{:S(2)}, u32[]{:S(2)}) collective-permute-start(f32[2,32,24,128]{3,2,1,0:T(8,128)S(1)} %cut.1), channel_id=1, source_target_pairs={{0,4},{4,0},{1,5},{5,1},{2,6},{6,2},{3,7},{7,3},{8,12},{12,8},{9,1... | collective-permute-start | bytes 2359304 | tf_op jit(solution)/shard_map/ppermute | solution.py:345
  4.9 15.7 %collective-permute-start.1 = (f32[5,8,8,256]{3,2,1,0:T(8,128)S(1)}, f32[5,8,8,256]{3,2,1,0:T(8,128)S(1)}, u32[]{:S(2)}, u32[]{:S(2)}) collective-permute-start(f32[5,8,8,256]{3,2,1,0:T(8,128)S(1)} %get-tuple-element.54), channel_id=1, source_target_pairs={{0,1},{1,2},{2,3},{3,0},{4,5},{5,6},{6,7},{7,4},{8,9},{9,10},{10,1... | collective-permute-start | bytes 983048 | tf_op jit(solution)/shard_map/ppermute | solution.py:373
  6.2 16.1 %collective-permute-start.2 = (f32[5,8,8,256]{3,2,1,0:T(8,128)S(1)}, f32[5,8,8,256]{3,2,1,0:T(8,128)S(1)}, u32[]{:S(2)}, u32[]{:S(2)}) collective-permute-start(f32[5,8,8,256]{3,2,1,0:T(8,128)S(1)} %get-tuple-element.55), channel_id=1, source_target_pairs={{0,3},{1,0},{2,1},{3,2},{4,7},{5,4},{6,5},{7,6},{8,11},{9,8},{10,9... | collective-permute-start | bytes 983048 | tf_op jit(solution)/shard_map/ppermute | solution.py:374
  8.3 23.1 %collective-permute-start.9 = (f32[4,8,8,256]{3,2,1,0:T(8,128)S(1)}, f32[4,8,8,256]{3,2,1,0:T(8,128)S(1)}, u32[]{:S(2)}, u32[]{:S(2)}) collective-permute-start(f32[4,8,8,256]{3,2,1,0:T(8,128)S(1)} %get-tuple-element.67), channel_id=1, source_target_pairs={{0,1},{1,2},{2,3},{3,0},{4,5},{5,6},{6,7},{7,4},{8,9},{9,10},{10,1... | collective-permute-start | bytes 786440 | tf_op jit(solution)/shard_map/ppermute | solution.py:373
  8.3 25.2 %collective-permute-start.10 = (f32[4,8,8,256]{3,2,1,0:T(8,128)S(1)}, f32[4,8,8,256]{3,2,1,0:T(8,128)S(1)}, u32[]{:S(2)}, u32[]{:S(2)}) collective-permute-start(f32[4,8,8,256]{3,2,1,0:T(8,128)S(1)} %get-tuple-element.68), channel_id=1, source_target_pairs={{0,3},{1,0},{2,1},{3,2},{4,7},{5,4},{6,5},{7,6},{8,11},{9,8},{10,9... | collective-permute-start | bytes 786440 | tf_op jit(solution)/shard_map/ppermute | solution.py:374
  16.2 27.7 %collective-permute-start.5 = (f32[6,8,8,256]{3,2,1,0:T(8,128)S(1)}, f32[6,8,8,256]{3,2,1,0:T(8,128)S(1)}, u32[]{:S(2)}, u32[]{:S(2)}) collective-permute-start(f32[6,8,8,256]{3,2,1,0:T(8,128)S(1)} %get-tuple-element.53.refs_0_), channel_id=1, source_target_pairs={{4,8},{8,4},{12,16},{16,12},{20,24},{24,20},{5,9},{9,5},{13,17},{1... | collective-permute-start | bytes 1179656 | tf_op jit(solution)/shard_map/ppermute | solution.py:414
  25.9 22.7 %collective-permute-start.6 = (f32[10,8,8,256]{3,2,1,0:T(8,128)S(1)}, f32[10,8,8,256]{3,2,1,0:T(8,128)S(1)}, u32[]{:S(2)}, u32[]{:S(2)}) collective-permute-start(f32[10,8,8,256]{3,2,1,0:T(8,128)S(1)} %get-tuple-element.64.refs_1_), channel_id=1, source_target_pairs={{4,8},{8,4},{12,16},{16,12},{20,24},{24,20},{5,9},{9,5},{13,17},{1... | collective-permute-start | bytes 1966088 | tf_op jit(solution)/shard_map/ppermute | solution.py:414
  31.4 17.2 %collective-permute-start.4 = (f32[10,8,8,256]{3,2,1,0:T(8,128)S(1)}, f32[10,8,8,256]{3,2,1,0:T(8,128)S(1)}, u32[]{:S(2)}, u32[]{:S(2)}) collective-permute-start(f32[10,8,8,256]{3,2,1,0:T(8,128)S(1)} %get-tuple-element.64.refs_1_), channel_id=1, source_target_pairs={{0,4},{4,0},{1,5},{5,1},{2,6},{6,2},{3,7},{7,3},{8,12},{12,8},{9,1... | collective-permute-start | bytes 1966088 | tf_op jit(solution)/shard_map/ppermute | solution.py:413
  31.4 6.7 %collective-permute-start.7 = (f32[2,8,8,256]{3,2,1,0:T(8,128)S(1)}, f32[2,8,8,256]{3,2,1,0:T(8,128)S(1)}, u32[]{:S(2)}, u32[]{:S(2)}) collective-permute-start(f32[2,8,8,256]{3,2,1,0:T(8,128)S(1)} %get-tuple-element.65), channel_id=1, source_target_pairs={{0,1},{1,2},{2,3},{3,0},{4,5},{5,6},{6,7},{7,4},{8,9},{9,10},{10,1... | collective-permute-start | bytes 393224 | tf_op jit(solution)/shard_map/ppermute | solution.py:373
  33.5 7.7 %collective-permute-start.8 = (f32[2,8,8,256]{3,2,1,0:T(8,128)S(1)}, f32[2,8,8,256]{3,2,1,0:T(8,128)S(1)}, u32[]{:S(2)}, u32[]{:S(2)}) collective-permute-start(f32[2,8,8,256]{3,2,1,0:T(8,128)S(1)} %get-tuple-element.66), channel_id=1, source_target_pairs={{0,3},{1,0},{2,1},{3,2},{4,7},{5,4},{6,5},{7,6},{8,11},{9,8},{10,9... | collective-permute-start | bytes 393224 | tf_op jit(solution)/shard_map/ppermute | solution.py:374
  38.2 10.4 %collective-permute-start.3 = (f32[6,8,8,256]{3,2,1,0:T(8,128)S(1)}, f32[6,8,8,256]{3,2,1,0:T(8,128)S(1)}, u32[]{:S(2)}, u32[]{:S(2)}) collective-permute-start(f32[6,8,8,256]{3,2,1,0:T(8,128)S(1)} %get-tuple-element.53.refs_0_), channel_id=1, source_target_pairs={{0,4},{4,0},{1,5},{5,1},{2,6},{6,2},{3,7},{7,3},{8,12},{12,8},{9,1... | collective-permute-start | bytes 1179656 | tf_op jit(solution)/shard_map/ppermute | solution.py:413
  41.2 14.6 %collective-permute-start.12 = (f32[8,8,8,256]{3,2,1,0:T(8,128)S(1)}, f32[8,8,8,256]{3,2,1,0:T(8,128)S(1)}, u32[]{:S(2)}, u32[]{:S(2)}) collective-permute-start(f32[8,8,8,256]{3,2,1,0:T(8,128)S(1)} %get-tuple-element.87.refs_2_.refs_0_), channel_id=1, source_target_pairs={{4,8},{8,4},{12,16},{16,12},{20,24},{24,20},{5,9},{9,5},{13,17},{1... | collective-permute-start | bytes 1572872 | tf_op jit(solution)/shard_map/ppermute | solution.py:414
  43.9 11.9 %collective-permute-start.11 = (f32[8,8,8,256]{3,2,1,0:T(8,128)S(1)}, f32[8,8,8,256]{3,2,1,0:T(8,128)S(1)}, u32[]{:S(2)}, u32[]{:S(2)}) collective-permute-start(f32[8,8,8,256]{3,2,1,0:T(8,128)S(1)} %get-tuple-element.87.refs_2_.refs_0_), channel_id=1, source_target_pairs={{0,4},{4,0},{1,5},{5,1},{2,6},{6,2},{3,7},{7,3},{8,12},{12,8},{9,1... | collective-permute-start | bytes 1572872 | tf_op jit(solution)/shard_map/ppermute | solution.py:413
  49.3 19.5 %collective-permute-start.17 = (f32[10,8,8,256]{3,2,1,0:T(8,128)S(1)}, f32[10,8,8,256]{3,2,1,0:T(8,128)S(1)}, u32[]{:S(2)}, u32[]{:S(2)}) collective-permute-start(f32[10,8,8,256]{3,2,1,0:T(8,128)S(1)} %get-tuple-element.97), channel_id=1, source_target_pairs={{0,4},{4,0},{1,5},{5,1},{2,6},{6,2},{3,7},{7,3},{8,12},{12,8},{9,1... | collective-permute-start | bytes 1966088 | tf_op jit(solution)/shard_map/ppermute | solution.py:443
  56.2 12.7 %collective-permute-start.18 = (f32[8,8,8,256]{3,2,1,0:T(8,128)S(1)}, f32[8,8,8,256]{3,2,1,0:T(8,128)S(1)}, u32[]{:S(2)}, u32[]{:S(2)}) collective-permute-start(f32[8,8,8,256]{3,2,1,0:T(8,128)S(1)} %get-tuple-element.98), channel_id=1, source_target_pairs={{0,4},{4,0},{1,5},{5,1},{2,6},{6,2},{3,7},{7,3},{8,12},{12,8},{9,1... | collective-permute-start | bytes 1572872 | tf_op jit(solution)/shard_map/ppermute | solution.py:443
  58.9 9.9 %collective-permute-start.16 = (f32[6,8,8,256]{3,2,1,0:T(8,128)S(1)}, f32[6,8,8,256]{3,2,1,0:T(8,128)S(1)}, u32[]{:S(2)}, u32[]{:S(2)}) collective-permute-start(f32[6,8,8,256]{3,2,1,0:T(8,128)S(1)} %get-tuple-element.96), channel_id=1, source_target_pairs={{0,4},{4,0},{1,5},{5,1},{2,6},{6,2},{3,7},{7,3},{8,12},{12,8},{9,1... | collective-permute-start | bytes 1179656 | tf_op jit(solution)/shard_map/ppermute | solution.py:443
  59.0 2.6 %collective-permute-start.13 = (f32[4,8,128]{2,1,0:T(8,128)S(1)}, f32[4,8,128]{2,1,0:T(8,128)S(1)}, u32[]{:S(2)}, u32[]{:S(2)}) collective-permute-start(f32[4,8,128]{2,1,0:T(8,128)S(1)} %get-tuple-element.92.a_ref), channel_id=1, source_target_pairs={{0,1},{1,0},{2,3},{3,2},{4,5},{5,4},{6,7},{7,6},{8,9},{9,8},{10,11... | collective-permute-start | bytes 49160 | tf_op jit(solution)/shard_map/ppermute | solution.py:316
  61.6 3.5 %collective-permute-start.14 = (f32[4,8,128]{2,1,0:T(8,128)S(1)}, f32[4,8,128]{2,1,0:T(8,128)S(1)}, u32[]{:S(2)}, u32[]{:S(2)}) collective-permute-start(f32[4,8,128]{2,1,0:T(8,128)S(1)} %add.2.a_ref), channel_id=1, source_target_pairs={{0,2},{1,3},{2,0},{3,1},{4,6},{5,7},{6,4},{7,5},{8,10},{9,11},{10,... | collective-permute-start | bytes 49160 | tf_op jit(solution)/shard_map/ppermute | solution.py:316
  65.1 3.7 %collective-permute-start.15 = (f32[4,8,128]{2,1,0:T(8,128)S(1)}, f32[4,8,128]{2,1,0:T(8,128)S(1)}, u32[]{:S(2)}, u32[]{:S(2)}) collective-permute-start(f32[4,8,128]{2,1,0:T(8,128)S(1)} %add.3.mine_sums), channel_id=1, source_target_pairs={{0,4},{4,0},{1,5},{5,1},{2,6},{6,2},{3,7},{7,3},{8,12},{12,8},{9,1... | collective-permute-start | bytes 49160 | tf_op jit(solution)/shard_map/ppermute | solution.py:445

commit v4 on v3

--- a/solution.py
+++ b/solution.py
@@ -21,9 +21,17 @@
 LAPS = 3
 FIELD = LAPS * RELAX
 REACH = FIELD + 2
-CHUNKS = (5, 4, 2)
+LEAD = 2
+CHUNKS = (4, 3, 2, 2)
 
 VMEM = pl.BlockSpec(memory_space=pltpu.VMEM)
+SCALE = 1.0
+
+
+def cost(rows):
+    return pl.CostEstimate(flops=0, bytes_accessed=int(SCALE * 130000 * rows), transcendentals=0)
+
+
 PARAMS = pltpu.CompilerParams(vmem_limit_bytes=8 << 20)
 
 
@@ -138,7 +146,15 @@
         lax.fori_loop(done, rows, plain, 0)
 
 
-def inner_kernel(rows, slab_ref, *outs):
+def send_rows(sends, slab_ref, pieces):
+    for piece, (start, count) in zip(pieces, sends):
+        for i in range(count):
+            piece[i] = slab_ref[start + i]
+
+
+def inner_kernel(rows, sends, slab_ref, *refs):
+    outs = refs[:FIELD]
+    send_rows(sends, slab_ref, refs[FIELD:])
     levels = [(slab_ref, 0)] + [(ref, -m) for m, ref in enumerate(outs, 1)]
     for m in range(1, FIELD + 1):
         count = (rows - 2 * m) // 2
@@ -146,8 +162,12 @@
         rows_of((levels, levels), m, start, stop, (levels[m], levels[m]))
 
 
-def edge_kernel(rows, before, after, low_ref, high_ref, *refs):
+def edge_kernel(rows, before, after, sends, early, slab_ref, low_ref, high_ref, *refs):
     count = after - before
+    n = len(sends)
+    refs = refs[:FIELD] + refs[FIELD + early :]
+    send_rows(sends, slab_ref, refs[FIELD : FIELD + n])
+    refs = refs[:FIELD] + refs[FIELD + n :]
     past, levels = refs[:FIELD], refs[-FIELD:]
     fields = refs[FIELD:-FIELD]
     sides = ([], [])
@@ -302,6 +322,7 @@
         in_specs=[VMEM] * 2,
         out_specs=VMEM,
         compiler_params=PARAMS,
+        cost_estimate=cost(1),
         name="add",
     )(a, b)
 
@@ -340,6 +361,7 @@
         out_specs=VMEM,
         scratch_shapes=[pltpu.SemaphoreType.DMA((tiles,))],
         compiler_params=PARAMS,
+        cost_estimate=cost(4),
         name="cut",
     )(initial_path)
     recv = lax.ppermute(other, "gx", swap)
@@ -350,68 +372,86 @@
         out_specs=VMEM,
         scratch_shapes=[pltpu.VMEM(part, jnp.float32), pltpu.SemaphoreType.DMA((tiles,))],
         compiler_params=PARAMS,
+        cost_estimate=cost(18),
         name="own",
     )(initial_path)
     known = [0]
     for n in CHUNKS:
         known.append(known[-1] + n)
-    sends = []
-    for a, b in zip(known, known[1:]):
-        sends += [(a, b - a), (rows - b, b - a)]
-    first = pl.pallas_call(
-        functools.partial(first_kernel, rows, sends),
-        out_shape=[slab(rows)] + [slab(n) for _, n in sends],
+    sends = [[(a, b - a), (rows - b, b - a)] for a, b in zip(known, known[1:])]
+    made = [[], [], []] + [[] for _ in CHUNKS]
+    for j, some in enumerate(sends):
+        made[max(0, j - LEAD)] += some
+    whole, *near = pl.pallas_call(
+        functools.partial(first_kernel, rows, made[0]),
+        out_shape=[slab(rows)] + [slab(n) for _, n in made[0]],
         in_specs=[VMEM] * 2,
-        out_specs=[VMEM] * (1 + len(sends)),
-        compiler_params=PARAMS,
+        out_specs=[VMEM] * (1 + len(made[0])),
+        compiler_params=PARAMS,
+        cost_estimate=cost(18),
         name="first",
     )(own, recv)
+    along_chain = []
+    for c in range(chains - 1):
+        along_chain += [(2 * c + 1, 2 * c + 2), (2 * c + 2, 2 * c + 1)]
+    from_partner, from_chain = [], []
+
+    def exchange(piece):
+        from_chain.append(lax.ppermute(piece, ("chain", "gx"), along_chain))
+        from_partner.append(lax.ppermute(piece, "gx", swap))
+
+    def halos_of(edges):
+        for low, high in zip(edges[::2], edges[1::2]):
+            halos.append((
+                lax.ppermute(high, "gy", ring("gy", 1)),
+                lax.ppermute(low, "gy", ring("gy", -1)),
+            ))
+
     halos = []
-    for j in range(len(CHUNKS)):
-        low, high = first[1 + 2 * j], first[2 + 2 * j]
-        halos.append((
-            lax.ppermute(high, "gy", ring("gy", 1)),
-            lax.ppermute(low, "gy", ring("gy", -1)),
-        ))
-
+    halos_of(near)
     inner = pl.pallas_call(
-        functools.partial(inner_kernel, rows),
-        out_shape=[slab(rows - 2 * m) for m in range(1, FIELD + 1)],
+        functools.partial(inner_kernel, rows, made[1]),
+        out_shape=[slab(rows - 2 * m) for m in range(1, FIELD + 1)] + [slab(n) for _, n in made[1]],
         in_specs=[VMEM],
-        out_specs=[VMEM] * FIELD,
-        compiler_params=PARAMS,
+        out_specs=[VMEM] * (FIELD + len(made[1])),
+        compiler_params=PARAMS,
+        cost_estimate=cost(126),
         name="inner",
-    )(first[0])
-    levels = [first[0]] + list(inner[:-1])
-    pieces = [inner[-1]]
+    )(whole)
+    levels = [whole] + list(inner[: FIELD - 1])
+    halos_of(inner[FIELD:])
+    pieces = [inner[FIELD - 1]]
+    exchange(pieces[0])
     segments = [[(FIELD, rows - 2 * FIELD, 0)]]
-    for (low, high), a, b in zip(halos, known, known[1:]):
+    for j, (a, b) in enumerate(zip(known, known[1:])):
         beyond = max(0, b - FIELD)
         kept = b - a - beyond
         fields = [slab(2 * n) for n in (kept, beyond) if n]
         buffers = [(2 * (b - a + context(m)), planes, SUB, nz) for m in range(FIELD)]
         last = b == REACH
-        outs = fields if last else fields + [slab(shape[0]) for shape in buffers]
+        ahead = made[j + 2]
+        outs = [slab(n) for _, n in ahead] + fields
+        if not last:
+            outs += [slab(shape[0]) for shape in buffers]
+        early = from_chain[j - 1 : j] if j else []
         done = pl.pallas_call(
-            functools.partial(edge_kernel, rows, a, b),
+            functools.partial(edge_kernel, rows, a, b, ahead, len(early)),
             out_shape=outs,
-            in_specs=[VMEM] * (FIELD + 2),
+            in_specs=[VMEM] * (FIELD + 3 + len(early)),
             out_specs=[VMEM] * len(outs),
             scratch_shapes=[pltpu.VMEM(shape, jnp.float32) for shape in buffers] if last else [],
             compiler_params=PARAMS,
+            cost_estimate=cost(2 * FIELD * (b - a)),
             name="edge",
-        )(low, high, *levels)
+        )(whole, *halos[j], *levels, *early)
+        halos_of(done[: len(ahead)])
+        done = done[len(ahead) :]
         if kept:
             pieces.append(done[0])
+            exchange(done[0])
             segments.append([(FIELD - a - kept, kept, 0), (rows - FIELD + a, kept, kept)])
         levels = list(done[len(fields) :])
-        halo = done[len(fields) - 1]
-
-    along_chain = []
-    for c in range(chains - 1):
-        along_chain += [(2 * c + 1, 2 * c + 2), (2 * c + 2, 2 * c + 1)]
-    from_partner = [lax.ppermute(p, "gx", swap) for p in pieces]
-    from_chain = [lax.ppermute(p, ("chain", "gx"), along_chain) for p in pieces]
+        beyond_rows = done[len(fields) - 1]
 
     chemical = pl.pallas_call(
         functools.partial(chemical_kernel, rows, segments),
@@ -423,8 +463,9 @@
             pltpu.VMEM((rows + 2, planes, SUB, nz), jnp.float32),
         ],
         compiler_params=PARAMS,
+        cost_estimate=cost(2 * rows),
         name="chemical",
-    )(halo, *pieces)
+    )(beyond_rows, *pieces)
     mine, halfway, total = [], [], None
     for some in (slice(0, -1), slice(-1, None)):
         n = len(pieces[some])
@@ -437,6 +478,7 @@
             in_specs=[VMEM] * (4 * n + len(before)),
             out_specs=[VMEM] * (1 + 2 * n),
             compiler_params=PARAMS,
+            cost_estimate=cost(rows // 2),
             name="sums",
         )(*before, *pieces[some], *from_partner[some], *from_chain[some], *chemical[some])
         mine += outs[::2]
@@ -453,6 +495,7 @@
             pltpu.SemaphoreType.DMA((2, tiles)),
         ],
         compiler_params=PARAMS,
+        cost_estimate=cost(2 * rows),
         name="last",
     )(total, other, *mine, *halfway)
 

time: 71.6 us -> 68.3 us (0.954)
  waiting for transfers between devices: 16.8 us -> 10.7 us
  starting transfers between devices: 33.1 us -> 35.2 us
    ppermute x12 -> x16, waiting for transfers between devices: 10.3 us -> 4.48 us  [the longest x4 3.43 us: halos_of(): lax.ppermute(high, 'gy', ring('gy', 1))]
    ppermute x12 -> x16, starting transfers between devices: 24.8 us -> 27.5 us  [the longest x4 15.2 us: exchange(): from_chain.append(lax.ppermute(piece, ('chain', 'gx'), along_chain))]
    pallas_call x5 -> x6, Pallas kernels: 13.6 us -> 14.1 us  [the longest x4 8.78 us: per_device(): pl.pallas_call(functools.partial(edge_kernel, rows, a, b, ahead, len(earl...]
    ppermute x3 -> x4, starting transfers between devices: 2.91 us -> 2.68 us  [per_device(): halfway += [lax.ppermute(send, 'gx', swap) for send in outs[1::2]]]
  transfers between devices with their start and end apart: 19 -> 24, of which waited for: 8 -> 7; matrix products, arithmetic and copies ran while one was open for 0% -> 0% of each run, Pallas kernels for 23% -> 25%
where the time goes in v4:
time: 68.3 us; the launch traced here: 68.1 us
  starting transfers between devices  35.2 us (52%)
  Pallas kernels  20.3 us (30%)
  waiting for transfers between devices  10.7 us (16%)
  local copies, waits for them, and re-layouts  1.41 us (2%)
    ppermute x4, starting transfers between devices, exchange(): from_chain.append(lax.ppermute(piece, ('chain', 'gx'), along_chain))  15.2 us
    ppermute x4, starting transfers between devices, halos_of(): lax.ppermute(low, 'gy', ring('gy', -1))  9.57 us
    pallas_call x4, Pallas kernels, per_device(): pl.pallas_call(functools.partial(edge_kernel, rows, a, b, ahead, len(earl...  8.78 us
    pallas_call x1, Pallas kernels, per_device(): pl.pallas_call(functools.partial(inner_kernel, rows, made[1]), out_shape=...  4.61 us
    ppermute x2, waiting for transfers between devices, total_over(): lax.ppermute(value, axis, [(i, i ^ d) for i in range(n)])  4.16 us
    ppermute x4, waiting for transfers between devices, halos_of(): lax.ppermute(high, 'gy', ring('gy', 1))  3.43 us
    ppermute x4, starting transfers between devices, per_device(): halfway += [lax.ppermute(send, 'gx', swap) for send in outs[1::2]]  2.68 us
    pallas_call x1, Pallas kernels, per_device(): pl.pallas_call(functools.partial(last_kernel, cells, segments), out_shape...  2.42 us
  transfers between devices with their start and end apart: 24, of which 7 were waited for; matrix products, arithmetic and copies ran while one was open for 0% of the time, Pallas kernels for 25%

profile of v4, /device:TPU:5, one launch (start us, length us, event | category | flops | bytes accessed | tf_op | source)
XLA Modules:
  0.0 68.1 jit_solution(12877218381197743089)
XLA Ops:
  0.0 1.4 %copy-done = f32[2,32,24,256]{3,2,1,0:T(8,128)S(1)} copy-done((f32[2,32,24,256]{3,2,1,0:T(8,128)S(1)}, f32[2,32,24,256]{3,2,1,0:T(8,128)}, u32[]{:S(2)}) %copy-start) | copy-done | bytes 1572888
  1.4 0.1 cut.1
  1.5 0.7 %collective-permute-start = (f32[2,32,24,128]{3,2,1,0:T(8,128)S(1)}, f32[2,32,24,128]{3,2,1,0:T(8,128)S(1)}, u32[]{:S(2)}, u32[]{:S(2)}) collective-permute-start(f32[2,32,24,128]{3,2,1,0:T(8,128)S(1)} %cut.1), channel_id=1, source_target_pairs={{0,4},{4,0},{1,5},{5,1},{2,6},{6,2},{3,7},{7,3},{8,12},{12,8},{9,1... | collective-permute-start | bytes 2359304 | tf_op jit(solution)/shard_map/ppermute | solution.py:367
  2.2 0.7 own.1.own_ref
  2.9 1.3 %collective-permute-done.recv_ref = f32[2,32,24,128]{3,2,1,0:T(8,128)S(1)} collective-permute-done((f32[2,32,24,128]{3,2,1,0:T(8,128)S(1)}, f32[2,32,24,128]{3,2,1,0:T(8,128)S(1)}, u32[]{:S(2)}, u32[]{:S(2)}) %collective-permute-start) | collective-permute-done | bytes 786464 | tf_op jit(solution)/shard_map/ppermute | solution.py:367
  4.1 0.7 %first.1 = (f32[24,8,8,256]{3,2,1,0:T(8,128)S(1)}, f32[4,8,8,256]{3,2,1,0:T(8,128)S(1)}, f32[4,8,8,256]{3,2,1,0:T(8,128)S(1)}, f32[3,8,8,256]{3,2,1,0:T(8,128)S(...) custom-call(f32[24,8,8,256]{3,2,1,0:T(8,128)S(1)} %own.1.own_ref, ...), custom_call_target="tpu_custom_call" | custom-call | bytes 2340000 | tf_op jit(solution)/shard_map/first/pallas_call | solution.py:385
  4.9 1.3 %collective-permute-start.1 = (f32[4,8,8,256]{3,2,1,0:T(8,128)S(1)}, f32[4,8,8,256]{3,2,1,0:T(8,128)S(1)}, u32[]{:S(2)}, u32[]{:S(2)}) collective-permute-start(f32[4,8,8,256]{3,2,1,0:T(8,128)S(1)} %get-tuple-element.69), channel_id=1, source_target_pairs={{0,1},{1,2},{2,3},{3,0},{4,5},{5,6},{6,7},{7,4},{8,9},{9,10},{10,1... | collective-permute-start | bytes 786440 | tf_op jit(solution)/shard_map/ppermute | solution.py:406
  6.2 2.1 %collective-permute-start.2 = (f32[4,8,8,256]{3,2,1,0:T(8,128)S(1)}, f32[4,8,8,256]{3,2,1,0:T(8,128)S(1)}, u32[]{:S(2)}, u32[]{:S(2)}) collective-permute-start(f32[4,8,8,256]{3,2,1,0:T(8,128)S(1)} %get-tuple-element.70), channel_id=1, source_target_pairs={{0,3},{1,0},{2,1},{3,2},{4,7},{5,4},{6,5},{7,6},{8,11},{9,8},{10,9... | collective-permute-start | bytes 786440 | tf_op jit(solution)/shard_map/ppermute | solution.py:407
  8.3 4.6 %inner.1 = (f32[22,8,8,256]{3,2,1,0:T(8,128)S(1)}, f32[20,8,8,256]{3,2,1,0:T(8,128)S(1)}, f32[18,8,8,256]{3,2,1,0:T(8,128)S(1)}, f32[16,8,8,256]{3,2,1,0:T(8,128...) custom-call(f32[24,8,8,256]{3,2,1,0:T(8,128)S(1)} %get-tuple-element, ...), custom_call_target="tpu_custom_call" | custom-call | bytes 16380000 | tf_op jit(solution)/shard_map/inner/pallas_call | solution.py:412
  12.9 3.8 %collective-permute-start.5 = (f32[6,8,8,256]{3,2,1,0:T(8,128)S(1)}, f32[6,8,8,256]{3,2,1,0:T(8,128)S(1)}, u32[]{:S(2)}, u32[]{:S(2)}) collective-permute-start(f32[6,8,8,256]{3,2,1,0:T(8,128)S(1)} %get-tuple-element.68.refs_0_), channel_id=1, source_target_pairs={{4,8},{8,4},{12,16},{16,12},{20,24},{24,20},{5,9},{9,5},{13,17},{1... | collective-permute-start | bytes 1179656 | tf_op jit(solution)/shard_map/ppermute | solution.py:400
  16.7 0.1 collective-permute-start.3
  16.8 3.3 %collective-permute-start.4 = (f32[3,8,8,256]{3,2,1,0:T(8,128)S(1)}, f32[3,8,8,256]{3,2,1,0:T(8,128)S(1)}, u32[]{:S(2)}, u32[]{:S(2)}) collective-permute-start(f32[3,8,8,256]{3,2,1,0:T(8,128)S(1)} %get-tuple-element.81), channel_id=1, source_target_pairs={{0,3},{1,0},{2,1},{3,2},{4,7},{5,4},{6,5},{7,6},{8,11},{9,8},{10,9... | collective-permute-start | bytes 589832 | tf_op jit(solution)/shard_map/ppermute | solution.py:407
  20.1 0.0 collective-permute-done.1.low_ref
  20.1 0.0 collective-permute-done.2.high_ref
  20.1 2.9 %edge.4 = (f32[8,8,8,256]{3,2,1,0:T(8,128)S(1)}, f32[14,8,8,256]{3,2,1,0:T(8,128)S(1)}, f32[12,8,8,256]{3,2,1,0:T(8,128)S(1)}, f32[12,8,8,256]{3,2,1,0:T(8,128)S...) custom-call(f32[24,8,8,256]{3,2,1,0:T(8,128)S(1)} %get-tuple-element, ...), custom_call_target="tpu_custom_call" | custom-call | bytes 9360000 | tf_op jit(solution)/shard_map/edge/pallas_call | solution.py:437
  23.0 4.9 %collective-permute-start.9 = (f32[8,8,8,256]{3,2,1,0:T(8,128)S(1)}, f32[8,8,8,256]{3,2,1,0:T(8,128)S(1)}, u32[]{:S(2)}, u32[]{:S(2)}) collective-permute-start(f32[8,8,8,256]{3,2,1,0:T(8,128)S(1)} %get-tuple-element.79.refs_1_), channel_id=1, source_target_pairs={{4,8},{8,4},{12,16},{16,12},{20,24},{24,20},{5,9},{9,5},{13,17},{1... | collective-permute-start | bytes 1572872 | tf_op jit(solution)/shard_map/ppermute | solution.py:400
  27.9 0.3 collective-permute-start.13
  28.2 3.0 %collective-permute-start.14 = (f32[2,8,8,256]{3,2,1,0:T(8,128)S(1)}, f32[2,8,8,256]{3,2,1,0:T(8,128)S(1)}, u32[]{:S(2)}, u32[]{:S(2)}) collective-permute-start(f32[2,8,8,256]{3,2,1,0:T(8,128)S(1)} %get-tuple-element.95), channel_id=1, source_target_pairs={{0,3},{1,0},{2,1},{3,2},{4,7},{5,4},{6,5},{7,6},{8,11},{9,8},{10,9... | collective-permute-start | bytes 393224 | tf_op jit(solution)/shard_map/ppermute | solution.py:407
  31.2 0.2 collective-permute-start.7
  31.4 2.2 %edge.5 = (f32[6,8,8,256]{3,2,1,0:T(8,128)S(1)}, f32[12,8,8,256]{3,2,1,0:T(8,128)S(1)}, f32[10,8,8,256]{3,2,1,0:T(8,128)S(1)}, f32[10,8,8,256]{3,2,1,0:T(8,128)S...) custom-call(f32[24,8,8,256]{3,2,1,0:T(8,128)S(1)} %get-tuple-element, ...), custom_call_target="tpu_custom_call" | custom-call | bytes 7020000 | tf_op jit(solution)/shard_map/edge/pallas_call | solution.py:437
  33.6 1.4 %collective-permute-done.13.low_ref = f32[2,8,8,256]{3,2,1,0:T(8,128)S(1)} collective-permute-done((f32[2,8,8,256]{3,2,1,0:T(8,128)S(1)}, f32[2,8,8,256]{3,2,1,0:T(8,128)S(1)}, u32[]{:S(2)}, u32[]{:S(2)}) %collective-permute-start.13) | collective-permute-done | bytes 131104 | tf_op jit(solution)/shard_map/ppermute | solution.py:406
  35.0 2.4 %collective-permute-start.10 = (f32[6,8,8,256]{3,2,1,0:T(8,128)S(1)}, f32[6,8,8,256]{3,2,1,0:T(8,128)S(1)}, u32[]{:S(2)}, u32[]{:S(2)}) collective-permute-start(f32[6,8,8,256]{3,2,1,0:T(8,128)S(1)} %get-tuple-element.91.refs_2_), channel_id=1, source_target_pairs={{4,8},{8,4},{12,16},{16,12},{20,24},{24,20},{5,9},{9,5},{13,17},{1... | collective-permute-start | bytes 1179656 | tf_op jit(solution)/shard_map/ppermute | solution.py:400
  37.4 0.1 collective-permute-start.6
  37.6 2.1 %collective-permute-done.11.low_ref = f32[2,8,8,256]{3,2,1,0:T(8,128)S(1)} collective-permute-done((f32[2,8,8,256]{3,2,1,0:T(8,128)S(1)}, f32[2,8,8,256]{3,2,1,0:T(8,128)S(1)}, u32[]{:S(2)}, u32[]{:S(2)}) %collective-permute-start.11) | collective-permute-done | bytes 131104 | tf_op jit(solution)/shard_map/ppermute | solution.py:406
  39.6 0.0 collective-permute-start.8
  39.6 0.0 collective-permute-done.9.refs_9_.refs_7_
  39.6 1.2 %collective-permute-start.12 = (f32[2,8,8,256]{3,2,1,0:T(8,128)S(1)}, f32[2,8,8,256]{3,2,1,0:T(8,128)S(1)}, u32[]{:S(2)}, u32[]{:S(2)}) collective-permute-start(f32[2,8,8,256]{3,2,1,0:T(8,128)S(1)} %get-tuple-element.93), channel_id=1, source_target_pairs={{0,3},{1,0},{2,1},{3,2},{4,7},{5,4},{6,5},{7,6},{8,11},{9,8},{10,9... | collective-permute-start | bytes 393224 | tf_op jit(solution)/shard_map/ppermute | solution.py:407
  40.9 1.8 %edge.6 = (f32[4,8,8,256]{3,2,1,0:T(8,128)S(1)}, f32[10,8,8,256]{3,2,1,0:T(8,128)S(1)}, f32[8,8,8,256]{3,2,1,0:T(8,128)S(1)}, f32[8,8,8,256]{3,2,1,0:T(8,128)S(1...) custom-call(f32[24,8,8,256]{3,2,1,0:T(8,128)S(1)} %get-tuple-element, ...), custom_call_target="tpu_custom_call" | custom-call | bytes 4680000 | tf_op jit(solution)/shard_map/edge/pallas_call | solution.py:437
  42.7 1.0 %collective-permute-done.12.high_ref = f32[2,8,8,256]{3,2,1,0:T(8,128)S(1)} collective-permute-done((f32[2,8,8,256]{3,2,1,0:T(8,128)S(1)}, f32[2,8,8,256]{3,2,1,0:T(8,128)S(1)}, u32[]{:S(2)}, u32[]{:S(2)}) %collective-permute-start.12) | collective-permute-done | bytes 131104 | tf_op jit(solution)/shard_map/ppermute | solution.py:407
  43.8 4.0 %collective-permute-start.16 = (f32[4,8,8,256]{3,2,1,0:T(8,128)S(1)}, f32[4,8,8,256]{3,2,1,0:T(8,128)S(1)}, u32[]{:S(2)}, u32[]{:S(2)}) collective-permute-start(f32[4,8,8,256]{3,2,1,0:T(8,128)S(1)} %get-tuple-element.114.refs_3_.refs_0_), channel_id=1, source_target_pairs={{4,8},{8,4},{12,16},{16,12},{20,24},{24,20},{5,9},{9,5},{13,17},{1... | collective-permute-start | bytes 786440 | tf_op jit(solution)/shard_map/ppermute | solution.py:400
  47.8 0.0 collective-permute-done.10.refs_9_.refs_8_
  47.8 0.7 %collective-permute-start.15 = (f32[4,8,8,256]{3,2,1,0:T(8,128)S(1)}, f32[4,8,8,256]{3,2,1,0:T(8,128)S(1)}, u32[]{:S(2)}, u32[]{:S(2)}) collective-permute-start(f32[4,8,8,256]{3,2,1,0:T(8,128)S(1)} %get-tuple-element.114.refs_3_.refs_0_), channel_id=1, source_target_pairs={{0,4},{4,0},{1,5},{5,1},{2,6},{6,2},{3,7},{7,3},{8,12},{12,8},{9,1... | collective-permute-start | bytes 786440 | tf_op jit(solution)/shard_map/ppermute | solution.py:401
  48.5 1.8 %edge.7.halo_ref = f32[4,8,8,256]{3,2,1,0:T(8,128)S(1)} custom-call(f32[24,8,8,256]{3,2,1,0:T(8,128)S(1)} %get-tuple-element.67.slab_ref.refs_0_, f32[2,8,8,256]{3,2,1,0:T(8,128)S(1)} %collective-permute-done.11.low_ref, f32[2,8,8,256]{3,2,1,0:T(8,128)S(1)} %collective-permute-done.12.high_ref, f32[10,8,8,256]{3,2,1,0:T(8,128)S(1)} %get-tuple-element.105.refs_0_, ...), custom_call_target="tpu_custom_call" | custom-call | bytes 4680000 | tf_op jit(solution)/shard_map/edge/pallas_call | solution.py:437
  50.3 2.0 %chemical.1 = (f32[6,8,8,256]{3,2,1,0:T(8,128)S(1)}, f32[8,8,8,256]{3,2,1,0:T(8,128)S(1)}, f32[6,8,8,256]{3,2,1,0:T(8,128)S(1)}, f32[4,8,8,256]{3,2,1,0:T(8,128)S(1)}) custom-call(f32[4,8,8,256]{3,2,1,0:T(8,128)S(1)} %edge.7.halo_ref, f32[6,8,8,256]{3,2,1,0:T(8,128)S(1)} %get-tuple-element.68.refs_0_, f32[8,8,8,256]{3,2,1,0:T(8,128)S(1)} %get-tuple-element.79.refs_1_, ...), custom_call_target="tpu_custom_call" | custom-call | bytes 6240000 | tf_op jit(solution)/shard_map/chemical/pallas_call | solution.py:456
  52.4 0.0 collective-permute-done.6.refs_3_
  52.4 0.0 collective-permute-done.8.refs_5_
  52.4 0.9 %sums.2 = (f32[4,8,128]{2,1,0:T(8,128)S(1)}, f32[6,8,8,256]{3,2,1,0:T(8,128)S(1)}, f32[6,8,8,256]{3,2,1,0:T(8,128)S(1)}, f32[8,8,8,256]{3,2,1,0:T(8,128)S(1)}, f...) custom-call(f32[6,8,8,256]{3,2,1,0:T(8,128)S(1)} %get-tuple-element.68.refs_0_, ...), custom_call_target="tpu_custom_call" | custom-call | bytes 1560000 | tf_op jit(solution)/shard_map/sums/pallas_call | solution.py:474
  53.3 0.1 collective-permute-start.21
  53.4 0.5 collective-permute-start.20
  53.9 0.1 collective-permute-start.22
  53.9 0.2 sums.3
  54.1 2.0 %collective-permute-start.23 = (f32[4,8,8,256]{3,2,1,0:T(8,128)S(1)}, f32[4,8,8,256]{3,2,1,0:T(8,128)S(1)}, u32[]{:S(2)}, u32[]{:S(2)}) collective-permute-start(f32[4,8,8,256]{3,2,1,0:T(8,128)S(1)} %get-tuple-element.128), channel_id=1, source_target_pairs={{0,4},{4,0},{1,5},{5,1},{2,6},{6,2},{3,7},{7,3},{8,12},{12,8},{9,1... | collective-permute-start | bytes 786440 | tf_op jit(solution)/shard_map/ppermute | solution.py:485
  56.2 2.6 %collective-permute-done.17.b_ref = f32[4,8,128]{2,1,0:T(8,128)S(1)} collective-permute-done((f32[4,8,128]{2,1,0:T(8,128)S(1)}, f32[4,8,128]{2,1,0:T(8,128)S(1)}, u32[]{:S(2)}, u32[]{:S(2)}) %collective-permute-start.17) | collective-permute-done | bytes 16416 | tf_op jit(solution)/shard_map/ppermute | solution.py:337
  58.8 1.9 %collective-permute-start.18 = (f32[4,8,128]{2,1,0:T(8,128)S(1)}, f32[4,8,128]{2,1,0:T(8,128)S(1)}, u32[]{:S(2)}, u32[]{:S(2)}) collective-permute-start(f32[4,8,128]{2,1,0:T(8,128)S(1)} %add.2.a_ref), channel_id=1, source_target_pairs={{0,2},{1,3},{2,0},{3,1},{4,6},{5,7},{6,4},{7,5},{8,10},{9,11},{10,... | collective-permute-start | bytes 49160 | tf_op jit(solution)/shard_map/ppermute | solution.py:337
  60.7 1.6 %collective-permute-done.18.b_ref = f32[4,8,128]{2,1,0:T(8,128)S(1)} collective-permute-done((f32[4,8,128]{2,1,0:T(8,128)S(1)}, f32[4,8,128]{2,1,0:T(8,128)S(1)}, u32[]{:S(2)}, u32[]{:S(2)}) %collective-permute-start.18) | collective-permute-done | bytes 16416 | tf_op jit(solution)/shard_map/ppermute | solution.py:337
  62.3 2.4 %collective-permute-start.19 = (f32[4,8,128]{2,1,0:T(8,128)S(1)}, f32[4,8,128]{2,1,0:T(8,128)S(1)}, u32[]{:S(2)}, u32[]{:S(2)}) collective-permute-start(f32[4,8,128]{2,1,0:T(8,128)S(1)} %add.3.mine_sums), channel_id=1, source_target_pairs={{0,4},{4,0},{1,5},{5,1},{2,6},{6,2},{3,7},{7,3},{8,12},{12,8},{9,1... | collective-permute-start | bytes 49160 | tf_op jit(solution)/shard_map/ppermute | solution.py:487
  64.6 0.8 %collective-permute-done.19.other_sums = f32[4,8,128]{2,1,0:T(8,128)S(1)} collective-permute-done((f32[4,8,128]{2,1,0:T(8,128)S(1)}, f32[4,8,128]{2,1,0:T(8,128)S(1)}, u32[]{:S(2)}, u32[]{:S(2)}) %collective-permute-start.19) | collective-permute-done | bytes 16416 | tf_op jit(solution)/shard_map/ppermute | solution.py:487
  65.5 2.4 %last.1 = f32[2,32,24,256]{3,2,1,0:T(8,128)} custom-call(f32[4,8,128]{2,1,0:T(8,128)S(1)} %add.3.mine_sums, f32[4,8,128]{2,1,0:T(8,128)S(1)} %collective-permute-done.19.other_sums, f32[6,8,8,256]{3,2,1,0:T(8,128)S(1)} %get-tuple-element.121.refs_0_, f32[8,8,8,256]{3,2,1,0:T(8,128)S(1)} %get-tuple-element.122.refs_1_, ...), custom_call_target="tpu_custom_call" | custom-call | bytes 6240000 | tf_op jit(solution)/shard_map/last/pallas_call | solution.py:488
  (16 shorter events, 0.0 us)
Async XLA Ops:
  0.0 1.4 %copy-start = (f32[2,32,24,256]{3,2,1,0:T(8,128)S(1)}, f32[2,32,24,256]{3,2,1,0:T(8,128)}, u32[]{:S(2)}) copy-start(f32[2,32,24,256]{3,2,1,0:T(8,128)} %whole_ref.3) | copy-start | bytes 4718596
  1.5 2.7 %collective-permute-start = (f32[2,32,24,128]{3,2,1,0:T(8,128)S(1)}, f32[2,32,24,128]{3,2,1,0:T(8,128)S(1)}, u32[]{:S(2)}, u32[]{:S(2)}) collective-permute-start(f32[2,32,24,128]{3,2,1,0:T(8,128)S(1)} %cut.1), channel_id=1, source_target_pairs={{0,4},{4,0},{1,5},{5,1},{2,6},{6,2},{3,7},{7,3},{8,12},{12,8},{9,1... | collective-permute-start | bytes 2359304 | tf_op jit(solution)/shard_map/ppermute | solution.py:367
  4.9 15.2 %collective-permute-start.1 = (f32[4,8,8,256]{3,2,1,0:T(8,128)S(1)}, f32[4,8,8,256]{3,2,1,0:T(8,128)S(1)}, u32[]{:S(2)}, u32[]{:S(2)}) collective-permute-start(f32[4,8,8,256]{3,2,1,0:T(8,128)S(1)} %get-tuple-element.69), channel_id=1, source_target_pairs={{0,1},{1,2},{2,3},{3,0},{4,5},{5,6},{6,7},{7,4},{8,9},{9,10},{10,1... | collective-permute-start | bytes 786440 | tf_op jit(solution)/shard_map/ppermute | solution.py:406
  6.2 13.9 %collective-permute-start.2 = (f32[4,8,8,256]{3,2,1,0:T(8,128)S(1)}, f32[4,8,8,256]{3,2,1,0:T(8,128)S(1)}, u32[]{:S(2)}, u32[]{:S(2)}) collective-permute-start(f32[4,8,8,256]{3,2,1,0:T(8,128)S(1)} %get-tuple-element.70), channel_id=1, source_target_pairs={{0,3},{1,0},{2,1},{3,2},{4,7},{5,4},{6,5},{7,6},{8,11},{9,8},{10,9... | collective-permute-start | bytes 786440 | tf_op jit(solution)/shard_map/ppermute | solution.py:407
  12.9 18.3 %collective-permute-start.5 = (f32[6,8,8,256]{3,2,1,0:T(8,128)S(1)}, f32[6,8,8,256]{3,2,1,0:T(8,128)S(1)}, u32[]{:S(2)}, u32[]{:S(2)}) collective-permute-start(f32[6,8,8,256]{3,2,1,0:T(8,128)S(1)} %get-tuple-element.68.refs_0_), channel_id=1, source_target_pairs={{4,8},{8,4},{12,16},{16,12},{20,24},{24,20},{5,9},{9,5},{13,17},{1... | collective-permute-start | bytes 1179656 | tf_op jit(solution)/shard_map/ppermute | solution.py:400
  16.7 11.5 %collective-permute-start.3 = (f32[3,8,8,256]{3,2,1,0:T(8,128)S(1)}, f32[3,8,8,256]{3,2,1,0:T(8,128)S(1)}, u32[]{:S(2)}, u32[]{:S(2)}) collective-permute-start(f32[3,8,8,256]{3,2,1,0:T(8,128)S(1)} %get-tuple-element.80), channel_id=1, source_target_pairs={{0,1},{1,2},{2,3},{3,0},{4,5},{5,6},{6,7},{7,4},{8,9},{9,10},{10,1... | collective-permute-start | bytes 589832 | tf_op jit(solution)/shard_map/ppermute | solution.py:406
  16.8 14.4 %collective-permute-start.4 = (f32[3,8,8,256]{3,2,1,0:T(8,128)S(1)}, f32[3,8,8,256]{3,2,1,0:T(8,128)S(1)}, u32[]{:S(2)}, u32[]{:S(2)}) collective-permute-start(f32[3,8,8,256]{3,2,1,0:T(8,128)S(1)} %get-tuple-element.81), channel_id=1, source_target_pairs={{0,3},{1,0},{2,1},{3,2},{4,7},{5,4},{6,5},{7,6},{8,11},{9,8},{10,9... | collective-permute-start | bytes 589832 | tf_op jit(solution)/shard_map/ppermute | solution.py:407
  23.0 16.7 %collective-permute-start.9 = (f32[8,8,8,256]{3,2,1,0:T(8,128)S(1)}, f32[8,8,8,256]{3,2,1,0:T(8,128)S(1)}, u32[]{:S(2)}, u32[]{:S(2)}) collective-permute-start(f32[8,8,8,256]{3,2,1,0:T(8,128)S(1)} %get-tuple-element.79.refs_1_), channel_id=1, source_target_pairs={{4,8},{8,4},{12,16},{16,12},{20,24},{24,20},{5,9},{9,5},{13,17},{1... | collective-permute-start | bytes 1572872 | tf_op jit(solution)/shard_map/ppermute | solution.py:400
  27.9 7.1 %collective-permute-start.13 = (f32[2,8,8,256]{3,2,1,0:T(8,128)S(1)}, f32[2,8,8,256]{3,2,1,0:T(8,128)S(1)}, u32[]{:S(2)}, u32[]{:S(2)}) collective-permute-start(f32[2,8,8,256]{3,2,1,0:T(8,128)S(1)} %get-tuple-element.94), channel_id=1, source_target_pairs={{0,1},{1,2},{2,3},{3,0},{4,5},{5,6},{6,7},{7,4},{8,9},{9,10},{10,1... | collective-permute-start | bytes 393224 | tf_op jit(solution)/shard_map/ppermute | solution.py:406
  28.2 9.2 %collective-permute-start.14 = (f32[2,8,8,256]{3,2,1,0:T(8,128)S(1)}, f32[2,8,8,256]{3,2,1,0:T(8,128)S(1)}, u32[]{:S(2)}, u32[]{:S(2)}) collective-permute-start(f32[2,8,8,256]{3,2,1,0:T(8,128)S(1)} %get-tuple-element.95), channel_id=1, source_target_pairs={{0,3},{1,0},{2,1},{3,2},{4,7},{5,4},{6,5},{7,6},{8,11},{9,8},{10,9... | collective-permute-start | bytes 393224 | tf_op jit(solution)/shard_map/ppermute | solution.py:407
  31.2 8.4 %collective-permute-start.11 = (f32[2,8,8,256]{3,2,1,0:T(8,128)S(1)}, f32[2,8,8,256]{3,2,1,0:T(8,128)S(1)}, u32[]{:S(2)}, u32[]{:S(2)}) collective-permute-start(f32[2,8,8,256]{3,2,1,0:T(8,128)S(1)} %get-tuple-element.92), channel_id=1, source_target_pairs={{0,1},{1,2},{2,3},{3,0},{4,5},{5,6},{6,7},{7,4},{8,9},{9,10},{10,1... | collective-permute-start | bytes 393224 | tf_op jit(solution)/shard_map/ppermute | solution.py:406
  31.2 21.2 %collective-permute-start.7 = (f32[8,8,8,256]{3,2,1,0:T(8,128)S(1)}, f32[8,8,8,256]{3,2,1,0:T(8,128)S(1)}, u32[]{:S(2)}, u32[]{:S(2)}) collective-permute-start(f32[8,8,8,256]{3,2,1,0:T(8,128)S(1)} %get-tuple-element.79.refs_1_), channel_id=1, source_target_pairs={{0,4},{4,0},{1,5},{5,1},{2,6},{6,2},{3,7},{7,3},{8,12},{12,8},{9,1... | collective-permute-start | bytes 1572872 | tf_op jit(solution)/shard_map/ppermute | solution.py:401
  35.0 12.8 %collective-permute-start.10 = (f32[6,8,8,256]{3,2,1,0:T(8,128)S(1)}, f32[6,8,8,256]{3,2,1,0:T(8,128)S(1)}, u32[]{:S(2)}, u32[]{:S(2)}) collective-permute-start(f32[6,8,8,256]{3,2,1,0:T(8,128)S(1)} %get-tuple-element.91.refs_2_), channel_id=1, source_target_pairs={{4,8},{8,4},{12,16},{16,12},{20,24},{24,20},{5,9},{9,5},{13,17},{1... | collective-permute-start | bytes 1179656 | tf_op jit(solution)/shard_map/ppermute | solution.py:400
  37.4 14.9 %collective-permute-start.6 = (f32[6,8,8,256]{3,2,1,0:T(8,128)S(1)}, f32[6,8,8,256]{3,2,1,0:T(8,128)S(1)}, u32[]{:S(2)}, u32[]{:S(2)}) collective-permute-start(f32[6,8,8,256]{3,2,1,0:T(8,128)S(1)} %get-tuple-element.68.refs_0_), channel_id=1, source_target_pairs={{0,4},{4,0},{1,5},{5,1},{2,6},{6,2},{3,7},{7,3},{8,12},{12,8},{9,1... | collective-permute-start | bytes 1179656 | tf_op jit(solution)/shard_map/ppermute | solution.py:401
  39.6 12.8 %collective-permute-start.8 = (f32[6,8,8,256]{3,2,1,0:T(8,128)S(1)}, f32[6,8,8,256]{3,2,1,0:T(8,128)S(1)}, u32[]{:S(2)}, u32[]{:S(2)}) collective-permute-start(f32[6,8,8,256]{3,2,1,0:T(8,128)S(1)} %get-tuple-element.91.refs_2_), channel_id=1, source_target_pairs={{0,4},{4,0},{1,5},{5,1},{2,6},{6,2},{3,7},{7,3},{8,12},{12,8},{9,1... | collective-permute-start | bytes 1179656 | tf_op jit(solution)/shard_map/ppermute | solution.py:401
  39.6 4.1 %collective-permute-start.12 = (f32[2,8,8,256]{3,2,1,0:T(8,128)S(1)}, f32[2,8,8,256]{3,2,1,0:T(8,128)S(1)}, u32[]{:S(2)}, u32[]{:S(2)}) collective-permute-start(f32[2,8,8,256]{3,2,1,0:T(8,128)S(1)} %get-tuple-element.93), channel_id=1, source_target_pairs={{0,3},{1,0},{2,1},{3,2},{4,7},{5,4},{6,5},{7,6},{8,11},{9,8},{10,9... | collective-permute-start | bytes 393224 | tf_op jit(solution)/shard_map/ppermute | solution.py:407
  43.8 10.2 %collective-permute-start.16 = (f32[4,8,8,256]{3,2,1,0:T(8,128)S(1)}, f32[4,8,8,256]{3,2,1,0:T(8,128)S(1)}, u32[]{:S(2)}, u32[]{:S(2)}) collective-permute-start(f32[4,8,8,256]{3,2,1,0:T(8,128)S(1)} %get-tuple-element.114.refs_3_.refs_0_), channel_id=1, source_target_pairs={{4,8},{8,4},{12,16},{16,12},{20,24},{24,20},{5,9},{9,5},{13,17},{1... | collective-permute-start | bytes 786440 | tf_op jit(solution)/shard_map/ppermute | solution.py:400
  47.8 6.1 %collective-permute-start.15 = (f32[4,8,8,256]{3,2,1,0:T(8,128)S(1)}, f32[4,8,8,256]{3,2,1,0:T(8,128)S(1)}, u32[]{:S(2)}, u32[]{:S(2)}) collective-permute-start(f32[4,8,8,256]{3,2,1,0:T(8,128)S(1)} %get-tuple-element.114.refs_3_.refs_0_), channel_id=1, source_target_pairs={{0,4},{4,0},{1,5},{5,1},{2,6},{6,2},{3,7},{7,3},{8,12},{12,8},{9,1... | collective-permute-start | bytes 786440 | tf_op jit(solution)/shard_map/ppermute | solution.py:401
  53.3 12.2 %collective-permute-start.21 = (f32[8,8,8,256]{3,2,1,0:T(8,128)S(1)}, f32[8,8,8,256]{3,2,1,0:T(8,128)S(1)}, u32[]{:S(2)}, u32[]{:S(2)}) collective-permute-start(f32[8,8,8,256]{3,2,1,0:T(8,128)S(1)} %get-tuple-element.126), channel_id=1, source_target_pairs={{0,4},{4,0},{1,5},{5,1},{2,6},{6,2},{3,7},{7,3},{8,12},{12,8},{9,1... | collective-permute-start | bytes 1572872 | tf_op jit(solution)/shard_map/ppermute | solution.py:485
  53.4 12.1 %collective-permute-start.20 = (f32[6,8,8,256]{3,2,1,0:T(8,128)S(1)}, f32[6,8,8,256]{3,2,1,0:T(8,128)S(1)}, u32[]{:S(2)}, u32[]{:S(2)}) collective-permute-start(f32[6,8,8,256]{3,2,1,0:T(8,128)S(1)} %get-tuple-element.125), channel_id=1, source_target_pairs={{0,4},{4,0},{1,5},{5,1},{2,6},{6,2},{3,7},{7,3},{8,12},{12,8},{9,1... | collective-permute-start | bytes 1179656 | tf_op jit(solution)/shard_map/ppermute | solution.py:485
  53.9 11.6 %collective-permute-start.22 = (f32[6,8,8,256]{3,2,1,0:T(8,128)S(1)}, f32[6,8,8,256]{3,2,1,0:T(8,128)S(1)}, u32[]{:S(2)}, u32[]{:S(2)}) collective-permute-start(f32[6,8,8,256]{3,2,1,0:T(8,128)S(1)} %get-tuple-element.127), channel_id=1, source_target_pairs={{0,4},{4,0},{1,5},{5,1},{2,6},{6,2},{3,7},{7,3},{8,12},{12,8},{9,1... | collective-permute-start | bytes 1179656 | tf_op jit(solution)/shard_map/ppermute | solution.py:485
  54.1 11.4 %collective-permute-start.23 = (f32[4,8,8,256]{3,2,1,0:T(8,128)S(1)}, f32[4,8,8,256]{3,2,1,0:T(8,128)S(1)}, u32[]{:S(2)}, u32[]{:S(2)}) collective-permute-start(f32[4,8,8,256]{3,2,1,0:T(8,128)S(1)} %get-tuple-element.128), channel_id=1, source_target_pairs={{0,4},{4,0},{1,5},{5,1},{2,6},{6,2},{3,7},{7,3},{8,12},{12,8},{9,1... | collective-permute-start | bytes 786440 | tf_op jit(solution)/shard_map/ppermute | solution.py:485
  56.2 2.6 %collective-permute-start.17 = (f32[4,8,128]{2,1,0:T(8,128)S(1)}, f32[4,8,128]{2,1,0:T(8,128)S(1)}, u32[]{:S(2)}, u32[]{:S(2)}) collective-permute-start(f32[4,8,128]{2,1,0:T(8,128)S(1)} %get-tuple-element.120.a_ref), channel_id=1, source_target_pairs={{0,1},{1,0},{2,3},{3,2},{4,5},{5,4},{6,7},{7,6},{8,9},{9,8},{10,11... | collective-permute-start | bytes 49160 | tf_op jit(solution)/shard_map/ppermute | solution.py:337
  58.8 3.5 %collective-permute-start.18 = (f32[4,8,128]{2,1,0:T(8,128)S(1)}, f32[4,8,128]{2,1,0:T(8,128)S(1)}, u32[]{:S(2)}, u32[]{:S(2)}) collective-permute-start(f32[4,8,128]{2,1,0:T(8,128)S(1)} %add.2.a_ref), channel_id=1, source_target_pairs={{0,2},{1,3},{2,0},{3,1},{4,6},{5,7},{6,4},{7,5},{8,10},{9,11},{10,... | collective-permute-start | bytes 49160 | tf_op jit(solution)/shard_map/ppermute | solution.py:337
  62.3 3.2 %collective-permute-start.19 = (f32[4,8,128]{2,1,0:T(8,128)S(1)}, f32[4,8,128]{2,1,0:T(8,128)S(1)}, u32[]{:S(2)}, u32[]{:S(2)}) collective-permute-start(f32[4,8,128]{2,1,0:T(8,128)S(1)} %add.3.mine_sums), channel_id=1, source_target_pairs={{0,4},{4,0},{1,5},{5,1},{2,6},{6,2},{3,7},{7,3},{8,12},{12,8},{9,1... | collective-permute-start | bytes 49160 | tf_op jit(solution)/shard_map/ppermute | solution.py:487

commit v5 on v4

--- a/solution.py
+++ b/solution.py
@@ -18,6 +18,7 @@
 
 SUB = 8
 LANES = 128
+BLOCKS = 4
 LAPS = 3
 FIELD = LAPS * RELAX
 REACH = FIELD + 2
@@ -258,91 +259,97 @@
         sums_ref[q] = totals[q]
 
 
-def last_kernel(cells, segments, mine_sums, other_sums, *refs):
+def layout_kernel(segments, low, *refs):
     n = len(segments)
-    out_ref, natural, sems = refs[2 * n :]
-    _, half, rows, _ = out_ref.shape
-    _, tiles, _, _, lanes = natural.shape
+    pair_ref, natural, sems = refs[n:]
+    _, tiles, half, rows, lanes = natural.shape
     flat = natural.reshape(2, tiles, half * rows, lanes)
     planes = 2 * half // SUB
     h = SUB // 2
-
-    gx = lax.axis_index("gx")
-    images = (gx, 1 - gx)
-
-    def factor(i):
-        sums_ref = (mine_sums, other_sums)[i]
-
-        def total(q):
-            return jnp.sum(sums_ref[q], keepdims=True) / cells
-
-        scale = lax.rsqrt(total(0) + epsilon)
-        spring = stiffness * (jnp.sqrt(total(1) + epsilon) - jnp.sqrt(total(2) + epsilon))
-        k = step_size * total(3) * scale * scale + spring * scale
-        return jnp.where(keeping(images[i]), jnp.zeros_like(k), k)
-
+    for parts, ref in zip(segments, refs[:n]):
+        for start, count, first in parts:
+            def body(j, carry, start=start, first=first, ref=ref):
+                for r in range(planes):
+                    for z in range(tiles):
+                        v = ref[first + j, r, :, z * lanes : (z + 1) * lanes]
+                        where = pl.ds(r * rows + start + j, h, stride=planes * rows)
+                        flat[0, z, where, :] = v[low : low + h]
+                        flat[1, z, where, :] = v[h - low : 2 * h - low]
+                return carry
+
+            lax.fori_loop(0, count, body, 0)
     copies = []
     for i in range(2):
-        k = factor(i)
-        image = images[i]
-        for parts, ref in zip(segments, refs[i * n : (i + 1) * n]):
-            for start, count, first in parts:
-                def body(j, carry, start=start, first=first, ref=ref, i=i, k=k):
-                    for r in range(planes):
-                        for z in range(tiles):
-                            at = slice(z * lanes, (z + 1) * lanes)
-                            v = ref[first + j, r, :, at]
-                            v = v + k * pltpu.roll(v, h, 0)
-                            where = pl.ds(r * rows + start + j, h, stride=planes * rows)
-                            flat[i, z, where, :] = v[i * h : i * h + h]
-                    return carry
-
-                lax.fori_loop(0, count, body, 0)
         for z in range(tiles):
-            part = out_ref.at[image, :, :, pl.ds(z * lanes, lanes)]
+            part = pair_ref.at[i, :, :, pl.ds(z * lanes, lanes)]
             copies.append(pltpu.make_async_copy(natural.at[i, z], part, sems.at[i, z]))
             copies[-1].start()
     for copy in copies:
         copy.wait()
 
 
+def last_kernel(cells, own, sums_ref, pair_ref, *refs):
+    out_ref, whole, sems = refs[-3:]
+    half = whole.shape[0]
+    gx = lax.axis_index("gx")
+    image = gx if own else 1 - gx
+
+    def total(q):
+        return jnp.sum(sums_ref[q], keepdims=True) / cells
+
+    scale = lax.rsqrt(total(0) + epsilon)
+    spring = stiffness * (jnp.sqrt(total(1) + epsilon) - jnp.sqrt(total(2) + epsilon))
+    k = step_size * total(3) * scale * scale + spring * scale
+    k = jnp.where(keeping(image), jnp.zeros_like(k), k)
+    copies = []
+    step = half // BLOCKS
+    for i in range(BLOCKS):
+        block = pl.ds(i * step, step)
+        whole[block] = pair_ref[0, block] + k * pair_ref[1, block]
+        copies.append(pltpu.make_async_copy(whole.at[block], out_ref.at[image, block], sems.at[i]))
+        copies[-1].start()
+    for copy in copies:
+        copy.wait()
+
+
 def ring(axis, distance):
     n = lax.axis_size(axis)
     return [(i, (i + distance) % n) for i in range(n)]
 
 
-def add_kernel(a_ref, b_ref, out_ref):
-    out_ref[...] = a_ref[...] + b_ref[...]
-
-
-def add(a, b):
+def add_kernel(a_ref, b_ref, *refs):
+    refs[-1][...] = a_ref[...] + b_ref[...]
+
+
+def add(a, b, *beside):
     return pl.pallas_call(
         add_kernel,
         out_shape=jax.ShapeDtypeStruct(a.shape, a.dtype),
-        in_specs=[VMEM] * 2,
+        in_specs=[VMEM] * (2 + len(beside)),
         out_specs=VMEM,
         compiler_params=PARAMS,
         cost_estimate=cost(1),
         name="add",
-    )(a, b)
-
-
-def total_over(value, axis):
+    )(a, b, *beside)
+
+
+def total_over(value, axis, beside):
     n = lax.axis_size(axis)
-    if n & (n - 1):
-        others = [lax.ppermute(value, axis, ring(axis, d)) for d in range(1, n)]
-        return functools.reduce(add, others, value)
-    d = 1
-    while d < n:
-        value = add(value, lax.ppermute(value, axis, [(i, i ^ d) for i in range(n)]))
-        d *= 2
+    routes = [ring(axis, d) for d in range(1, n)]
+    if n & (n - 1) == 0:
+        routes = [[(i, i ^ d) for i in range(n)] for d in (1 << b for b in range(n.bit_length() - 1))]
+    start = value
+    for route in routes:
+        last = route is routes[-1]
+        moved = lax.ppermute(start if n & (n - 1) else value, axis, route)
+        value = add(value, moved, *(beside if last else ()))
     return value
 
 
 def per_device(initial_path):
     count, half, rows, nz = initial_path.shape
     assert count == lax.axis_size("gx") == 2
-    assert rows % 2 == 0 and rows >= 2 * REACH and half % SUB == 0 and nz % LANES == 0
+    assert rows % 2 == 0 and rows >= 2 * REACH and half % (SUB * BLOCKS) == 0 and nz % LANES == 0
     planes = 2 * half // SUB
     cells = 2 * half * rows * lax.axis_size("gy") * nz
     chains = lax.axis_size("chain")
@@ -483,21 +490,35 @@
         )(*before, *pieces[some], *from_partner[some], *from_chain[some], *chemical[some])
         mine += outs[::2]
         halfway += [lax.ppermute(send, "gx", swap) for send in outs[1::2]]
-    total = total_over(total, "gy")
+    pairs = [
+        pl.pallas_call(
+            functools.partial(layout_kernel, segments, low),
+            out_shape=jax.ShapeDtypeStruct((2, half, rows, nz), jnp.float32),
+            in_specs=[VMEM] * len(some),
+            out_specs=VMEM,
+            scratch_shapes=[pltpu.VMEM((2, *part), jnp.float32), pltpu.SemaphoreType.DMA((2, tiles))],
+            compiler_params=PARAMS,
+            cost_estimate=cost(rows),
+            name="layout",
+        )(*some)
+        for low, some in ((0, mine), (SUB // 2, halfway))
+    ]
+    total = total_over(total, "gy", pairs)
     other = lax.ppermute(total, "gx", swap)
-    return pl.pallas_call(
-        functools.partial(last_kernel, cells, segments),
-        out_shape=jax.ShapeDtypeStruct(initial_path.shape, jnp.float32),
-        in_specs=[VMEM] * (2 + 2 * len(pieces)),
-        out_specs=hbm,
-        scratch_shapes=[
-            pltpu.VMEM((2, *part), jnp.float32),
-            pltpu.SemaphoreType.DMA((2, tiles)),
-        ],
-        compiler_params=PARAMS,
-        cost_estimate=cost(2 * rows),
-        name="last",
-    )(total, other, *mine, *halfway)
+    out = []
+    for own, sums, pair in ((True, total, pairs[0]), (False, other, pairs[1])):
+        out = [pl.pallas_call(
+            functools.partial(last_kernel, cells, own),
+            out_shape=jax.ShapeDtypeStruct(initial_path.shape, jnp.float32),
+            in_specs=[VMEM] * 2 + [hbm] * len(out),
+            out_specs=hbm,
+            scratch_shapes=[pltpu.VMEM((half, rows, nz), jnp.float32), pltpu.SemaphoreType.DMA((BLOCKS,))],
+            input_output_aliases={2: 0} if out else {},
+            compiler_params=PARAMS,
+            cost_estimate=cost(rows),
+            name="last",
+        )(sums, pair, *out)]
+    return out[0]
 
 
 def solution(mesh):

time: 68.3 us -> 67.4 us (0.987)
  waiting for transfers between devices: 10.7 us -> 8.35 us
  Pallas kernels: 20.3 us -> 22.4 us
  starting transfers between devices: 35.2 us -> 34.4 us
    pallas_call x1 -> x4, Pallas kernels: 2.42 us -> 4.44 us  [the longest x2 2.31 us: per_device(): pl.pallas_call(functools.partial(layout_kernel, segments, low), out_shape...]
    ppermute x2, waiting for transfers between devices: 4.16 us -> 2.6 us  [total_over(): moved = lax.ppermute(start if n & n - 1 else value, axis, route)]
    ppermute x1, waiting for transfers between devices: 0.84 us -> 0.01 us  [per_device(): other = lax.ppermute(total, 'gx', swap)]
    ppermute x1, starting transfers between devices: 2.36 us -> 1.53 us  [per_device(): other = lax.ppermute(total, 'gx', swap)]
  transfers between devices with their start and end apart: 24 -> 24, of which waited for: 7 -> 5; matrix products, arithmetic and copies ran while one was open for 0% -> 0% of each run, Pallas kernels for 25% -> 31%
where the time goes in v5:
time: 67.4 us; the launch traced here: 66.9 us
  starting transfers between devices  34.4 us (51%)
  Pallas kernels  22.4 us (33%)
  waiting for transfers between devices  8.35 us (12%)
  local copies, waits for them, and re-layouts  1.41 us (2%)
    ppermute x4, starting transfers between devices, exchange(): from_chain.append(lax.ppermute(piece, ('chain', 'gx'), along_chain))  15.2 us
    ppermute x4, starting transfers between devices, halos_of(): lax.ppermute(low, 'gy', ring('gy', -1))  9.57 us
    pallas_call x4, Pallas kernels, per_device(): pl.pallas_call(functools.partial(edge_kernel, rows, a, b, ahead, len(earl...  8.78 us
    pallas_call x1, Pallas kernels, per_device(): pl.pallas_call(functools.partial(inner_kernel, rows, made[1]), out_shape=...  4.61 us
    ppermute x4, waiting for transfers between devices, halos_of(): lax.ppermute(high, 'gy', ring('gy', 1))  3.43 us
    ppermute x4, starting transfers between devices, per_device(): halfway += [lax.ppermute(send, 'gx', swap) for send in outs[1::2]]  2.68 us
    ppermute x2, waiting for transfers between devices, total_over(): moved = lax.ppermute(start if n & n - 1 else value, axis, route)  2.6 us
    pallas_call x2, Pallas kernels, per_device(): pl.pallas_call(functools.partial(layout_kernel, segments, low), out_shape...  2.31 us
  transfers between devices with their start and end apart: 24, of which 5 were waited for; matrix products, arithmetic and copies ran while one was open for 0% of the time, Pallas kernels for 31%

profile of v5, /device:TPU:5, one launch (start us, length us, event | category | flops | bytes accessed | tf_op | source)
XLA Modules:
  0.0 66.9 jit_solution(16986826958911539491)
XLA Ops:
  0.0 1.4 %copy-done = f32[2,32,24,256]{3,2,1,0:T(8,128)S(1)} copy-done((f32[2,32,24,256]{3,2,1,0:T(8,128)S(1)}, f32[2,32,24,256]{3,2,1,0:T(8,128)}, u32[]{:S(2)}) %copy-start) | copy-done | bytes 1572888
  1.4 0.1 cut.1
  1.5 0.7 %collective-permute-start = (f32[2,32,24,128]{3,2,1,0:T(8,128)S(1)}, f32[2,32,24,128]{3,2,1,0:T(8,128)S(1)}, u32[]{:S(2)}, u32[]{:S(2)}) collective-permute-start(f32[2,32,24,128]{3,2,1,0:T(8,128)S(1)} %cut.1), channel_id=1, source_target_pairs={{0,4},{4,0},{1,5},{5,1},{2,6},{6,2},{3,7},{7,3},{8,12},{12,8},{9,1... | collective-permute-start | bytes 2359304 | tf_op jit(solution)/shard_map/ppermute | solution.py:374
  2.2 0.7 own.1.own_ref
  2.9 1.3 %collective-permute-done.recv_ref = f32[2,32,24,128]{3,2,1,0:T(8,128)S(1)} collective-permute-done((f32[2,32,24,128]{3,2,1,0:T(8,128)S(1)}, f32[2,32,24,128]{3,2,1,0:T(8,128)S(1)}, u32[]{:S(2)}, u32[]{:S(2)}) %collective-permute-start) | collective-permute-done | bytes 786464 | tf_op jit(solution)/shard_map/ppermute | solution.py:374
  4.1 0.7 %first.1 = (f32[24,8,8,256]{3,2,1,0:T(8,128)S(1)}, f32[4,8,8,256]{3,2,1,0:T(8,128)S(1)}, f32[4,8,8,256]{3,2,1,0:T(8,128)S(1)}, f32[3,8,8,256]{3,2,1,0:T(8,128)S(...) custom-call(f32[24,8,8,256]{3,2,1,0:T(8,128)S(1)} %own.1.own_ref, ...), custom_call_target="tpu_custom_call" | custom-call | bytes 2340000 | tf_op jit(solution)/shard_map/first/pallas_call | solution.py:392
  4.9 1.3 %collective-permute-start.1 = (f32[4,8,8,256]{3,2,1,0:T(8,128)S(1)}, f32[4,8,8,256]{3,2,1,0:T(8,128)S(1)}, u32[]{:S(2)}, u32[]{:S(2)}) collective-permute-start(f32[4,8,8,256]{3,2,1,0:T(8,128)S(1)} %get-tuple-element.69), channel_id=1, source_target_pairs={{0,1},{1,2},{2,3},{3,0},{4,5},{5,6},{6,7},{7,4},{8,9},{9,10},{10,1... | collective-permute-start | bytes 786440 | tf_op jit(solution)/shard_map/ppermute | solution.py:413
  6.2 2.1 %collective-permute-start.2 = (f32[4,8,8,256]{3,2,1,0:T(8,128)S(1)}, f32[4,8,8,256]{3,2,1,0:T(8,128)S(1)}, u32[]{:S(2)}, u32[]{:S(2)}) collective-permute-start(f32[4,8,8,256]{3,2,1,0:T(8,128)S(1)} %get-tuple-element.70), channel_id=1, source_target_pairs={{0,3},{1,0},{2,1},{3,2},{4,7},{5,4},{6,5},{7,6},{8,11},{9,8},{10,9... | collective-permute-start | bytes 786440 | tf_op jit(solution)/shard_map/ppermute | solution.py:414
  8.3 4.6 %inner.1 = (f32[22,8,8,256]{3,2,1,0:T(8,128)S(1)}, f32[20,8,8,256]{3,2,1,0:T(8,128)S(1)}, f32[18,8,8,256]{3,2,1,0:T(8,128)S(1)}, f32[16,8,8,256]{3,2,1,0:T(8,128...) custom-call(f32[24,8,8,256]{3,2,1,0:T(8,128)S(1)} %get-tuple-element, ...), custom_call_target="tpu_custom_call" | custom-call | bytes 16380000 | tf_op jit(solution)/shard_map/inner/pallas_call | solution.py:419
  12.9 3.8 %collective-permute-start.5 = (f32[6,8,8,256]{3,2,1,0:T(8,128)S(1)}, f32[6,8,8,256]{3,2,1,0:T(8,128)S(1)}, u32[]{:S(2)}, u32[]{:S(2)}) collective-permute-start(f32[6,8,8,256]{3,2,1,0:T(8,128)S(1)} %get-tuple-element.68.refs_0_), channel_id=1, source_target_pairs={{4,8},{8,4},{12,16},{16,12},{20,24},{24,20},{5,9},{9,5},{13,17},{1... | collective-permute-start | bytes 1179656 | tf_op jit(solution)/shard_map/ppermute | solution.py:407
  16.7 0.1 collective-permute-start.3
  16.8 3.3 %collective-permute-start.4 = (f32[3,8,8,256]{3,2,1,0:T(8,128)S(1)}, f32[3,8,8,256]{3,2,1,0:T(8,128)S(1)}, u32[]{:S(2)}, u32[]{:S(2)}) collective-permute-start(f32[3,8,8,256]{3,2,1,0:T(8,128)S(1)} %get-tuple-element.81), channel_id=1, source_target_pairs={{0,3},{1,0},{2,1},{3,2},{4,7},{5,4},{6,5},{7,6},{8,11},{9,8},{10,9... | collective-permute-start | bytes 589832 | tf_op jit(solution)/shard_map/ppermute | solution.py:414
  20.1 0.0 collective-permute-done.1.low_ref
  20.1 0.0 collective-permute-done.2.high_ref
  20.1 2.9 %edge.4 = (f32[8,8,8,256]{3,2,1,0:T(8,128)S(1)}, f32[14,8,8,256]{3,2,1,0:T(8,128)S(1)}, f32[12,8,8,256]{3,2,1,0:T(8,128)S(1)}, f32[12,8,8,256]{3,2,1,0:T(8,128)S...) custom-call(f32[24,8,8,256]{3,2,1,0:T(8,128)S(1)} %get-tuple-element, ...), custom_call_target="tpu_custom_call" | custom-call | bytes 9360000 | tf_op jit(solution)/shard_map/edge/pallas_call | solution.py:444
  23.0 4.9 %collective-permute-start.9 = (f32[8,8,8,256]{3,2,1,0:T(8,128)S(1)}, f32[8,8,8,256]{3,2,1,0:T(8,128)S(1)}, u32[]{:S(2)}, u32[]{:S(2)}) collective-permute-start(f32[8,8,8,256]{3,2,1,0:T(8,128)S(1)} %get-tuple-element.79.refs_1_), channel_id=1, source_target_pairs={{4,8},{8,4},{12,16},{16,12},{20,24},{24,20},{5,9},{9,5},{13,17},{1... | collective-permute-start | bytes 1572872 | tf_op jit(solution)/shard_map/ppermute | solution.py:407
  27.9 0.3 collective-permute-start.13
  28.2 0.0 collective-permute-done.3.low_ref
  28.2 3.0 %collective-permute-start.14 = (f32[2,8,8,256]{3,2,1,0:T(8,128)S(1)}, f32[2,8,8,256]{3,2,1,0:T(8,128)S(1)}, u32[]{:S(2)}, u32[]{:S(2)}) collective-permute-start(f32[2,8,8,256]{3,2,1,0:T(8,128)S(1)} %get-tuple-element.95), channel_id=1, source_target_pairs={{0,3},{1,0},{2,1},{3,2},{4,7},{5,4},{6,5},{7,6},{8,11},{9,8},{10,9... | collective-permute-start | bytes 393224 | tf_op jit(solution)/shard_map/ppermute | solution.py:414
  31.2 0.0 collective-permute-start.11
  31.2 0.0 collective-permute-done.5.refs_9_.refs_6_
  31.2 0.2 collective-permute-start.7
  31.4 2.2 %edge.5 = (f32[6,8,8,256]{3,2,1,0:T(8,128)S(1)}, f32[12,8,8,256]{3,2,1,0:T(8,128)S(1)}, f32[10,8,8,256]{3,2,1,0:T(8,128)S(1)}, f32[10,8,8,256]{3,2,1,0:T(8,128)S...) custom-call(f32[24,8,8,256]{3,2,1,0:T(8,128)S(1)} %get-tuple-element, ...), custom_call_target="tpu_custom_call" | custom-call | bytes 7020000 | tf_op jit(solution)/shard_map/edge/pallas_call | solution.py:444
  33.6 1.4 %collective-permute-done.13.low_ref = f32[2,8,8,256]{3,2,1,0:T(8,128)S(1)} collective-permute-done((f32[2,8,8,256]{3,2,1,0:T(8,128)S(1)}, f32[2,8,8,256]{3,2,1,0:T(8,128)S(1)}, u32[]{:S(2)}, u32[]{:S(2)}) %collective-permute-start.13) | collective-permute-done | bytes 131104 | tf_op jit(solution)/shard_map/ppermute | solution.py:413
  35.0 2.4 %collective-permute-start.10 = (f32[6,8,8,256]{3,2,1,0:T(8,128)S(1)}, f32[6,8,8,256]{3,2,1,0:T(8,128)S(1)}, u32[]{:S(2)}, u32[]{:S(2)}) collective-permute-start(f32[6,8,8,256]{3,2,1,0:T(8,128)S(1)} %get-tuple-element.91.refs_2_), channel_id=1, source_target_pairs={{4,8},{8,4},{12,16},{16,12},{20,24},{24,20},{5,9},{9,5},{13,17},{1... | collective-permute-start | bytes 1179656 | tf_op jit(solution)/shard_map/ppermute | solution.py:407
  37.4 0.0 collective-permute-done.14.high_ref
  37.4 0.1 collective-permute-start.6
  37.6 2.1 %collective-permute-done.11.low_ref = f32[2,8,8,256]{3,2,1,0:T(8,128)S(1)} collective-permute-done((f32[2,8,8,256]{3,2,1,0:T(8,128)S(1)}, f32[2,8,8,256]{3,2,1,0:T(8,128)S(1)}, u32[]{:S(2)}, u32[]{:S(2)}) %collective-permute-start.11) | collective-permute-done | bytes 131104 | tf_op jit(solution)/shard_map/ppermute | solution.py:413
  39.6 1.2 %collective-permute-start.12 = (f32[2,8,8,256]{3,2,1,0:T(8,128)S(1)}, f32[2,8,8,256]{3,2,1,0:T(8,128)S(1)}, u32[]{:S(2)}, u32[]{:S(2)}) collective-permute-start(f32[2,8,8,256]{3,2,1,0:T(8,128)S(1)} %get-tuple-element.93), channel_id=1, source_target_pairs={{0,3},{1,0},{2,1},{3,2},{4,7},{5,4},{6,5},{7,6},{8,11},{9,8},{10,9... | collective-permute-start | bytes 393224 | tf_op jit(solution)/shard_map/ppermute | solution.py:414
  40.9 1.8 %edge.6 = (f32[4,8,8,256]{3,2,1,0:T(8,128)S(1)}, f32[10,8,8,256]{3,2,1,0:T(8,128)S(1)}, f32[8,8,8,256]{3,2,1,0:T(8,128)S(1)}, f32[8,8,8,256]{3,2,1,0:T(8,128)S(1...) custom-call(f32[24,8,8,256]{3,2,1,0:T(8,128)S(1)} %get-tuple-element, ...), custom_call_target="tpu_custom_call" | custom-call | bytes 4680000 | tf_op jit(solution)/shard_map/edge/pallas_call | solution.py:444
  42.7 1.0 %collective-permute-done.12.high_ref = f32[2,8,8,256]{3,2,1,0:T(8,128)S(1)} collective-permute-done((f32[2,8,8,256]{3,2,1,0:T(8,128)S(1)}, f32[2,8,8,256]{3,2,1,0:T(8,128)S(1)}, u32[]{:S(2)}, u32[]{:S(2)}) %collective-permute-start.12) | collective-permute-done | bytes 131104 | tf_op jit(solution)/shard_map/ppermute | solution.py:414
  43.8 4.0 %collective-permute-start.16 = (f32[4,8,8,256]{3,2,1,0:T(8,128)S(1)}, f32[4,8,8,256]{3,2,1,0:T(8,128)S(1)}, u32[]{:S(2)}, u32[]{:S(2)}) collective-permute-start(f32[4,8,8,256]{3,2,1,0:T(8,128)S(1)} %get-tuple-element.114.refs_3_.refs_0_), channel_id=1, source_target_pairs={{4,8},{8,4},{12,16},{16,12},{20,24},{24,20},{5,9},{9,5},{13,17},{1... | collective-permute-start | bytes 786440 | tf_op jit(solution)/shard_map/ppermute | solution.py:407
  47.8 0.7 %collective-permute-start.15 = (f32[4,8,8,256]{3,2,1,0:T(8,128)S(1)}, f32[4,8,8,256]{3,2,1,0:T(8,128)S(1)}, u32[]{:S(2)}, u32[]{:S(2)}) collective-permute-start(f32[4,8,8,256]{3,2,1,0:T(8,128)S(1)} %get-tuple-element.114.refs_3_.refs_0_), channel_id=1, source_target_pairs={{0,4},{4,0},{1,5},{5,1},{2,6},{6,2},{3,7},{7,3},{8,12},{12,8},{9,1... | collective-permute-start | bytes 786440 | tf_op jit(solution)/shard_map/ppermute | solution.py:408
  48.5 1.8 %edge.7.halo_ref = f32[4,8,8,256]{3,2,1,0:T(8,128)S(1)} custom-call(f32[24,8,8,256]{3,2,1,0:T(8,128)S(1)} %get-tuple-element.67.slab_ref.refs_0_, f32[2,8,8,256]{3,2,1,0:T(8,128)S(1)} %collective-permute-done.11.low_ref, f32[2,8,8,256]{3,2,1,0:T(8,128)S(1)} %collective-permute-done.12.high_ref, f32[10,8,8,256]{3,2,1,0:T(8,128)S(1)} %get-tuple-element.105.refs_0_, ...), custom_call_target="tpu_custom_call" | custom-call | bytes 4680000 | tf_op jit(solution)/shard_map/edge/pallas_call | solution.py:444
  50.3 2.0 %chemical.1 = (f32[6,8,8,256]{3,2,1,0:T(8,128)S(1)}, f32[8,8,8,256]{3,2,1,0:T(8,128)S(1)}, f32[6,8,8,256]{3,2,1,0:T(8,128)S(1)}, f32[4,8,8,256]{3,2,1,0:T(8,128)S(1)}) custom-call(f32[4,8,8,256]{3,2,1,0:T(8,128)S(1)} %edge.7.halo_ref, f32[6,8,8,256]{3,2,1,0:T(8,128)S(1)} %get-tuple-element.68.refs_0_, f32[8,8,8,256]{3,2,1,0:T(8,128)S(1)} %get-tuple-element.79.refs_1_, ...), custom_call_target="tpu_custom_call" | custom-call | bytes 6240000 | tf_op jit(solution)/shard_map/chemical/pallas_call | solution.py:463
  52.4 0.9 %sums.2 = (f32[4,8,128]{2,1,0:T(8,128)S(1)}, f32[6,8,8,256]{3,2,1,0:T(8,128)S(1)}, f32[6,8,8,256]{3,2,1,0:T(8,128)S(1)}, f32[8,8,8,256]{3,2,1,0:T(8,128)S(1)}, f...) custom-call(f32[6,8,8,256]{3,2,1,0:T(8,128)S(1)} %get-tuple-element.68.refs_0_, ...), custom_call_target="tpu_custom_call" | custom-call | bytes 1560000 | tf_op jit(solution)/shard_map/sums/pallas_call | solution.py:481
  53.3 0.1 collective-permute-start.20
  53.4 0.5 collective-permute-start.19
  53.9 0.1 collective-permute-start.21
  53.9 0.2 sums.3
  54.1 2.0 %collective-permute-start.22 = (f32[4,8,8,256]{3,2,1,0:T(8,128)S(1)}, f32[4,8,8,256]{3,2,1,0:T(8,128)S(1)}, u32[]{:S(2)}, u32[]{:S(2)}) collective-permute-start(f32[4,8,8,256]{3,2,1,0:T(8,128)S(1)} %get-tuple-element.128), channel_id=1, source_target_pairs={{0,4},{4,0},{1,5},{5,1},{2,6},{6,2},{3,7},{7,3},{8,12},{12,8},{9,1... | collective-permute-start | bytes 786440 | tf_op jit(solution)/shard_map/ppermute | solution.py:492
  56.2 2.6 %collective-permute-done.17.b_ref = f32[4,8,128]{2,1,0:T(8,128)S(1)} collective-permute-done((f32[4,8,128]{2,1,0:T(8,128)S(1)}, f32[4,8,128]{2,1,0:T(8,128)S(1)}, u32[]{:S(2)}, u32[]{:S(2)}) %collective-permute-start.17) | collective-permute-done | bytes 16416 | tf_op jit(solution)/shard_map/ppermute | solution.py:344
  58.8 1.9 %collective-permute-start.18 = (f32[4,8,128]{2,1,0:T(8,128)S(1)}, f32[4,8,128]{2,1,0:T(8,128)S(1)}, u32[]{:S(2)}, u32[]{:S(2)}) collective-permute-start(f32[4,8,128]{2,1,0:T(8,128)S(1)} %add.2.a_ref), channel_id=1, source_target_pairs={{0,2},{1,3},{2,0},{3,1},{4,6},{5,7},{6,4},{7,5},{8,10},{9,11},{10,... | collective-permute-start | bytes 49160 | tf_op jit(solution)/shard_map/ppermute | solution.py:344
  60.7 1.2 %layout.2.refs_0_.pair_ref = f32[2,32,24,256]{3,2,1,0:T(8,128)S(1)} custom-call(f32[6,8,8,256]{3,2,1,0:T(8,128)S(1)} %get-tuple-element.121.refs_0_, f32[8,8,8,256]{3,2,1,0:T(8,128)S(1)} %get-tuple-element.122.refs_1_, f32[6,8,8,256]{3,2,1,0:T(8,128)S(1)} %get-tuple-element.123.refs_2_, f32[4,8,8,256]{3,2,1,0:T(8,128)S(1)} %get-tuple-element.124.refs_3_), custom_call_target="tpu_custom_call" | custom-call | bytes 3120000 | tf_op jit(solution)/shard_map/layout/pallas_call | solution.py:494
  61.9 1.2 %layout.3.refs_1_.pair_ref = f32[2,32,24,256]{3,2,1,0:T(8,128)S(1)} custom-call(f32[6,8,8,256]{3,2,1,0:T(8,128)S(1)} %collective-permute-done.19.refs_0_, f32[8,8,8,256]{3,2,1,0:T(8,128)S(1)} %collective-permute-done.20.refs_1_, f32[6,8,8,256]{3,2,1,0:T(8,128)S(1)} %collective-permute-done.21.refs_2_, f32[4,8,8,256]{3,2,1,0:T(8,128)S(1)} %collective-permute-done.22.refs_3_), custom_call_target="tpu_custom_call" | custom-call | bytes 3120000 | tf_op jit(solution)/shard_map/layout/pallas_call | solution.py:494
  63.1 1.5 %collective-permute-start.23 = (f32[4,8,128]{2,1,0:T(8,128)S(1)}, f32[4,8,128]{2,1,0:T(8,128)S(1)}, u32[]{:S(2)}, u32[]{:S(2)}) collective-permute-start(f32[4,8,128]{2,1,0:T(8,128)S(1)} %add.3.sums_ref), channel_id=1, source_target_pairs={{0,4},{4,0},{1,5},{5,1},{2,6},{6,2},{3,7},{7,3},{8,12},{12,8},{9,1... | collective-permute-start | bytes 49160 | tf_op jit(solution)/shard_map/ppermute | solution.py:507
  64.6 1.1 %last.2.refs_0_ = f32[2,32,24,256]{3,2,1,0:T(8,128)} custom-call(f32[4,8,128]{2,1,0:T(8,128)S(1)} %add.3.sums_ref, f32[2,32,24,256]{3,2,1,0:T(8,128)S(1)} %layout.2.refs_0_.pair_ref), custom_call_target="tpu_custom_call" | custom-call | bytes 3120000 | tf_op jit(solution)/shard_map/last/pallas_call | solution.py:510
  65.7 1.1 %last.3 = f32[2,32,24,256]{3,2,1,0:T(8,128)} custom-call(f32[4,8,128]{2,1,0:T(8,128)S(1)} %collective-permute-done.23.sums_ref, f32[2,32,24,256]{3,2,1,0:T(8,128)S(1)} %layout.3.refs_1_.pair_ref, f32[2,32,24,256]{3,2,1,0:T(8,128)} %last.2.refs_0_), custom_call_target="tpu_custom_call", output_to_operand_aliasing={{}: (2, {})} | custom-call | bytes 3120000 | tf_op jit(solution)/shard_map/last/pallas_call | solution.py:510
  (19 shorter events, 0.1 us)
Async XLA Ops:
  0.0 1.4 %copy-start = (f32[2,32,24,256]{3,2,1,0:T(8,128)S(1)}, f32[2,32,24,256]{3,2,1,0:T(8,128)}, u32[]{:S(2)}) copy-start(f32[2,32,24,256]{3,2,1,0:T(8,128)} %whole_ref.3) | copy-start | bytes 4718596
  1.5 2.7 %collective-permute-start = (f32[2,32,24,128]{3,2,1,0:T(8,128)S(1)}, f32[2,32,24,128]{3,2,1,0:T(8,128)S(1)}, u32[]{:S(2)}, u32[]{:S(2)}) collective-permute-start(f32[2,32,24,128]{3,2,1,0:T(8,128)S(1)} %cut.1), channel_id=1, source_target_pairs={{0,4},{4,0},{1,5},{5,1},{2,6},{6,2},{3,7},{7,3},{8,12},{12,8},{9,1... | collective-permute-start | bytes 2359304 | tf_op jit(solution)/shard_map/ppermute | solution.py:374
  4.9 15.2 %collective-permute-start.1 = (f32[4,8,8,256]{3,2,1,0:T(8,128)S(1)}, f32[4,8,8,256]{3,2,1,0:T(8,128)S(1)}, u32[]{:S(2)}, u32[]{:S(2)}) collective-permute-start(f32[4,8,8,256]{3,2,1,0:T(8,128)S(1)} %get-tuple-element.69), channel_id=1, source_target_pairs={{0,1},{1,2},{2,3},{3,0},{4,5},{5,6},{6,7},{7,4},{8,9},{9,10},{10,1... | collective-permute-start | bytes 786440 | tf_op jit(solution)/shard_map/ppermute | solution.py:413
  6.2 13.9 %collective-permute-start.2 = (f32[4,8,8,256]{3,2,1,0:T(8,128)S(1)}, f32[4,8,8,256]{3,2,1,0:T(8,128)S(1)}, u32[]{:S(2)}, u32[]{:S(2)}) collective-permute-start(f32[4,8,8,256]{3,2,1,0:T(8,128)S(1)} %get-tuple-element.70), channel_id=1, source_target_pairs={{0,3},{1,0},{2,1},{3,2},{4,7},{5,4},{6,5},{7,6},{8,11},{9,8},{10,9... | collective-permute-start | bytes 786440 | tf_op jit(solution)/shard_map/ppermute | solution.py:414
  12.9 18.3 %collective-permute-start.5 = (f32[6,8,8,256]{3,2,1,0:T(8,128)S(1)}, f32[6,8,8,256]{3,2,1,0:T(8,128)S(1)}, u32[]{:S(2)}, u32[]{:S(2)}) collective-permute-start(f32[6,8,8,256]{3,2,1,0:T(8,128)S(1)} %get-tuple-element.68.refs_0_), channel_id=1, source_target_pairs={{4,8},{8,4},{12,16},{16,12},{20,24},{24,20},{5,9},{9,5},{13,17},{1... | collective-permute-start | bytes 1179656 | tf_op jit(solution)/shard_map/ppermute | solution.py:407
  16.7 11.5 %collective-permute-start.3 = (f32[3,8,8,256]{3,2,1,0:T(8,128)S(1)}, f32[3,8,8,256]{3,2,1,0:T(8,128)S(1)}, u32[]{:S(2)}, u32[]{:S(2)}) collective-permute-start(f32[3,8,8,256]{3,2,1,0:T(8,128)S(1)} %get-tuple-element.80), channel_id=1, source_target_pairs={{0,1},{1,2},{2,3},{3,0},{4,5},{5,6},{6,7},{7,4},{8,9},{9,10},{10,1... | collective-permute-start | bytes 589832 | tf_op jit(solution)/shard_map/ppermute | solution.py:413
  16.8 14.4 %collective-permute-start.4 = (f32[3,8,8,256]{3,2,1,0:T(8,128)S(1)}, f32[3,8,8,256]{3,2,1,0:T(8,128)S(1)}, u32[]{:S(2)}, u32[]{:S(2)}) collective-permute-start(f32[3,8,8,256]{3,2,1,0:T(8,128)S(1)} %get-tuple-element.81), channel_id=1, source_target_pairs={{0,3},{1,0},{2,1},{3,2},{4,7},{5,4},{6,5},{7,6},{8,11},{9,8},{10,9... | collective-permute-start | bytes 589832 | tf_op jit(solution)/shard_map/ppermute | solution.py:414
  23.0 16.7 %collective-permute-start.9 = (f32[8,8,8,256]{3,2,1,0:T(8,128)S(1)}, f32[8,8,8,256]{3,2,1,0:T(8,128)S(1)}, u32[]{:S(2)}, u32[]{:S(2)}) collective-permute-start(f32[8,8,8,256]{3,2,1,0:T(8,128)S(1)} %get-tuple-element.79.refs_1_), channel_id=1, source_target_pairs={{4,8},{8,4},{12,16},{16,12},{20,24},{24,20},{5,9},{9,5},{13,17},{1... | collective-permute-start | bytes 1572872 | tf_op jit(solution)/shard_map/ppermute | solution.py:407
  27.9 7.1 %collective-permute-start.13 = (f32[2,8,8,256]{3,2,1,0:T(8,128)S(1)}, f32[2,8,8,256]{3,2,1,0:T(8,128)S(1)}, u32[]{:S(2)}, u32[]{:S(2)}) collective-permute-start(f32[2,8,8,256]{3,2,1,0:T(8,128)S(1)} %get-tuple-element.94), channel_id=1, source_target_pairs={{0,1},{1,2},{2,3},{3,0},{4,5},{5,6},{6,7},{7,4},{8,9},{9,10},{10,1... | collective-permute-start | bytes 393224 | tf_op jit(solution)/shard_map/ppermute | solution.py:413
  28.2 9.2 %collective-permute-start.14 = (f32[2,8,8,256]{3,2,1,0:T(8,128)S(1)}, f32[2,8,8,256]{3,2,1,0:T(8,128)S(1)}, u32[]{:S(2)}, u32[]{:S(2)}) collective-permute-start(f32[2,8,8,256]{3,2,1,0:T(8,128)S(1)} %get-tuple-element.95), channel_id=1, source_target_pairs={{0,3},{1,0},{2,1},{3,2},{4,7},{5,4},{6,5},{7,6},{8,11},{9,8},{10,9... | collective-permute-start | bytes 393224 | tf_op jit(solution)/shard_map/ppermute | solution.py:414
  31.2 8.4 %collective-permute-start.11 = (f32[2,8,8,256]{3,2,1,0:T(8,128)S(1)}, f32[2,8,8,256]{3,2,1,0:T(8,128)S(1)}, u32[]{:S(2)}, u32[]{:S(2)}) collective-permute-start(f32[2,8,8,256]{3,2,1,0:T(8,128)S(1)} %get-tuple-element.92), channel_id=1, source_target_pairs={{0,1},{1,2},{2,3},{3,0},{4,5},{5,6},{6,7},{7,4},{8,9},{9,10},{10,1... | collective-permute-start | bytes 393224 | tf_op jit(solution)/shard_map/ppermute | solution.py:413
  31.2 21.2 %collective-permute-start.7 = (f32[8,8,8,256]{3,2,1,0:T(8,128)S(1)}, f32[8,8,8,256]{3,2,1,0:T(8,128)S(1)}, u32[]{:S(2)}, u32[]{:S(2)}) collective-permute-start(f32[8,8,8,256]{3,2,1,0:T(8,128)S(1)} %get-tuple-element.79.refs_1_), channel_id=1, source_target_pairs={{0,4},{4,0},{1,5},{5,1},{2,6},{6,2},{3,7},{7,3},{8,12},{12,8},{9,1... | collective-permute-start | bytes 1572872 | tf_op jit(solution)/shard_map/ppermute | solution.py:408
  35.0 12.8 %collective-permute-start.10 = (f32[6,8,8,256]{3,2,1,0:T(8,128)S(1)}, f32[6,8,8,256]{3,2,1,0:T(8,128)S(1)}, u32[]{:S(2)}, u32[]{:S(2)}) collective-permute-start(f32[6,8,8,256]{3,2,1,0:T(8,128)S(1)} %get-tuple-element.91.refs_2_), channel_id=1, source_target_pairs={{4,8},{8,4},{12,16},{16,12},{20,24},{24,20},{5,9},{9,5},{13,17},{1... | collective-permute-start | bytes 1179656 | tf_op jit(solution)/shard_map/ppermute | solution.py:407
  37.4 14.9 %collective-permute-start.6 = (f32[6,8,8,256]{3,2,1,0:T(8,128)S(1)}, f32[6,8,8,256]{3,2,1,0:T(8,128)S(1)}, u32[]{:S(2)}, u32[]{:S(2)}) collective-permute-start(f32[6,8,8,256]{3,2,1,0:T(8,128)S(1)} %get-tuple-element.68.refs_0_), channel_id=1, source_target_pairs={{0,4},{4,0},{1,5},{5,1},{2,6},{6,2},{3,7},{7,3},{8,12},{12,8},{9,1... | collective-permute-start | bytes 1179656 | tf_op jit(solution)/shard_map/ppermute | solution.py:408
  39.6 12.8 %collective-permute-start.8 = (f32[6,8,8,256]{3,2,1,0:T(8,128)S(1)}, f32[6,8,8,256]{3,2,1,0:T(8,128)S(1)}, u32[]{:S(2)}, u32[]{:S(2)}) collective-permute-start(f32[6,8,8,256]{3,2,1,0:T(8,128)S(1)} %get-tuple-element.91.refs_2_), channel_id=1, source_target_pairs={{0,4},{4,0},{1,5},{5,1},{2,6},{6,2},{3,7},{7,3},{8,12},{12,8},{9,1... | collective-permute-start | bytes 1179656 | tf_op jit(solution)/shard_map/ppermute | solution.py:408
  39.6 4.1 %collective-permute-start.12 = (f32[2,8,8,256]{3,2,1,0:T(8,128)S(1)}, f32[2,8,8,256]{3,2,1,0:T(8,128)S(1)}, u32[]{:S(2)}, u32[]{:S(2)}) collective-permute-start(f32[2,8,8,256]{3,2,1,0:T(8,128)S(1)} %get-tuple-element.93), channel_id=1, source_target_pairs={{0,3},{1,0},{2,1},{3,2},{4,7},{5,4},{6,5},{7,6},{8,11},{9,8},{10,9... | collective-permute-start | bytes 393224 | tf_op jit(solution)/shard_map/ppermute | solution.py:414
  43.8 10.2 %collective-permute-start.16 = (f32[4,8,8,256]{3,2,1,0:T(8,128)S(1)}, f32[4,8,8,256]{3,2,1,0:T(8,128)S(1)}, u32[]{:S(2)}, u32[]{:S(2)}) collective-permute-start(f32[4,8,8,256]{3,2,1,0:T(8,128)S(1)} %get-tuple-element.114.refs_3_.refs_0_), channel_id=1, source_target_pairs={{4,8},{8,4},{12,16},{16,12},{20,24},{24,20},{5,9},{9,5},{13,17},{1... | collective-permute-start | bytes 786440 | tf_op jit(solution)/shard_map/ppermute | solution.py:407
  47.8 6.1 %collective-permute-start.15 = (f32[4,8,8,256]{3,2,1,0:T(8,128)S(1)}, f32[4,8,8,256]{3,2,1,0:T(8,128)S(1)}, u32[]{:S(2)}, u32[]{:S(2)}) collective-permute-start(f32[4,8,8,256]{3,2,1,0:T(8,128)S(1)} %get-tuple-element.114.refs_3_.refs_0_), channel_id=1, source_target_pairs={{0,4},{4,0},{1,5},{5,1},{2,6},{6,2},{3,7},{7,3},{8,12},{12,8},{9,1... | collective-permute-start | bytes 786440 | tf_op jit(solution)/shard_map/ppermute | solution.py:408
  53.3 8.6 %collective-permute-start.20 = (f32[8,8,8,256]{3,2,1,0:T(8,128)S(1)}, f32[8,8,8,256]{3,2,1,0:T(8,128)S(1)}, u32[]{:S(2)}, u32[]{:S(2)}) collective-permute-start(f32[8,8,8,256]{3,2,1,0:T(8,128)S(1)} %get-tuple-element.126), channel_id=1, source_target_pairs={{0,4},{4,0},{1,5},{5,1},{2,6},{6,2},{3,7},{7,3},{8,12},{12,8},{9,1... | collective-permute-start | bytes 1572872 | tf_op jit(solution)/shard_map/ppermute | solution.py:492
  53.4 8.5 %collective-permute-start.19 = (f32[6,8,8,256]{3,2,1,0:T(8,128)S(1)}, f32[6,8,8,256]{3,2,1,0:T(8,128)S(1)}, u32[]{:S(2)}, u32[]{:S(2)}) collective-permute-start(f32[6,8,8,256]{3,2,1,0:T(8,128)S(1)} %get-tuple-element.125), channel_id=1, source_target_pairs={{0,4},{4,0},{1,5},{5,1},{2,6},{6,2},{3,7},{7,3},{8,12},{12,8},{9,1... | collective-permute-start | bytes 1179656 | tf_op jit(solution)/shard_map/ppermute | solution.py:492
  53.9 8.0 %collective-permute-start.21 = (f32[6,8,8,256]{3,2,1,0:T(8,128)S(1)}, f32[6,8,8,256]{3,2,1,0:T(8,128)S(1)}, u32[]{:S(2)}, u32[]{:S(2)}) collective-permute-start(f32[6,8,8,256]{3,2,1,0:T(8,128)S(1)} %get-tuple-element.127), channel_id=1, source_target_pairs={{0,4},{4,0},{1,5},{5,1},{2,6},{6,2},{3,7},{7,3},{8,12},{12,8},{9,1... | collective-permute-start | bytes 1179656 | tf_op jit(solution)/shard_map/ppermute | solution.py:492
  54.1 7.8 %collective-permute-start.22 = (f32[4,8,8,256]{3,2,1,0:T(8,128)S(1)}, f32[4,8,8,256]{3,2,1,0:T(8,128)S(1)}, u32[]{:S(2)}, u32[]{:S(2)}) collective-permute-start(f32[4,8,8,256]{3,2,1,0:T(8,128)S(1)} %get-tuple-element.128), channel_id=1, source_target_pairs={{0,4},{4,0},{1,5},{5,1},{2,6},{6,2},{3,7},{7,3},{8,12},{12,8},{9,1... | collective-permute-start | bytes 786440 | tf_op jit(solution)/shard_map/ppermute | solution.py:492
  56.2 2.6 %collective-permute-start.17 = (f32[4,8,128]{2,1,0:T(8,128)S(1)}, f32[4,8,128]{2,1,0:T(8,128)S(1)}, u32[]{:S(2)}, u32[]{:S(2)}) collective-permute-start(f32[4,8,128]{2,1,0:T(8,128)S(1)} %get-tuple-element.120.a_ref), channel_id=1, source_target_pairs={{0,1},{1,0},{2,3},{3,2},{4,5},{5,4},{6,7},{7,6},{8,9},{9,8},{10,11... | collective-permute-start | bytes 49160 | tf_op jit(solution)/shard_map/ppermute | solution.py:344
  58.8 4.3 %collective-permute-start.18 = (f32[4,8,128]{2,1,0:T(8,128)S(1)}, f32[4,8,128]{2,1,0:T(8,128)S(1)}, u32[]{:S(2)}, u32[]{:S(2)}) collective-permute-start(f32[4,8,128]{2,1,0:T(8,128)S(1)} %add.2.a_ref), channel_id=1, source_target_pairs={{0,2},{1,3},{2,0},{3,1},{4,6},{5,7},{6,4},{7,5},{8,10},{9,11},{10,... | collective-permute-start | bytes 49160 | tf_op jit(solution)/shard_map/ppermute | solution.py:344
  63.1 2.6 %collective-permute-start.23 = (f32[4,8,128]{2,1,0:T(8,128)S(1)}, f32[4,8,128]{2,1,0:T(8,128)S(1)}, u32[]{:S(2)}, u32[]{:S(2)}) collective-permute-start(f32[4,8,128]{2,1,0:T(8,128)S(1)} %add.3.sums_ref), channel_id=1, source_target_pairs={{0,4},{4,0},{1,5},{5,1},{2,6},{6,2},{3,7},{7,3},{8,12},{12,8},{9,1... | collective-permute-start | bytes 49160 | tf_op jit(solution)/shard_map/ppermute | solution.py:507

commit v6 on v5

--- a/solution.py
+++ b/solution.py
@@ -36,12 +36,13 @@
 PARAMS = pltpu.CompilerParams(vmem_limit_bytes=8 << 20)
 
 
-def neighbours(ref, i):
+def neighbours(ref, i, side=None):
     c = ref[i]
     up = jnp.concatenate([c[1:], pltpu.roll(c[:1], SUB - 1, 1)], axis=0)
     down = jnp.concatenate([pltpu.roll(c[-1:], 1, 1), c[:-1]], axis=0)
     nz = c.shape[-1]
-    side = pltpu.roll(c, 1, 2) + pltpu.roll(c, nz - 1, 2)
+    if side is None:
+        side = pltpu.roll(c, 1, 2) + pltpu.roll(c, nz - 1, 2)
     return (ref[i - 1] + ref[i + 1]) + (up + down) + side - 6.0 * c
 
 
@@ -54,9 +55,9 @@
     return LAPS if m % LAPS == 0 else 2
 
 
-def level_row(levels, m, y):
+def level_row(levels, m, y, side=None):
     below, off = levels[m - 1]
-    d = neighbours(below, y + off)
+    d = neighbours(below, y + off, side)
     kind = m % LAPS
     if kind == 1:
         return d
@@ -68,12 +69,32 @@
     return v + (time_step / (spacing * spacing)) * d
 
 
-def rows_of(levels, m, start, stop, into):
-    for i in range(stop[0] - start[0]):
+def ring_matrix(nz):
+    apart = jnp.abs(lax.broadcasted_iota(jnp.int32, (nz, nz), 0) - lax.broadcasted_iota(jnp.int32, (nz, nz), 1))
+    return jnp.where((apart == 1) | (apart == nz - 1), 1.0, 0.0).astype(jnp.bfloat16)
+
+
+def side_sums(ref, start, count, ring):
+    v = ref[pl.ds(start, count)]
+    flat = v.reshape(-1, v.shape[-1])
+    high = flat.astype(jnp.bfloat16)
+    low = (flat - high.astype(jnp.float32)).astype(jnp.bfloat16)
+    total = jnp.dot(high, ring, preferred_element_type=jnp.float32)
+    total = total + jnp.dot(low, ring, preferred_element_type=jnp.float32)
+    return total.reshape(v.shape)
+
+
+def rows_of(levels, m, start, stop, into, ring=None):
+    count = stop[0] - start[0]
+    sums = None
+    if ring is not None:
+        below, off = levels[1][m - 1]
+        sums = side_sums(below, start[1] + off, count, ring)
+    for i in range(count):
         for side in range(2):
             ref, off = into[side]
             y = start[side] + i
-            ref[y + off] = level_row(levels[side], m, y)
+            ref[y + off] = level_row(levels[side], m, y, sums[i] if side and ring is not None else None)
 
 
 def cut_kernel(whole_ref, half_ref, sems):
@@ -165,6 +186,7 @@
 
 def edge_kernel(rows, before, after, sends, early, slab_ref, low_ref, high_ref, *refs):
     count = after - before
+    ring = ring_matrix(low_ref.shape[-1])
     n = len(sends)
     refs = refs[:FIELD] + refs[FIELD + early :]
     send_rows(sends, slab_ref, refs[FIELD : FIELD + n])
@@ -190,17 +212,17 @@
     for m in range(1, FIELD):
         start = (m - after, rows - m + before)
         stop = (m - before, rows - m + after)
-        rows_of(sides, m, start, stop, (sides[0][m], sides[1][m]))
+        rows_of(sides, m, start, stop, (sides[0][m], sides[1][m]), ring)
     beyond = max(0, after - FIELD)
     kept = count - beyond
     if kept:
         low = FIELD - after + beyond
         high = rows - FIELD + before
         into = ((fields[0], -low), (fields[0], kept - high))
-        rows_of(sides, FIELD, (low, high), (low + kept, high + kept), into)
+        rows_of(sides, FIELD, (low, high), (low + kept, high + kept), into, ring)
     if beyond:
         into = ((fields[-1], beyond), (fields[-1], beyond - rows))
-        rows_of(sides, FIELD, (-beyond, rows), (0, rows + beyond), into)
+        rows_of(sides, FIELD, (-beyond, rows), (0, rows + beyond), into, ring)
 
 
 def keeping(gx):

time: 67.4 us -> 67 us (level)
  starting transfers between devices: 34.4 us -> 35.8 us
  Pallas kernels: 22.4 us -> 21.3 us
    pallas_call x4, Pallas kernels: 8.78 us -> 7.76 us  [per_device(): pl.pallas_call(functools.partial(edge_kernel, rows, a, b, ahead, len(earl...]
  transfers between devices with their start and end apart: 24 -> 24, of which waited for: 5 -> 5; matrix products, arithmetic and copies ran while one was open for 0% -> 0% of each run, Pallas kernels for 31% -> 29%
where the time goes in v6:
time: 67 us; the launch traced here: 66.8 us
  starting transfers between devices  35.8 us (53%)
  Pallas kernels  21.3 us (32%)
  waiting for transfers between devices  7.77 us (12%)
  local copies, waits for them, and re-layouts  1.41 us (2%)
    ppermute x4, starting transfers between devices, exchange(): from_chain.append(lax.ppermute(piece, ('chain', 'gx'), along_chain))  15.4 us
    ppermute x4, starting transfers between devices, halos_of(): lax.ppermute(low, 'gy', ring('gy', -1))  9.43 us
    pallas_call x4, Pallas kernels, per_device(): pl.pallas_call(functools.partial(edge_kernel, rows, a, b, ahead, len(earl...  7.76 us
    pallas_call x1, Pallas kernels, per_device(): pl.pallas_call(functools.partial(inner_kernel, rows, made[1]), out_shape=...  4.61 us
    ppermute x4, starting transfers between devices, per_device(): halfway += [lax.ppermute(send, 'gx', swap) for send in outs[1::2]]  3.12 us
    ppermute x4, waiting for transfers between devices, halos_of(): lax.ppermute(high, 'gy', ring('gy', 1))  2.88 us
    pallas_call x2, Pallas kernels, per_device(): pl.pallas_call(functools.partial(layout_kernel, segments, low), out_shape...  2.31 us
    ppermute x2, waiting for transfers between devices, total_over(): moved = lax.ppermute(start if n & n - 1 else value, axis, route)  2.21 us
  transfers between devices with their start and end apart: 24, of which 5 were waited for; matrix products, arithmetic and copies ran while one was open for 0% of the time, Pallas kernels for 29%

profile of v6, /device:TPU:5, one launch (start us, length us, event | category | flops | bytes accessed | tf_op | source)
XLA Modules:
  0.0 66.8 jit_solution(2226826183463559429)
XLA Ops:
  0.0 1.4 %copy-done = f32[2,32,24,256]{3,2,1,0:T(8,128)S(1)} copy-done((f32[2,32,24,256]{3,2,1,0:T(8,128)S(1)}, f32[2,32,24,256]{3,2,1,0:T(8,128)}, u32[]{:S(2)}) %copy-start) | copy-done | bytes 1572888
  1.4 0.1 cut.1
  1.5 0.7 %collective-permute-start = (f32[2,32,24,128]{3,2,1,0:T(8,128)S(1)}, f32[2,32,24,128]{3,2,1,0:T(8,128)S(1)}, u32[]{:S(2)}, u32[]{:S(2)}) collective-permute-start(f32[2,32,24,128]{3,2,1,0:T(8,128)S(1)} %cut.1), channel_id=1, source_target_pairs={{0,4},{4,0},{1,5},{5,1},{2,6},{6,2},{3,7},{7,3},{8,12},{12,8},{9,1... | collective-permute-start | bytes 2359304 | tf_op jit(solution)/shard_map/ppermute | solution.py:396
  2.2 0.7 own.1.own_ref
  2.9 1.3 %collective-permute-done.recv_ref = f32[2,32,24,128]{3,2,1,0:T(8,128)S(1)} collective-permute-done((f32[2,32,24,128]{3,2,1,0:T(8,128)S(1)}, f32[2,32,24,128]{3,2,1,0:T(8,128)S(1)}, u32[]{:S(2)}, u32[]{:S(2)}) %collective-permute-start) | collective-permute-done | bytes 786464 | tf_op jit(solution)/shard_map/ppermute | solution.py:396
  4.1 0.7 %first.1 = (f32[24,8,8,256]{3,2,1,0:T(8,128)S(1)}, f32[4,8,8,256]{3,2,1,0:T(8,128)S(1)}, f32[4,8,8,256]{3,2,1,0:T(8,128)S(1)}, f32[3,8,8,256]{3,2,1,0:T(8,128)S(...) custom-call(f32[24,8,8,256]{3,2,1,0:T(8,128)S(1)} %own.1.own_ref, ...), custom_call_target="tpu_custom_call" | custom-call | bytes 2340000 | tf_op jit(solution)/shard_map/first/pallas_call | solution.py:414
  4.9 1.3 %collective-permute-start.1 = (f32[4,8,8,256]{3,2,1,0:T(8,128)S(1)}, f32[4,8,8,256]{3,2,1,0:T(8,128)S(1)}, u32[]{:S(2)}, u32[]{:S(2)}) collective-permute-start(f32[4,8,8,256]{3,2,1,0:T(8,128)S(1)} %get-tuple-element.69), channel_id=1, source_target_pairs={{0,1},{1,2},{2,3},{3,0},{4,5},{5,6},{6,7},{7,4},{8,9},{9,10},{10,1... | collective-permute-start | bytes 786440 | tf_op jit(solution)/shard_map/ppermute | solution.py:435
  6.2 2.1 %collective-permute-start.2 = (f32[4,8,8,256]{3,2,1,0:T(8,128)S(1)}, f32[4,8,8,256]{3,2,1,0:T(8,128)S(1)}, u32[]{:S(2)}, u32[]{:S(2)}) collective-permute-start(f32[4,8,8,256]{3,2,1,0:T(8,128)S(1)} %get-tuple-element.70), channel_id=1, source_target_pairs={{0,3},{1,0},{2,1},{3,2},{4,7},{5,4},{6,5},{7,6},{8,11},{9,8},{10,9... | collective-permute-start | bytes 786440 | tf_op jit(solution)/shard_map/ppermute | solution.py:436
  8.3 4.6 %inner.1 = (f32[22,8,8,256]{3,2,1,0:T(8,128)S(1)}, f32[20,8,8,256]{3,2,1,0:T(8,128)S(1)}, f32[18,8,8,256]{3,2,1,0:T(8,128)S(1)}, f32[16,8,8,256]{3,2,1,0:T(8,128...) custom-call(f32[24,8,8,256]{3,2,1,0:T(8,128)S(1)} %get-tuple-element, ...), custom_call_target="tpu_custom_call" | custom-call | bytes 16380000 | tf_op jit(solution)/shard_map/inner/pallas_call | solution.py:441
  12.9 3.8 %collective-permute-start.5 = (f32[6,8,8,256]{3,2,1,0:T(8,128)S(1)}, f32[6,8,8,256]{3,2,1,0:T(8,128)S(1)}, u32[]{:S(2)}, u32[]{:S(2)}) collective-permute-start(f32[6,8,8,256]{3,2,1,0:T(8,128)S(1)} %get-tuple-element.68.refs_0_), channel_id=1, source_target_pairs={{4,8},{8,4},{12,16},{16,12},{20,24},{24,20},{5,9},{9,5},{13,17},{1... | collective-permute-start | bytes 1179656 | tf_op jit(solution)/shard_map/ppermute | solution.py:429
  16.7 0.1 collective-permute-start.3
  16.8 3.3 %collective-permute-start.4 = (f32[3,8,8,256]{3,2,1,0:T(8,128)S(1)}, f32[3,8,8,256]{3,2,1,0:T(8,128)S(1)}, u32[]{:S(2)}, u32[]{:S(2)}) collective-permute-start(f32[3,8,8,256]{3,2,1,0:T(8,128)S(1)} %get-tuple-element.81), channel_id=1, source_target_pairs={{0,3},{1,0},{2,1},{3,2},{4,7},{5,4},{6,5},{7,6},{8,11},{9,8},{10,9... | collective-permute-start | bytes 589832 | tf_op jit(solution)/shard_map/ppermute | solution.py:436
  20.1 0.0 collective-permute-done.1.low_ref
  20.1 0.0 collective-permute-done.2.high_ref
  20.1 2.5 %edge.4 = (f32[8,8,8,256]{3,2,1,0:T(8,128)S(1)}, f32[14,8,8,256]{3,2,1,0:T(8,128)S(1)}, f32[12,8,8,256]{3,2,1,0:T(8,128)S(1)}, f32[12,8,8,256]{3,2,1,0:T(8,128)S...) custom-call(f32[24,8,8,256]{3,2,1,0:T(8,128)S(1)} %get-tuple-element, ...), custom_call_target="tpu_custom_call" | custom-call | bytes 9360000 | tf_op jit(solution)/shard_map/edge/pallas_call | solution.py:466
  22.6 4.9 %collective-permute-start.9 = (f32[8,8,8,256]{3,2,1,0:T(8,128)S(1)}, f32[8,8,8,256]{3,2,1,0:T(8,128)S(1)}, u32[]{:S(2)}, u32[]{:S(2)}) collective-permute-start(f32[8,8,8,256]{3,2,1,0:T(8,128)S(1)} %get-tuple-element.79.refs_1_), channel_id=1, source_target_pairs={{4,8},{8,4},{12,16},{16,12},{20,24},{24,20},{5,9},{9,5},{13,17},{1... | collective-permute-start | bytes 1572872 | tf_op jit(solution)/shard_map/ppermute | solution.py:429
  27.5 0.3 collective-permute-start.13
  27.8 3.0 %collective-permute-start.14 = (f32[2,8,8,256]{3,2,1,0:T(8,128)S(1)}, f32[2,8,8,256]{3,2,1,0:T(8,128)S(1)}, u32[]{:S(2)}, u32[]{:S(2)}) collective-permute-start(f32[2,8,8,256]{3,2,1,0:T(8,128)S(1)} %get-tuple-element.95), channel_id=1, source_target_pairs={{0,3},{1,0},{2,1},{3,2},{4,7},{5,4},{6,5},{7,6},{8,11},{9,8},{10,9... | collective-permute-start | bytes 393224 | tf_op jit(solution)/shard_map/ppermute | solution.py:436
  30.8 0.0 collective-permute-done.5.refs_9_.refs_6_
  30.8 0.6 collective-permute-start.7
  31.4 2.0 %edge.5 = (f32[6,8,8,256]{3,2,1,0:T(8,128)S(1)}, f32[12,8,8,256]{3,2,1,0:T(8,128)S(1)}, f32[10,8,8,256]{3,2,1,0:T(8,128)S(1)}, f32[10,8,8,256]{3,2,1,0:T(8,128)S...) custom-call(f32[24,8,8,256]{3,2,1,0:T(8,128)S(1)} %get-tuple-element, ...), custom_call_target="tpu_custom_call" | custom-call | bytes 7020000 | tf_op jit(solution)/shard_map/edge/pallas_call | solution.py:466
  33.4 1.2 %collective-permute-done.13.low_ref = f32[2,8,8,256]{3,2,1,0:T(8,128)S(1)} collective-permute-done((f32[2,8,8,256]{3,2,1,0:T(8,128)S(1)}, f32[2,8,8,256]{3,2,1,0:T(8,128)S(1)}, u32[]{:S(2)}, u32[]{:S(2)}) %collective-permute-start.13) | collective-permute-done | bytes 131104 | tf_op jit(solution)/shard_map/ppermute | solution.py:435
  34.6 2.9 %collective-permute-start.10 = (f32[6,8,8,256]{3,2,1,0:T(8,128)S(1)}, f32[6,8,8,256]{3,2,1,0:T(8,128)S(1)}, u32[]{:S(2)}, u32[]{:S(2)}) collective-permute-start(f32[6,8,8,256]{3,2,1,0:T(8,128)S(1)} %get-tuple-element.91.refs_2_), channel_id=1, source_target_pairs={{4,8},{8,4},{12,16},{16,12},{20,24},{24,20},{5,9},{9,5},{13,17},{1... | collective-permute-start | bytes 1179656 | tf_op jit(solution)/shard_map/ppermute | solution.py:429
  37.5 0.0 collective-permute-done.14.high_ref
  37.5 0.1 collective-permute-start.6
  37.6 1.7 %collective-permute-done.11.low_ref = f32[2,8,8,256]{3,2,1,0:T(8,128)S(1)} collective-permute-done((f32[2,8,8,256]{3,2,1,0:T(8,128)S(1)}, f32[2,8,8,256]{3,2,1,0:T(8,128)S(1)}, u32[]{:S(2)}, u32[]{:S(2)}) %collective-permute-start.11) | collective-permute-done | bytes 131104 | tf_op jit(solution)/shard_map/ppermute | solution.py:435
  39.2 0.3 collective-permute-start.8
  39.5 1.1 %collective-permute-start.12 = (f32[2,8,8,256]{3,2,1,0:T(8,128)S(1)}, f32[2,8,8,256]{3,2,1,0:T(8,128)S(1)}, u32[]{:S(2)}, u32[]{:S(2)}) collective-permute-start(f32[2,8,8,256]{3,2,1,0:T(8,128)S(1)} %get-tuple-element.93), channel_id=1, source_target_pairs={{0,3},{1,0},{2,1},{3,2},{4,7},{5,4},{6,5},{7,6},{8,11},{9,8},{10,9... | collective-permute-start | bytes 393224 | tf_op jit(solution)/shard_map/ppermute | solution.py:436
  40.6 1.7 %edge.6 = (f32[4,8,8,256]{3,2,1,0:T(8,128)S(1)}, f32[10,8,8,256]{3,2,1,0:T(8,128)S(1)}, f32[8,8,8,256]{3,2,1,0:T(8,128)S(1)}, f32[8,8,8,256]{3,2,1,0:T(8,128)S(1...) custom-call(f32[24,8,8,256]{3,2,1,0:T(8,128)S(1)} %get-tuple-element, ...), custom_call_target="tpu_custom_call" | custom-call | bytes 4680000 | tf_op jit(solution)/shard_map/edge/pallas_call | solution.py:466
  42.3 1.4 %collective-permute-done.12.high_ref = f32[2,8,8,256]{3,2,1,0:T(8,128)S(1)} collective-permute-done((f32[2,8,8,256]{3,2,1,0:T(8,128)S(1)}, f32[2,8,8,256]{3,2,1,0:T(8,128)S(1)}, u32[]{:S(2)}, u32[]{:S(2)}) %collective-permute-start.12) | collective-permute-done | bytes 131104 | tf_op jit(solution)/shard_map/ppermute | solution.py:436
  43.7 3.8 %collective-permute-start.16 = (f32[4,8,8,256]{3,2,1,0:T(8,128)S(1)}, f32[4,8,8,256]{3,2,1,0:T(8,128)S(1)}, u32[]{:S(2)}, u32[]{:S(2)}) collective-permute-start(f32[4,8,8,256]{3,2,1,0:T(8,128)S(1)} %get-tuple-element.114.refs_3_.refs_0_), channel_id=1, source_target_pairs={{4,8},{8,4},{12,16},{16,12},{20,24},{24,20},{5,9},{9,5},{13,17},{1... | collective-permute-start | bytes 786440 | tf_op jit(solution)/shard_map/ppermute | solution.py:429
  47.5 0.6 collective-permute-start.15
  48.1 1.6 %edge.7.halo_ref = f32[4,8,8,256]{3,2,1,0:T(8,128)S(1)} custom-call(f32[24,8,8,256]{3,2,1,0:T(8,128)S(1)} %get-tuple-element.67.slab_ref.refs_0_, f32[2,8,8,256]{3,2,1,0:T(8,128)S(1)} %collective-permute-done.11.low_ref, f32[2,8,8,256]{3,2,1,0:T(8,128)S(1)} %collective-permute-done.12.high_ref, f32[10,8,8,256]{3,2,1,0:T(8,128)S(1)} %get-tuple-element.105.refs_0_, ...), custom_call_target="tpu_custom_call" | custom-call | bytes 4680000 | tf_op jit(solution)/shard_map/edge/pallas_call | solution.py:466
  49.8 2.0 %chemical.1 = (f32[6,8,8,256]{3,2,1,0:T(8,128)S(1)}, f32[8,8,8,256]{3,2,1,0:T(8,128)S(1)}, f32[6,8,8,256]{3,2,1,0:T(8,128)S(1)}, f32[4,8,8,256]{3,2,1,0:T(8,128)S(1)}) custom-call(f32[4,8,8,256]{3,2,1,0:T(8,128)S(1)} %edge.7.halo_ref, f32[6,8,8,256]{3,2,1,0:T(8,128)S(1)} %get-tuple-element.68.refs_0_, f32[8,8,8,256]{3,2,1,0:T(8,128)S(1)} %get-tuple-element.79.refs_1_, ...), custom_call_target="tpu_custom_call" | custom-call | bytes 6240000 | tf_op jit(solution)/shard_map/chemical/pallas_call | solution.py:485
  51.8 0.9 %sums.2 = (f32[4,8,128]{2,1,0:T(8,128)S(1)}, f32[6,8,8,256]{3,2,1,0:T(8,128)S(1)}, f32[6,8,8,256]{3,2,1,0:T(8,128)S(1)}, f32[8,8,8,256]{3,2,1,0:T(8,128)S(1)}, f...) custom-call(f32[6,8,8,256]{3,2,1,0:T(8,128)S(1)} %get-tuple-element.68.refs_0_, ...), custom_call_target="tpu_custom_call" | custom-call | bytes 1560000 | tf_op jit(solution)/shard_map/sums/pallas_call | solution.py:503
  52.7 0.1 collective-permute-start.20
  52.8 0.5 collective-permute-start.19
  53.3 0.1 collective-permute-start.21
  53.4 0.2 sums.3
  53.6 2.5 %collective-permute-start.22 = (f32[4,8,8,256]{3,2,1,0:T(8,128)S(1)}, f32[4,8,8,256]{3,2,1,0:T(8,128)S(1)}, u32[]{:S(2)}, u32[]{:S(2)}) collective-permute-start(f32[4,8,8,256]{3,2,1,0:T(8,128)S(1)} %get-tuple-element.128), channel_id=1, source_target_pairs={{0,4},{4,0},{1,5},{5,1},{2,6},{6,2},{3,7},{7,3},{8,12},{12,8},{9,1... | collective-permute-start | bytes 786440 | tf_op jit(solution)/shard_map/ppermute | solution.py:514
  56.0 0.4 collective-permute-start.17
  56.4 2.2 %collective-permute-done.17.b_ref = f32[4,8,128]{2,1,0:T(8,128)S(1)} collective-permute-done((f32[4,8,128]{2,1,0:T(8,128)S(1)}, f32[4,8,128]{2,1,0:T(8,128)S(1)}, u32[]{:S(2)}, u32[]{:S(2)}) %collective-permute-start.17) | collective-permute-done | bytes 16416 | tf_op jit(solution)/shard_map/ppermute | solution.py:366
  58.6 1.7 %collective-permute-start.18 = (f32[4,8,128]{2,1,0:T(8,128)S(1)}, f32[4,8,128]{2,1,0:T(8,128)S(1)}, u32[]{:S(2)}, u32[]{:S(2)}) collective-permute-start(f32[4,8,128]{2,1,0:T(8,128)S(1)} %add.2.a_ref), channel_id=1, source_target_pairs={{0,2},{1,3},{2,0},{3,1},{4,6},{5,7},{6,4},{7,5},{8,10},{9,11},{10,... | collective-permute-start | bytes 49160 | tf_op jit(solution)/shard_map/ppermute | solution.py:366
  60.3 1.2 %layout.2.refs_0_.pair_ref = f32[2,32,24,256]{3,2,1,0:T(8,128)S(1)} custom-call(f32[6,8,8,256]{3,2,1,0:T(8,128)S(1)} %get-tuple-element.121.refs_0_, f32[8,8,8,256]{3,2,1,0:T(8,128)S(1)} %get-tuple-element.122.refs_1_, f32[6,8,8,256]{3,2,1,0:T(8,128)S(1)} %get-tuple-element.123.refs_2_, f32[4,8,8,256]{3,2,1,0:T(8,128)S(1)} %get-tuple-element.124.refs_3_), custom_call_target="tpu_custom_call" | custom-call | bytes 3120000 | tf_op jit(solution)/shard_map/layout/pallas_call | solution.py:516
  61.5 1.2 %layout.3.refs_1_.pair_ref = f32[2,32,24,256]{3,2,1,0:T(8,128)S(1)} custom-call(f32[6,8,8,256]{3,2,1,0:T(8,128)S(1)} %collective-permute-done.19.refs_0_, f32[8,8,8,256]{3,2,1,0:T(8,128)S(1)} %collective-permute-done.20.refs_1_, f32[6,8,8,256]{3,2,1,0:T(8,128)S(1)} %collective-permute-done.21.refs_2_, f32[4,8,8,256]{3,2,1,0:T(8,128)S(1)} %collective-permute-done.22.refs_3_), custom_call_target="tpu_custom_call" | custom-call | bytes 3120000 | tf_op jit(solution)/shard_map/layout/pallas_call | solution.py:516
  62.7 1.8 %collective-permute-start.23 = (f32[4,8,128]{2,1,0:T(8,128)S(1)}, f32[4,8,128]{2,1,0:T(8,128)S(1)}, u32[]{:S(2)}, u32[]{:S(2)}) collective-permute-start(f32[4,8,128]{2,1,0:T(8,128)S(1)} %add.3.sums_ref), channel_id=1, source_target_pairs={{0,4},{4,0},{1,5},{5,1},{2,6},{6,2},{3,7},{7,3},{8,12},{12,8},{9,1... | collective-permute-start | bytes 49160 | tf_op jit(solution)/shard_map/ppermute | solution.py:529
  64.5 1.1 %last.2.refs_0_ = f32[2,32,24,256]{3,2,1,0:T(8,128)} custom-call(f32[4,8,128]{2,1,0:T(8,128)S(1)} %add.3.sums_ref, f32[2,32,24,256]{3,2,1,0:T(8,128)S(1)} %layout.2.refs_0_.pair_ref), custom_call_target="tpu_custom_call" | custom-call | bytes 3120000 | tf_op jit(solution)/shard_map/last/pallas_call | solution.py:532
  65.6 1.1 %last.3 = f32[2,32,24,256]{3,2,1,0:T(8,128)} custom-call(f32[4,8,128]{2,1,0:T(8,128)S(1)} %collective-permute-done.23.sums_ref, f32[2,32,24,256]{3,2,1,0:T(8,128)S(1)} %layout.3.refs_1_.pair_ref, f32[2,32,24,256]{3,2,1,0:T(8,128)} %last.2.refs_0_), custom_call_target="tpu_custom_call", output_to_operand_aliasing={{}: (2, {})} | custom-call | bytes 3120000 | tf_op jit(solution)/shard_map/last/pallas_call | solution.py:532
  (19 shorter events, 0.1 us)
Async XLA Ops:
  0.0 1.4 %copy-start = (f32[2,32,24,256]{3,2,1,0:T(8,128)S(1)}, f32[2,32,24,256]{3,2,1,0:T(8,128)}, u32[]{:S(2)}) copy-start(f32[2,32,24,256]{3,2,1,0:T(8,128)} %whole_ref.3) | copy-start | bytes 4718596
  1.5 2.7 %collective-permute-start = (f32[2,32,24,128]{3,2,1,0:T(8,128)S(1)}, f32[2,32,24,128]{3,2,1,0:T(8,128)S(1)}, u32[]{:S(2)}, u32[]{:S(2)}) collective-permute-start(f32[2,32,24,128]{3,2,1,0:T(8,128)S(1)} %cut.1), channel_id=1, source_target_pairs={{0,4},{4,0},{1,5},{5,1},{2,6},{6,2},{3,7},{7,3},{8,12},{12,8},{9,1... | collective-permute-start | bytes 2359304 | tf_op jit(solution)/shard_map/ppermute | solution.py:396
  4.9 15.2 %collective-permute-start.1 = (f32[4,8,8,256]{3,2,1,0:T(8,128)S(1)}, f32[4,8,8,256]{3,2,1,0:T(8,128)S(1)}, u32[]{:S(2)}, u32[]{:S(2)}) collective-permute-start(f32[4,8,8,256]{3,2,1,0:T(8,128)S(1)} %get-tuple-element.69), channel_id=1, source_target_pairs={{0,1},{1,2},{2,3},{3,0},{4,5},{5,6},{6,7},{7,4},{8,9},{9,10},{10,1... | collective-permute-start | bytes 786440 | tf_op jit(solution)/shard_map/ppermute | solution.py:435
  6.2 13.9 %collective-permute-start.2 = (f32[4,8,8,256]{3,2,1,0:T(8,128)S(1)}, f32[4,8,8,256]{3,2,1,0:T(8,128)S(1)}, u32[]{:S(2)}, u32[]{:S(2)}) collective-permute-start(f32[4,8,8,256]{3,2,1,0:T(8,128)S(1)} %get-tuple-element.70), channel_id=1, source_target_pairs={{0,3},{1,0},{2,1},{3,2},{4,7},{5,4},{6,5},{7,6},{8,11},{9,8},{10,9... | collective-permute-start | bytes 786440 | tf_op jit(solution)/shard_map/ppermute | solution.py:436
  12.9 17.9 %collective-permute-start.5 = (f32[6,8,8,256]{3,2,1,0:T(8,128)S(1)}, f32[6,8,8,256]{3,2,1,0:T(8,128)S(1)}, u32[]{:S(2)}, u32[]{:S(2)}) collective-permute-start(f32[6,8,8,256]{3,2,1,0:T(8,128)S(1)} %get-tuple-element.68.refs_0_), channel_id=1, source_target_pairs={{4,8},{8,4},{12,16},{16,12},{20,24},{24,20},{5,9},{9,5},{13,17},{1... | collective-permute-start | bytes 1179656 | tf_op jit(solution)/shard_map/ppermute | solution.py:429
  16.7 11.1 %collective-permute-start.3 = (f32[3,8,8,256]{3,2,1,0:T(8,128)S(1)}, f32[3,8,8,256]{3,2,1,0:T(8,128)S(1)}, u32[]{:S(2)}, u32[]{:S(2)}) collective-permute-start(f32[3,8,8,256]{3,2,1,0:T(8,128)S(1)} %get-tuple-element.80), channel_id=1, source_target_pairs={{0,1},{1,2},{2,3},{3,0},{4,5},{5,6},{6,7},{7,4},{8,9},{9,10},{10,1... | collective-permute-start | bytes 589832 | tf_op jit(solution)/shard_map/ppermute | solution.py:435
  16.8 14.0 %collective-permute-start.4 = (f32[3,8,8,256]{3,2,1,0:T(8,128)S(1)}, f32[3,8,8,256]{3,2,1,0:T(8,128)S(1)}, u32[]{:S(2)}, u32[]{:S(2)}) collective-permute-start(f32[3,8,8,256]{3,2,1,0:T(8,128)S(1)} %get-tuple-element.81), channel_id=1, source_target_pairs={{0,3},{1,0},{2,1},{3,2},{4,7},{5,4},{6,5},{7,6},{8,11},{9,8},{10,9... | collective-permute-start | bytes 589832 | tf_op jit(solution)/shard_map/ppermute | solution.py:436
  22.6 17.0 %collective-permute-start.9 = (f32[8,8,8,256]{3,2,1,0:T(8,128)S(1)}, f32[8,8,8,256]{3,2,1,0:T(8,128)S(1)}, u32[]{:S(2)}, u32[]{:S(2)}) collective-permute-start(f32[8,8,8,256]{3,2,1,0:T(8,128)S(1)} %get-tuple-element.79.refs_1_), channel_id=1, source_target_pairs={{4,8},{8,4},{12,16},{16,12},{20,24},{24,20},{5,9},{9,5},{13,17},{1... | collective-permute-start | bytes 1572872 | tf_op jit(solution)/shard_map/ppermute | solution.py:429
  27.5 7.1 %collective-permute-start.13 = (f32[2,8,8,256]{3,2,1,0:T(8,128)S(1)}, f32[2,8,8,256]{3,2,1,0:T(8,128)S(1)}, u32[]{:S(2)}, u32[]{:S(2)}) collective-permute-start(f32[2,8,8,256]{3,2,1,0:T(8,128)S(1)} %get-tuple-element.94), channel_id=1, source_target_pairs={{0,1},{1,2},{2,3},{3,0},{4,5},{5,6},{6,7},{7,4},{8,9},{9,10},{10,1... | collective-permute-start | bytes 393224 | tf_op jit(solution)/shard_map/ppermute | solution.py:435
  27.8 9.7 %collective-permute-start.14 = (f32[2,8,8,256]{3,2,1,0:T(8,128)S(1)}, f32[2,8,8,256]{3,2,1,0:T(8,128)S(1)}, u32[]{:S(2)}, u32[]{:S(2)}) collective-permute-start(f32[2,8,8,256]{3,2,1,0:T(8,128)S(1)} %get-tuple-element.95), channel_id=1, source_target_pairs={{0,3},{1,0},{2,1},{3,2},{4,7},{5,4},{6,5},{7,6},{8,11},{9,8},{10,9... | collective-permute-start | bytes 393224 | tf_op jit(solution)/shard_map/ppermute | solution.py:436
  30.8 8.4 %collective-permute-start.11 = (f32[2,8,8,256]{3,2,1,0:T(8,128)S(1)}, f32[2,8,8,256]{3,2,1,0:T(8,128)S(1)}, u32[]{:S(2)}, u32[]{:S(2)}) collective-permute-start(f32[2,8,8,256]{3,2,1,0:T(8,128)S(1)} %get-tuple-element.92), channel_id=1, source_target_pairs={{0,1},{1,2},{2,3},{3,0},{4,5},{5,6},{6,7},{7,4},{8,9},{9,10},{10,1... | collective-permute-start | bytes 393224 | tf_op jit(solution)/shard_map/ppermute | solution.py:435
  30.8 21.0 %collective-permute-start.7 = (f32[8,8,8,256]{3,2,1,0:T(8,128)S(1)}, f32[8,8,8,256]{3,2,1,0:T(8,128)S(1)}, u32[]{:S(2)}, u32[]{:S(2)}) collective-permute-start(f32[8,8,8,256]{3,2,1,0:T(8,128)S(1)} %get-tuple-element.79.refs_1_), channel_id=1, source_target_pairs={{0,4},{4,0},{1,5},{5,1},{2,6},{6,2},{3,7},{7,3},{8,12},{12,8},{9,1... | collective-permute-start | bytes 1572872 | tf_op jit(solution)/shard_map/ppermute | solution.py:430
  34.6 12.9 %collective-permute-start.10 = (f32[6,8,8,256]{3,2,1,0:T(8,128)S(1)}, f32[6,8,8,256]{3,2,1,0:T(8,128)S(1)}, u32[]{:S(2)}, u32[]{:S(2)}) collective-permute-start(f32[6,8,8,256]{3,2,1,0:T(8,128)S(1)} %get-tuple-element.91.refs_2_), channel_id=1, source_target_pairs={{4,8},{8,4},{12,16},{16,12},{20,24},{24,20},{5,9},{9,5},{13,17},{1... | collective-permute-start | bytes 1179656 | tf_op jit(solution)/shard_map/ppermute | solution.py:429
  37.5 14.3 %collective-permute-start.6 = (f32[6,8,8,256]{3,2,1,0:T(8,128)S(1)}, f32[6,8,8,256]{3,2,1,0:T(8,128)S(1)}, u32[]{:S(2)}, u32[]{:S(2)}) collective-permute-start(f32[6,8,8,256]{3,2,1,0:T(8,128)S(1)} %get-tuple-element.68.refs_0_), channel_id=1, source_target_pairs={{0,4},{4,0},{1,5},{5,1},{2,6},{6,2},{3,7},{7,3},{8,12},{12,8},{9,1... | collective-permute-start | bytes 1179656 | tf_op jit(solution)/shard_map/ppermute | solution.py:430
  39.2 12.6 %collective-permute-start.8 = (f32[6,8,8,256]{3,2,1,0:T(8,128)S(1)}, f32[6,8,8,256]{3,2,1,0:T(8,128)S(1)}, u32[]{:S(2)}, u32[]{:S(2)}) collective-permute-start(f32[6,8,8,256]{3,2,1,0:T(8,128)S(1)} %get-tuple-element.91.refs_2_), channel_id=1, source_target_pairs={{0,4},{4,0},{1,5},{5,1},{2,6},{6,2},{3,7},{7,3},{8,12},{12,8},{9,1... | collective-permute-start | bytes 1179656 | tf_op jit(solution)/shard_map/ppermute | solution.py:430
  39.5 4.1 %collective-permute-start.12 = (f32[2,8,8,256]{3,2,1,0:T(8,128)S(1)}, f32[2,8,8,256]{3,2,1,0:T(8,128)S(1)}, u32[]{:S(2)}, u32[]{:S(2)}) collective-permute-start(f32[2,8,8,256]{3,2,1,0:T(8,128)S(1)} %get-tuple-element.93), channel_id=1, source_target_pairs={{0,3},{1,0},{2,1},{3,2},{4,7},{5,4},{6,5},{7,6},{8,11},{9,8},{10,9... | collective-permute-start | bytes 393224 | tf_op jit(solution)/shard_map/ppermute | solution.py:436
  43.7 9.7 %collective-permute-start.16 = (f32[4,8,8,256]{3,2,1,0:T(8,128)S(1)}, f32[4,8,8,256]{3,2,1,0:T(8,128)S(1)}, u32[]{:S(2)}, u32[]{:S(2)}) collective-permute-start(f32[4,8,8,256]{3,2,1,0:T(8,128)S(1)} %get-tuple-element.114.refs_3_.refs_0_), channel_id=1, source_target_pairs={{4,8},{8,4},{12,16},{16,12},{20,24},{24,20},{5,9},{9,5},{13,17},{1... | collective-permute-start | bytes 786440 | tf_op jit(solution)/shard_map/ppermute | solution.py:429
  47.5 5.9 %collective-permute-start.15 = (f32[4,8,8,256]{3,2,1,0:T(8,128)S(1)}, f32[4,8,8,256]{3,2,1,0:T(8,128)S(1)}, u32[]{:S(2)}, u32[]{:S(2)}) collective-permute-start(f32[4,8,8,256]{3,2,1,0:T(8,128)S(1)} %get-tuple-element.114.refs_3_.refs_0_), channel_id=1, source_target_pairs={{0,4},{4,0},{1,5},{5,1},{2,6},{6,2},{3,7},{7,3},{8,12},{12,8},{9,1... | collective-permute-start | bytes 786440 | tf_op jit(solution)/shard_map/ppermute | solution.py:430
  52.7 8.8 %collective-permute-start.20 = (f32[8,8,8,256]{3,2,1,0:T(8,128)S(1)}, f32[8,8,8,256]{3,2,1,0:T(8,128)S(1)}, u32[]{:S(2)}, u32[]{:S(2)}) collective-permute-start(f32[8,8,8,256]{3,2,1,0:T(8,128)S(1)} %get-tuple-element.126), channel_id=1, source_target_pairs={{0,4},{4,0},{1,5},{5,1},{2,6},{6,2},{3,7},{7,3},{8,12},{12,8},{9,1... | collective-permute-start | bytes 1572872 | tf_op jit(solution)/shard_map/ppermute | solution.py:514
  52.8 8.7 %collective-permute-start.19 = (f32[6,8,8,256]{3,2,1,0:T(8,128)S(1)}, f32[6,8,8,256]{3,2,1,0:T(8,128)S(1)}, u32[]{:S(2)}, u32[]{:S(2)}) collective-permute-start(f32[6,8,8,256]{3,2,1,0:T(8,128)S(1)} %get-tuple-element.125), channel_id=1, source_target_pairs={{0,4},{4,0},{1,5},{5,1},{2,6},{6,2},{3,7},{7,3},{8,12},{12,8},{9,1... | collective-permute-start | bytes 1179656 | tf_op jit(solution)/shard_map/ppermute | solution.py:514
  53.3 8.2 %collective-permute-start.21 = (f32[6,8,8,256]{3,2,1,0:T(8,128)S(1)}, f32[6,8,8,256]{3,2,1,0:T(8,128)S(1)}, u32[]{:S(2)}, u32[]{:S(2)}) collective-permute-start(f32[6,8,8,256]{3,2,1,0:T(8,128)S(1)} %get-tuple-element.127), channel_id=1, source_target_pairs={{0,4},{4,0},{1,5},{5,1},{2,6},{6,2},{3,7},{7,3},{8,12},{12,8},{9,1... | collective-permute-start | bytes 1179656 | tf_op jit(solution)/shard_map/ppermute | solution.py:514
  53.6 7.9 %collective-permute-start.22 = (f32[4,8,8,256]{3,2,1,0:T(8,128)S(1)}, f32[4,8,8,256]{3,2,1,0:T(8,128)S(1)}, u32[]{:S(2)}, u32[]{:S(2)}) collective-permute-start(f32[4,8,8,256]{3,2,1,0:T(8,128)S(1)} %get-tuple-element.128), channel_id=1, source_target_pairs={{0,4},{4,0},{1,5},{5,1},{2,6},{6,2},{3,7},{7,3},{8,12},{12,8},{9,1... | collective-permute-start | bytes 786440 | tf_op jit(solution)/shard_map/ppermute | solution.py:514
  56.0 2.6 %collective-permute-start.17 = (f32[4,8,128]{2,1,0:T(8,128)S(1)}, f32[4,8,128]{2,1,0:T(8,128)S(1)}, u32[]{:S(2)}, u32[]{:S(2)}) collective-permute-start(f32[4,8,128]{2,1,0:T(8,128)S(1)} %get-tuple-element.120.a_ref), channel_id=1, source_target_pairs={{0,1},{1,0},{2,3},{3,2},{4,5},{5,4},{6,7},{7,6},{8,9},{9,8},{10,11... | collective-permute-start | bytes 49160 | tf_op jit(solution)/shard_map/ppermute | solution.py:366
  58.6 4.1 %collective-permute-start.18 = (f32[4,8,128]{2,1,0:T(8,128)S(1)}, f32[4,8,128]{2,1,0:T(8,128)S(1)}, u32[]{:S(2)}, u32[]{:S(2)}) collective-permute-start(f32[4,8,128]{2,1,0:T(8,128)S(1)} %add.2.a_ref), channel_id=1, source_target_pairs={{0,2},{1,3},{2,0},{3,1},{4,6},{5,7},{6,4},{7,5},{8,10},{9,11},{10,... | collective-permute-start | bytes 49160 | tf_op jit(solution)/shard_map/ppermute | solution.py:366
  62.7 2.9 %collective-permute-start.23 = (f32[4,8,128]{2,1,0:T(8,128)S(1)}, f32[4,8,128]{2,1,0:T(8,128)S(1)}, u32[]{:S(2)}, u32[]{:S(2)}) collective-permute-start(f32[4,8,128]{2,1,0:T(8,128)S(1)} %add.3.sums_ref), channel_id=1, source_target_pairs={{0,4},{4,0},{1,5},{5,1},{2,6},{6,2},{3,7},{7,3},{8,12},{12,8},{9,1... | collective-permute-start | bytes 49160 | tf_op jit(solution)/shard_map/ppermute | solution.py:529

commit v7 on v6

--- a/solution.py
+++ b/solution.py
@@ -176,12 +176,13 @@
 
 def inner_kernel(rows, sends, slab_ref, *refs):
     outs = refs[:FIELD]
+    ring = ring_matrix(slab_ref.shape[-1])
     send_rows(sends, slab_ref, refs[FIELD:])
     levels = [(slab_ref, 0)] + [(ref, -m) for m, ref in enumerate(outs, 1)]
     for m in range(1, FIELD + 1):
         count = (rows - 2 * m) // 2
         start, stop = (m, m + count), (m + count, rows - m)
-        rows_of((levels, levels), m, start, stop, (levels[m], levels[m]))
+        rows_of((levels, levels), m, start, stop, (levels[m], levels[m]), ring)
 
 
 def edge_kernel(rows, before, after, sends, early, slab_ref, low_ref, high_ref, *refs):

time: 67 us -> 67.2 us (level)
  Pallas kernels: 21.3 us -> 20.4 us
  starting transfers between devices: 35.8 us -> 36.5 us
    pallas_call x1, Pallas kernels: 4.61 us -> 3.68 us  [per_device(): pl.pallas_call(functools.partial(inner_kernel, rows, made[1]), out_shape=...]
    ppermute x4, starting transfers between devices: 15.4 us -> 16.3 us  [exchange(): from_chain.append(lax.ppermute(piece, ('chain', 'gx'), along_chain))]
  transfers between devices with their start and end apart: 24 -> 24, of which waited for: 5 -> 6; matrix products, arithmetic and copies ran while one was open for 0% -> 0% of each run, Pallas kernels for 29% -> 28%
where the time goes in v7:
time: 67.2 us; the launch traced here: 67 us
  starting transfers between devices  36.5 us (54%)
  Pallas kernels  20.4 us (30%)
  waiting for transfers between devices  8.2 us (12%)
  local copies, waits for them, and re-layouts  1.41 us (2%)
    ppermute x4, starting transfers between devices, exchange(): from_chain.append(lax.ppermute(piece, ('chain', 'gx'), along_chain))  16.3 us
    ppermute x4, starting transfers between devices, halos_of(): lax.ppermute(low, 'gy', ring('gy', -1))  9.28 us
    pallas_call x4, Pallas kernels, per_device(): pl.pallas_call(functools.partial(edge_kernel, rows, a, b, ahead, len(earl...  7.76 us
    pallas_call x1, Pallas kernels, per_device(): pl.pallas_call(functools.partial(inner_kernel, rows, made[1]), out_shape=...  3.68 us
    ppermute x4, starting transfers between devices, per_device(): halfway += [lax.ppermute(send, 'gx', swap) for send in outs[1::2]]  2.78 us
    ppermute x2, waiting for transfers between devices, total_over(): moved = lax.ppermute(start if n & n - 1 else value, axis, route)  2.59 us
    ppermute x4, waiting for transfers between devices, halos_of(): lax.ppermute(high, 'gy', ring('gy', 1))  2.46 us
    pallas_call x2, Pallas kernels, per_device(): pl.pallas_call(functools.partial(layout_kernel, segments, low), out_shape...  2.31 us
  transfers between devices with their start and end apart: 24, of which 6 were waited for; matrix products, arithmetic and copies ran while one was open for 0% of the time, Pallas kernels for 28%

profile of v7, /device:TPU:5, one launch (start us, length us, event | category | flops | bytes accessed | tf_op | source)
XLA Modules:
  0.0 67.0 jit_solution(10212137150496041808)
XLA Ops:
  0.0 1.4 %copy-done = f32[2,32,24,256]{3,2,1,0:T(8,128)S(1)} copy-done((f32[2,32,24,256]{3,2,1,0:T(8,128)S(1)}, f32[2,32,24,256]{3,2,1,0:T(8,128)}, u32[]{:S(2)}) %copy-start) | copy-done | bytes 1572888
  1.4 0.1 cut.1
  1.5 0.7 %collective-permute-start = (f32[2,32,24,128]{3,2,1,0:T(8,128)S(1)}, f32[2,32,24,128]{3,2,1,0:T(8,128)S(1)}, u32[]{:S(2)}, u32[]{:S(2)}) collective-permute-start(f32[2,32,24,128]{3,2,1,0:T(8,128)S(1)} %cut.1), channel_id=1, source_target_pairs={{0,4},{4,0},{1,5},{5,1},{2,6},{6,2},{3,7},{7,3},{8,12},{12,8},{9,1... | collective-permute-start | bytes 2359304 | tf_op jit(solution)/shard_map/ppermute | solution.py:397
  2.2 0.7 own.1.own_ref
  2.9 1.3 %collective-permute-done.recv_ref = f32[2,32,24,128]{3,2,1,0:T(8,128)S(1)} collective-permute-done((f32[2,32,24,128]{3,2,1,0:T(8,128)S(1)}, f32[2,32,24,128]{3,2,1,0:T(8,128)S(1)}, u32[]{:S(2)}, u32[]{:S(2)}) %collective-permute-start) | collective-permute-done | bytes 786464 | tf_op jit(solution)/shard_map/ppermute | solution.py:397
  4.1 0.7 %first.1 = (f32[24,8,8,256]{3,2,1,0:T(8,128)S(1)}, f32[4,8,8,256]{3,2,1,0:T(8,128)S(1)}, f32[4,8,8,256]{3,2,1,0:T(8,128)S(1)}, f32[3,8,8,256]{3,2,1,0:T(8,128)S(...) custom-call(f32[24,8,8,256]{3,2,1,0:T(8,128)S(1)} %own.1.own_ref, ...), custom_call_target="tpu_custom_call" | custom-call | bytes 2340000 | tf_op jit(solution)/shard_map/first/pallas_call | solution.py:415
  4.9 1.3 %collective-permute-start.1 = (f32[4,8,8,256]{3,2,1,0:T(8,128)S(1)}, f32[4,8,8,256]{3,2,1,0:T(8,128)S(1)}, u32[]{:S(2)}, u32[]{:S(2)}) collective-permute-start(f32[4,8,8,256]{3,2,1,0:T(8,128)S(1)} %get-tuple-element.69), channel_id=1, source_target_pairs={{0,1},{1,2},{2,3},{3,0},{4,5},{5,6},{6,7},{7,4},{8,9},{9,10},{10,1... | collective-permute-start | bytes 786440 | tf_op jit(solution)/shard_map/ppermute | solution.py:436
  6.2 2.1 %collective-permute-start.2 = (f32[4,8,8,256]{3,2,1,0:T(8,128)S(1)}, f32[4,8,8,256]{3,2,1,0:T(8,128)S(1)}, u32[]{:S(2)}, u32[]{:S(2)}) collective-permute-start(f32[4,8,8,256]{3,2,1,0:T(8,128)S(1)} %get-tuple-element.70), channel_id=1, source_target_pairs={{0,3},{1,0},{2,1},{3,2},{4,7},{5,4},{6,5},{7,6},{8,11},{9,8},{10,9... | collective-permute-start | bytes 786440 | tf_op jit(solution)/shard_map/ppermute | solution.py:437
  8.3 3.7 %inner.1 = (f32[22,8,8,256]{3,2,1,0:T(8,128)S(1)}, f32[20,8,8,256]{3,2,1,0:T(8,128)S(1)}, f32[18,8,8,256]{3,2,1,0:T(8,128)S(1)}, f32[16,8,8,256]{3,2,1,0:T(8,128...) custom-call(f32[24,8,8,256]{3,2,1,0:T(8,128)S(1)} %get-tuple-element, ...), custom_call_target="tpu_custom_call" | custom-call | bytes 16380000 | tf_op jit(solution)/shard_map/inner/pallas_call | solution.py:442
  12.0 3.8 %collective-permute-start.5 = (f32[6,8,8,256]{3,2,1,0:T(8,128)S(1)}, f32[6,8,8,256]{3,2,1,0:T(8,128)S(1)}, u32[]{:S(2)}, u32[]{:S(2)}) collective-permute-start(f32[6,8,8,256]{3,2,1,0:T(8,128)S(1)} %get-tuple-element.68.refs_0_), channel_id=1, source_target_pairs={{4,8},{8,4},{12,16},{16,12},{20,24},{24,20},{5,9},{9,5},{13,17},{1... | collective-permute-start | bytes 1179656 | tf_op jit(solution)/shard_map/ppermute | solution.py:430
  15.8 0.1 collective-permute-start.3
  15.9 3.3 %collective-permute-start.4 = (f32[3,8,8,256]{3,2,1,0:T(8,128)S(1)}, f32[3,8,8,256]{3,2,1,0:T(8,128)S(1)}, u32[]{:S(2)}, u32[]{:S(2)}) collective-permute-start(f32[3,8,8,256]{3,2,1,0:T(8,128)S(1)} %get-tuple-element.81), channel_id=1, source_target_pairs={{0,3},{1,0},{2,1},{3,2},{4,7},{5,4},{6,5},{7,6},{8,11},{9,8},{10,9... | collective-permute-start | bytes 589832 | tf_op jit(solution)/shard_map/ppermute | solution.py:437
  19.1 0.0 collective-permute-done.1.low_ref
  19.1 0.3 collective-permute-done.2.high_ref
  19.5 2.5 %edge.4 = (f32[8,8,8,256]{3,2,1,0:T(8,128)S(1)}, f32[14,8,8,256]{3,2,1,0:T(8,128)S(1)}, f32[12,8,8,256]{3,2,1,0:T(8,128)S(1)}, f32[12,8,8,256]{3,2,1,0:T(8,128)S...) custom-call(f32[24,8,8,256]{3,2,1,0:T(8,128)S(1)} %get-tuple-element, ...), custom_call_target="tpu_custom_call" | custom-call | bytes 9360000 | tf_op jit(solution)/shard_map/edge/pallas_call | solution.py:467
  22.0 5.5 %collective-permute-start.9 = (f32[8,8,8,256]{3,2,1,0:T(8,128)S(1)}, f32[8,8,8,256]{3,2,1,0:T(8,128)S(1)}, u32[]{:S(2)}, u32[]{:S(2)}) collective-permute-start(f32[8,8,8,256]{3,2,1,0:T(8,128)S(1)} %get-tuple-element.79.refs_1_), channel_id=1, source_target_pairs={{4,8},{8,4},{12,16},{16,12},{20,24},{24,20},{5,9},{9,5},{13,17},{1... | collective-permute-start | bytes 1572872 | tf_op jit(solution)/shard_map/ppermute | solution.py:430
  27.5 0.3 collective-permute-start.13
  27.8 3.0 %collective-permute-start.14 = (f32[2,8,8,256]{3,2,1,0:T(8,128)S(1)}, f32[2,8,8,256]{3,2,1,0:T(8,128)S(1)}, u32[]{:S(2)}, u32[]{:S(2)}) collective-permute-start(f32[2,8,8,256]{3,2,1,0:T(8,128)S(1)} %get-tuple-element.95), channel_id=1, source_target_pairs={{0,3},{1,0},{2,1},{3,2},{4,7},{5,4},{6,5},{7,6},{8,11},{9,8},{10,9... | collective-permute-start | bytes 393224 | tf_op jit(solution)/shard_map/ppermute | solution.py:437
  30.8 0.0 collective-permute-done.4.high_ref
  30.8 0.0 collective-permute-start.11
  30.8 0.6 collective-permute-start.7
  31.4 2.0 %edge.5 = (f32[6,8,8,256]{3,2,1,0:T(8,128)S(1)}, f32[12,8,8,256]{3,2,1,0:T(8,128)S(1)}, f32[10,8,8,256]{3,2,1,0:T(8,128)S(1)}, f32[10,8,8,256]{3,2,1,0:T(8,128)S...) custom-call(f32[24,8,8,256]{3,2,1,0:T(8,128)S(1)} %get-tuple-element, ...), custom_call_target="tpu_custom_call" | custom-call | bytes 7020000 | tf_op jit(solution)/shard_map/edge/pallas_call | solution.py:467
  33.4 1.2 %collective-permute-done.13.low_ref = f32[2,8,8,256]{3,2,1,0:T(8,128)S(1)} collective-permute-done((f32[2,8,8,256]{3,2,1,0:T(8,128)S(1)}, f32[2,8,8,256]{3,2,1,0:T(8,128)S(1)}, u32[]{:S(2)}, u32[]{:S(2)}) %collective-permute-start.13) | collective-permute-done | bytes 131104 | tf_op jit(solution)/shard_map/ppermute | solution.py:436
  34.5 3.3 %collective-permute-start.10 = (f32[6,8,8,256]{3,2,1,0:T(8,128)S(1)}, f32[6,8,8,256]{3,2,1,0:T(8,128)S(1)}, u32[]{:S(2)}, u32[]{:S(2)}) collective-permute-start(f32[6,8,8,256]{3,2,1,0:T(8,128)S(1)} %get-tuple-element.91.refs_2_), channel_id=1, source_target_pairs={{4,8},{8,4},{12,16},{16,12},{20,24},{24,20},{5,9},{9,5},{13,17},{1... | collective-permute-start | bytes 1179656 | tf_op jit(solution)/shard_map/ppermute | solution.py:430
  37.8 0.1 collective-permute-start.6
  37.9 1.3 %collective-permute-done.11.low_ref = f32[2,8,8,256]{3,2,1,0:T(8,128)S(1)} collective-permute-done((f32[2,8,8,256]{3,2,1,0:T(8,128)S(1)}, f32[2,8,8,256]{3,2,1,0:T(8,128)S(1)}, u32[]{:S(2)}, u32[]{:S(2)}) %collective-permute-start.11) | collective-permute-done | bytes 131104 | tf_op jit(solution)/shard_map/ppermute | solution.py:436
  39.2 0.3 collective-permute-start.8
  39.5 0.9 %collective-permute-start.12 = (f32[2,8,8,256]{3,2,1,0:T(8,128)S(1)}, f32[2,8,8,256]{3,2,1,0:T(8,128)S(1)}, u32[]{:S(2)}, u32[]{:S(2)}) collective-permute-start(f32[2,8,8,256]{3,2,1,0:T(8,128)S(1)} %get-tuple-element.93), channel_id=1, source_target_pairs={{0,3},{1,0},{2,1},{3,2},{4,7},{5,4},{6,5},{7,6},{8,11},{9,8},{10,9... | collective-permute-start | bytes 393224 | tf_op jit(solution)/shard_map/ppermute | solution.py:437
  40.5 1.7 %edge.6 = (f32[4,8,8,256]{3,2,1,0:T(8,128)S(1)}, f32[10,8,8,256]{3,2,1,0:T(8,128)S(1)}, f32[8,8,8,256]{3,2,1,0:T(8,128)S(1)}, f32[8,8,8,256]{3,2,1,0:T(8,128)S(1...) custom-call(f32[24,8,8,256]{3,2,1,0:T(8,128)S(1)} %get-tuple-element, ...), custom_call_target="tpu_custom_call" | custom-call | bytes 4680000 | tf_op jit(solution)/shard_map/edge/pallas_call | solution.py:467
  42.1 1.5 %collective-permute-done.12.high_ref = f32[2,8,8,256]{3,2,1,0:T(8,128)S(1)} collective-permute-done((f32[2,8,8,256]{3,2,1,0:T(8,128)S(1)}, f32[2,8,8,256]{3,2,1,0:T(8,128)S(1)}, u32[]{:S(2)}, u32[]{:S(2)}) %collective-permute-start.12) | collective-permute-done | bytes 131104 | tf_op jit(solution)/shard_map/ppermute | solution.py:437
  43.6 3.8 %collective-permute-start.16 = (f32[4,8,8,256]{3,2,1,0:T(8,128)S(1)}, f32[4,8,8,256]{3,2,1,0:T(8,128)S(1)}, u32[]{:S(2)}, u32[]{:S(2)}) collective-permute-start(f32[4,8,8,256]{3,2,1,0:T(8,128)S(1)} %get-tuple-element.114.refs_3_.refs_0_), channel_id=1, source_target_pairs={{4,8},{8,4},{12,16},{16,12},{20,24},{24,20},{5,9},{9,5},{13,17},{1... | collective-permute-start | bytes 786440 | tf_op jit(solution)/shard_map/ppermute | solution.py:430
  47.4 1.2 %collective-permute-start.15 = (f32[4,8,8,256]{3,2,1,0:T(8,128)S(1)}, f32[4,8,8,256]{3,2,1,0:T(8,128)S(1)}, u32[]{:S(2)}, u32[]{:S(2)}) collective-permute-start(f32[4,8,8,256]{3,2,1,0:T(8,128)S(1)} %get-tuple-element.114.refs_3_.refs_0_), channel_id=1, source_target_pairs={{0,4},{4,0},{1,5},{5,1},{2,6},{6,2},{3,7},{7,3},{8,12},{12,8},{9,1... | collective-permute-start | bytes 786440 | tf_op jit(solution)/shard_map/ppermute | solution.py:431
  48.6 1.6 %edge.7.halo_ref = f32[4,8,8,256]{3,2,1,0:T(8,128)S(1)} custom-call(f32[24,8,8,256]{3,2,1,0:T(8,128)S(1)} %get-tuple-element.67.slab_ref.refs_0_, f32[2,8,8,256]{3,2,1,0:T(8,128)S(1)} %collective-permute-done.11.low_ref, f32[2,8,8,256]{3,2,1,0:T(8,128)S(1)} %collective-permute-done.12.high_ref, f32[10,8,8,256]{3,2,1,0:T(8,128)S(1)} %get-tuple-element.105.refs_0_, ...), custom_call_target="tpu_custom_call" | custom-call | bytes 4680000 | tf_op jit(solution)/shard_map/edge/pallas_call | solution.py:467
  50.2 2.0 %chemical.1 = (f32[6,8,8,256]{3,2,1,0:T(8,128)S(1)}, f32[8,8,8,256]{3,2,1,0:T(8,128)S(1)}, f32[6,8,8,256]{3,2,1,0:T(8,128)S(1)}, f32[4,8,8,256]{3,2,1,0:T(8,128)S(1)}) custom-call(f32[4,8,8,256]{3,2,1,0:T(8,128)S(1)} %edge.7.halo_ref, f32[6,8,8,256]{3,2,1,0:T(8,128)S(1)} %get-tuple-element.68.refs_0_, f32[8,8,8,256]{3,2,1,0:T(8,128)S(1)} %get-tuple-element.79.refs_1_, ...), custom_call_target="tpu_custom_call" | custom-call | bytes 6240000 | tf_op jit(solution)/shard_map/chemical/pallas_call | solution.py:486
  52.3 0.9 %sums.2 = (f32[4,8,128]{2,1,0:T(8,128)S(1)}, f32[6,8,8,256]{3,2,1,0:T(8,128)S(1)}, f32[6,8,8,256]{3,2,1,0:T(8,128)S(1)}, f32[8,8,8,256]{3,2,1,0:T(8,128)S(1)}, f...) custom-call(f32[6,8,8,256]{3,2,1,0:T(8,128)S(1)} %get-tuple-element.68.refs_0_, ...), custom_call_target="tpu_custom_call" | custom-call | bytes 1560000 | tf_op jit(solution)/shard_map/sums/pallas_call | solution.py:504
  53.2 0.1 collective-permute-start.20
  53.3 0.5 collective-permute-start.19
  53.8 0.1 collective-permute-start.21
  53.9 0.2 sums.3
  54.0 2.1 %collective-permute-start.22 = (f32[4,8,8,256]{3,2,1,0:T(8,128)S(1)}, f32[4,8,8,256]{3,2,1,0:T(8,128)S(1)}, u32[]{:S(2)}, u32[]{:S(2)}) collective-permute-start(f32[4,8,8,256]{3,2,1,0:T(8,128)S(1)} %get-tuple-element.128), channel_id=1, source_target_pairs={{0,4},{4,0},{1,5},{5,1},{2,6},{6,2},{3,7},{7,3},{8,12},{12,8},{9,1... | collective-permute-start | bytes 786440 | tf_op jit(solution)/shard_map/ppermute | solution.py:515
  56.2 0.0 collective-permute-start.17
  56.2 2.6 %collective-permute-done.17.b_ref = f32[4,8,128]{2,1,0:T(8,128)S(1)} collective-permute-done((f32[4,8,128]{2,1,0:T(8,128)S(1)}, f32[4,8,128]{2,1,0:T(8,128)S(1)}, u32[]{:S(2)}, u32[]{:S(2)}) %collective-permute-start.17) | collective-permute-done | bytes 16416 | tf_op jit(solution)/shard_map/ppermute | solution.py:367
  58.8 1.5 %collective-permute-start.18 = (f32[4,8,128]{2,1,0:T(8,128)S(1)}, f32[4,8,128]{2,1,0:T(8,128)S(1)}, u32[]{:S(2)}, u32[]{:S(2)}) collective-permute-start(f32[4,8,128]{2,1,0:T(8,128)S(1)} %add.2.a_ref), channel_id=1, source_target_pairs={{0,2},{1,3},{2,0},{3,1},{4,6},{5,7},{6,4},{7,5},{8,10},{9,11},{10,... | collective-permute-start | bytes 49160 | tf_op jit(solution)/shard_map/ppermute | solution.py:367
  60.3 1.2 %layout.2.refs_0_.pair_ref = f32[2,32,24,256]{3,2,1,0:T(8,128)S(1)} custom-call(f32[6,8,8,256]{3,2,1,0:T(8,128)S(1)} %get-tuple-element.121.refs_0_, f32[8,8,8,256]{3,2,1,0:T(8,128)S(1)} %get-tuple-element.122.refs_1_, f32[6,8,8,256]{3,2,1,0:T(8,128)S(1)} %get-tuple-element.123.refs_2_, f32[4,8,8,256]{3,2,1,0:T(8,128)S(1)} %get-tuple-element.124.refs_3_), custom_call_target="tpu_custom_call" | custom-call | bytes 3120000 | tf_op jit(solution)/shard_map/layout/pallas_call | solution.py:517
  61.5 1.2 %layout.3.refs_1_.pair_ref = f32[2,32,24,256]{3,2,1,0:T(8,128)S(1)} custom-call(f32[6,8,8,256]{3,2,1,0:T(8,128)S(1)} %collective-permute-done.19.refs_0_, f32[8,8,8,256]{3,2,1,0:T(8,128)S(1)} %collective-permute-done.20.refs_1_, f32[6,8,8,256]{3,2,1,0:T(8,128)S(1)} %collective-permute-done.21.refs_2_, f32[4,8,8,256]{3,2,1,0:T(8,128)S(1)} %collective-permute-done.22.refs_3_), custom_call_target="tpu_custom_call" | custom-call | bytes 3120000 | tf_op jit(solution)/shard_map/layout/pallas_call | solution.py:517
  62.7 1.9 %collective-permute-start.23 = (f32[4,8,128]{2,1,0:T(8,128)S(1)}, f32[4,8,128]{2,1,0:T(8,128)S(1)}, u32[]{:S(2)}, u32[]{:S(2)}) collective-permute-start(f32[4,8,128]{2,1,0:T(8,128)S(1)} %add.3.sums_ref), channel_id=1, source_target_pairs={{0,4},{4,0},{1,5},{5,1},{2,6},{6,2},{3,7},{7,3},{8,12},{12,8},{9,1... | collective-permute-start | bytes 49160 | tf_op jit(solution)/shard_map/ppermute | solution.py:530
  64.6 1.1 %last.2.refs_0_ = f32[2,32,24,256]{3,2,1,0:T(8,128)} custom-call(f32[4,8,128]{2,1,0:T(8,128)S(1)} %add.3.sums_ref, f32[2,32,24,256]{3,2,1,0:T(8,128)S(1)} %layout.2.refs_0_.pair_ref), custom_call_target="tpu_custom_call" | custom-call | bytes 3120000 | tf_op jit(solution)/shard_map/last/pallas_call | solution.py:533
  65.7 1.1 %last.3 = f32[2,32,24,256]{3,2,1,0:T(8,128)} custom-call(f32[4,8,128]{2,1,0:T(8,128)S(1)} %collective-permute-done.23.sums_ref, f32[2,32,24,256]{3,2,1,0:T(8,128)S(1)} %layout.3.refs_1_.pair_ref, f32[2,32,24,256]{3,2,1,0:T(8,128)} %last.2.refs_0_), custom_call_target="tpu_custom_call", output_to_operand_aliasing={{}: (2, {})} | custom-call | bytes 3120000 | tf_op jit(solution)/shard_map/last/pallas_call | solution.py:533
  (19 shorter events, 0.1 us)
Async XLA Ops:
  0.0 1.4 %copy-start = (f32[2,32,24,256]{3,2,1,0:T(8,128)S(1)}, f32[2,32,24,256]{3,2,1,0:T(8,128)}, u32[]{:S(2)}) copy-start(f32[2,32,24,256]{3,2,1,0:T(8,128)} %whole_ref.3) | copy-start | bytes 4718596
  1.5 2.7 %collective-permute-start = (f32[2,32,24,128]{3,2,1,0:T(8,128)S(1)}, f32[2,32,24,128]{3,2,1,0:T(8,128)S(1)}, u32[]{:S(2)}, u32[]{:S(2)}) collective-permute-start(f32[2,32,24,128]{3,2,1,0:T(8,128)S(1)} %cut.1), channel_id=1, source_target_pairs={{0,4},{4,0},{1,5},{5,1},{2,6},{6,2},{3,7},{7,3},{8,12},{12,8},{9,1... | collective-permute-start | bytes 2359304 | tf_op jit(solution)/shard_map/ppermute | solution.py:397
  4.9 14.3 %collective-permute-start.1 = (f32[4,8,8,256]{3,2,1,0:T(8,128)S(1)}, f32[4,8,8,256]{3,2,1,0:T(8,128)S(1)}, u32[]{:S(2)}, u32[]{:S(2)}) collective-permute-start(f32[4,8,8,256]{3,2,1,0:T(8,128)S(1)} %get-tuple-element.69), channel_id=1, source_target_pairs={{0,1},{1,2},{2,3},{3,0},{4,5},{5,6},{6,7},{7,4},{8,9},{9,10},{10,1... | collective-permute-start | bytes 786440 | tf_op jit(solution)/shard_map/ppermute | solution.py:436
  6.2 13.3 %collective-permute-start.2 = (f32[4,8,8,256]{3,2,1,0:T(8,128)S(1)}, f32[4,8,8,256]{3,2,1,0:T(8,128)S(1)}, u32[]{:S(2)}, u32[]{:S(2)}) collective-permute-start(f32[4,8,8,256]{3,2,1,0:T(8,128)S(1)} %get-tuple-element.70), channel_id=1, source_target_pairs={{0,3},{1,0},{2,1},{3,2},{4,7},{5,4},{6,5},{7,6},{8,11},{9,8},{10,9... | collective-permute-start | bytes 786440 | tf_op jit(solution)/shard_map/ppermute | solution.py:437
  12.0 18.8 %collective-permute-start.5 = (f32[6,8,8,256]{3,2,1,0:T(8,128)S(1)}, f32[6,8,8,256]{3,2,1,0:T(8,128)S(1)}, u32[]{:S(2)}, u32[]{:S(2)}) collective-permute-start(f32[6,8,8,256]{3,2,1,0:T(8,128)S(1)} %get-tuple-element.68.refs_0_), channel_id=1, source_target_pairs={{4,8},{8,4},{12,16},{16,12},{20,24},{24,20},{5,9},{9,5},{13,17},{1... | collective-permute-start | bytes 1179656 | tf_op jit(solution)/shard_map/ppermute | solution.py:430
  15.8 12.0 %collective-permute-start.3 = (f32[3,8,8,256]{3,2,1,0:T(8,128)S(1)}, f32[3,8,8,256]{3,2,1,0:T(8,128)S(1)}, u32[]{:S(2)}, u32[]{:S(2)}) collective-permute-start(f32[3,8,8,256]{3,2,1,0:T(8,128)S(1)} %get-tuple-element.80), channel_id=1, source_target_pairs={{0,1},{1,2},{2,3},{3,0},{4,5},{5,6},{6,7},{7,4},{8,9},{9,10},{10,1... | collective-permute-start | bytes 589832 | tf_op jit(solution)/shard_map/ppermute | solution.py:436
  15.9 14.9 %collective-permute-start.4 = (f32[3,8,8,256]{3,2,1,0:T(8,128)S(1)}, f32[3,8,8,256]{3,2,1,0:T(8,128)S(1)}, u32[]{:S(2)}, u32[]{:S(2)}) collective-permute-start(f32[3,8,8,256]{3,2,1,0:T(8,128)S(1)} %get-tuple-element.81), channel_id=1, source_target_pairs={{0,3},{1,0},{2,1},{3,2},{4,7},{5,4},{6,5},{7,6},{8,11},{9,8},{10,9... | collective-permute-start | bytes 589832 | tf_op jit(solution)/shard_map/ppermute | solution.py:437
  22.0 17.5 %collective-permute-start.9 = (f32[8,8,8,256]{3,2,1,0:T(8,128)S(1)}, f32[8,8,8,256]{3,2,1,0:T(8,128)S(1)}, u32[]{:S(2)}, u32[]{:S(2)}) collective-permute-start(f32[8,8,8,256]{3,2,1,0:T(8,128)S(1)} %get-tuple-element.79.refs_1_), channel_id=1, source_target_pairs={{4,8},{8,4},{12,16},{16,12},{20,24},{24,20},{5,9},{9,5},{13,17},{1... | collective-permute-start | bytes 1572872 | tf_op jit(solution)/shard_map/ppermute | solution.py:430
  27.5 7.1 %collective-permute-start.13 = (f32[2,8,8,256]{3,2,1,0:T(8,128)S(1)}, f32[2,8,8,256]{3,2,1,0:T(8,128)S(1)}, u32[]{:S(2)}, u32[]{:S(2)}) collective-permute-start(f32[2,8,8,256]{3,2,1,0:T(8,128)S(1)} %get-tuple-element.94), channel_id=1, source_target_pairs={{0,1},{1,2},{2,3},{3,0},{4,5},{5,6},{6,7},{7,4},{8,9},{9,10},{10,1... | collective-permute-start | bytes 393224 | tf_op jit(solution)/shard_map/ppermute | solution.py:436
  27.8 10.0 %collective-permute-start.14 = (f32[2,8,8,256]{3,2,1,0:T(8,128)S(1)}, f32[2,8,8,256]{3,2,1,0:T(8,128)S(1)}, u32[]{:S(2)}, u32[]{:S(2)}) collective-permute-start(f32[2,8,8,256]{3,2,1,0:T(8,128)S(1)} %get-tuple-element.95), channel_id=1, source_target_pairs={{0,3},{1,0},{2,1},{3,2},{4,7},{5,4},{6,5},{7,6},{8,11},{9,8},{10,9... | collective-permute-start | bytes 393224 | tf_op jit(solution)/shard_map/ppermute | solution.py:437
  30.8 8.4 %collective-permute-start.11 = (f32[2,8,8,256]{3,2,1,0:T(8,128)S(1)}, f32[2,8,8,256]{3,2,1,0:T(8,128)S(1)}, u32[]{:S(2)}, u32[]{:S(2)}) collective-permute-start(f32[2,8,8,256]{3,2,1,0:T(8,128)S(1)} %get-tuple-element.92), channel_id=1, source_target_pairs={{0,1},{1,2},{2,3},{3,0},{4,5},{5,6},{6,7},{7,4},{8,9},{9,10},{10,1... | collective-permute-start | bytes 393224 | tf_op jit(solution)/shard_map/ppermute | solution.py:436
  30.8 21.5 %collective-permute-start.7 = (f32[8,8,8,256]{3,2,1,0:T(8,128)S(1)}, f32[8,8,8,256]{3,2,1,0:T(8,128)S(1)}, u32[]{:S(2)}, u32[]{:S(2)}) collective-permute-start(f32[8,8,8,256]{3,2,1,0:T(8,128)S(1)} %get-tuple-element.79.refs_1_), channel_id=1, source_target_pairs={{0,4},{4,0},{1,5},{5,1},{2,6},{6,2},{3,7},{7,3},{8,12},{12,8},{9,1... | collective-permute-start | bytes 1572872 | tf_op jit(solution)/shard_map/ppermute | solution.py:431
  34.5 12.9 %collective-permute-start.10 = (f32[6,8,8,256]{3,2,1,0:T(8,128)S(1)}, f32[6,8,8,256]{3,2,1,0:T(8,128)S(1)}, u32[]{:S(2)}, u32[]{:S(2)}) collective-permute-start(f32[6,8,8,256]{3,2,1,0:T(8,128)S(1)} %get-tuple-element.91.refs_2_), channel_id=1, source_target_pairs={{4,8},{8,4},{12,16},{16,12},{20,24},{24,20},{5,9},{9,5},{13,17},{1... | collective-permute-start | bytes 1179656 | tf_op jit(solution)/shard_map/ppermute | solution.py:430
  37.8 14.4 %collective-permute-start.6 = (f32[6,8,8,256]{3,2,1,0:T(8,128)S(1)}, f32[6,8,8,256]{3,2,1,0:T(8,128)S(1)}, u32[]{:S(2)}, u32[]{:S(2)}) collective-permute-start(f32[6,8,8,256]{3,2,1,0:T(8,128)S(1)} %get-tuple-element.68.refs_0_), channel_id=1, source_target_pairs={{0,4},{4,0},{1,5},{5,1},{2,6},{6,2},{3,7},{7,3},{8,12},{12,8},{9,1... | collective-permute-start | bytes 1179656 | tf_op jit(solution)/shard_map/ppermute | solution.py:431
  39.2 13.1 %collective-permute-start.8 = (f32[6,8,8,256]{3,2,1,0:T(8,128)S(1)}, f32[6,8,8,256]{3,2,1,0:T(8,128)S(1)}, u32[]{:S(2)}, u32[]{:S(2)}) collective-permute-start(f32[6,8,8,256]{3,2,1,0:T(8,128)S(1)} %get-tuple-element.91.refs_2_), channel_id=1, source_target_pairs={{0,4},{4,0},{1,5},{5,1},{2,6},{6,2},{3,7},{7,3},{8,12},{12,8},{9,1... | collective-permute-start | bytes 1179656 | tf_op jit(solution)/shard_map/ppermute | solution.py:431
  39.5 4.1 %collective-permute-start.12 = (f32[2,8,8,256]{3,2,1,0:T(8,128)S(1)}, f32[2,8,8,256]{3,2,1,0:T(8,128)S(1)}, u32[]{:S(2)}, u32[]{:S(2)}) collective-permute-start(f32[2,8,8,256]{3,2,1,0:T(8,128)S(1)} %get-tuple-element.93), channel_id=1, source_target_pairs={{0,3},{1,0},{2,1},{3,2},{4,7},{5,4},{6,5},{7,6},{8,11},{9,8},{10,9... | collective-permute-start | bytes 393224 | tf_op jit(solution)/shard_map/ppermute | solution.py:437
  43.6 10.2 %collective-permute-start.16 = (f32[4,8,8,256]{3,2,1,0:T(8,128)S(1)}, f32[4,8,8,256]{3,2,1,0:T(8,128)S(1)}, u32[]{:S(2)}, u32[]{:S(2)}) collective-permute-start(f32[4,8,8,256]{3,2,1,0:T(8,128)S(1)} %get-tuple-element.114.refs_3_.refs_0_), channel_id=1, source_target_pairs={{4,8},{8,4},{12,16},{16,12},{20,24},{24,20},{5,9},{9,5},{13,17},{1... | collective-permute-start | bytes 786440 | tf_op jit(solution)/shard_map/ppermute | solution.py:430
  47.4 6.4 %collective-permute-start.15 = (f32[4,8,8,256]{3,2,1,0:T(8,128)S(1)}, f32[4,8,8,256]{3,2,1,0:T(8,128)S(1)}, u32[]{:S(2)}, u32[]{:S(2)}) collective-permute-start(f32[4,8,8,256]{3,2,1,0:T(8,128)S(1)} %get-tuple-element.114.refs_3_.refs_0_), channel_id=1, source_target_pairs={{0,4},{4,0},{1,5},{5,1},{2,6},{6,2},{3,7},{7,3},{8,12},{12,8},{9,1... | collective-permute-start | bytes 786440 | tf_op jit(solution)/shard_map/ppermute | solution.py:431
  53.2 8.3 %collective-permute-start.20 = (f32[8,8,8,256]{3,2,1,0:T(8,128)S(1)}, f32[8,8,8,256]{3,2,1,0:T(8,128)S(1)}, u32[]{:S(2)}, u32[]{:S(2)}) collective-permute-start(f32[8,8,8,256]{3,2,1,0:T(8,128)S(1)} %get-tuple-element.126), channel_id=1, source_target_pairs={{0,4},{4,0},{1,5},{5,1},{2,6},{6,2},{3,7},{7,3},{8,12},{12,8},{9,1... | collective-permute-start | bytes 1572872 | tf_op jit(solution)/shard_map/ppermute | solution.py:515
  53.3 8.2 %collective-permute-start.19 = (f32[6,8,8,256]{3,2,1,0:T(8,128)S(1)}, f32[6,8,8,256]{3,2,1,0:T(8,128)S(1)}, u32[]{:S(2)}, u32[]{:S(2)}) collective-permute-start(f32[6,8,8,256]{3,2,1,0:T(8,128)S(1)} %get-tuple-element.125), channel_id=1, source_target_pairs={{0,4},{4,0},{1,5},{5,1},{2,6},{6,2},{3,7},{7,3},{8,12},{12,8},{9,1... | collective-permute-start | bytes 1179656 | tf_op jit(solution)/shard_map/ppermute | solution.py:515
  53.8 7.7 %collective-permute-start.21 = (f32[6,8,8,256]{3,2,1,0:T(8,128)S(1)}, f32[6,8,8,256]{3,2,1,0:T(8,128)S(1)}, u32[]{:S(2)}, u32[]{:S(2)}) collective-permute-start(f32[6,8,8,256]{3,2,1,0:T(8,128)S(1)} %get-tuple-element.127), channel_id=1, source_target_pairs={{0,4},{4,0},{1,5},{5,1},{2,6},{6,2},{3,7},{7,3},{8,12},{12,8},{9,1... | collective-permute-start | bytes 1179656 | tf_op jit(solution)/shard_map/ppermute | solution.py:515
  54.0 7.5 %collective-permute-start.22 = (f32[4,8,8,256]{3,2,1,0:T(8,128)S(1)}, f32[4,8,8,256]{3,2,1,0:T(8,128)S(1)}, u32[]{:S(2)}, u32[]{:S(2)}) collective-permute-start(f32[4,8,8,256]{3,2,1,0:T(8,128)S(1)} %get-tuple-element.128), channel_id=1, source_target_pairs={{0,4},{4,0},{1,5},{5,1},{2,6},{6,2},{3,7},{7,3},{8,12},{12,8},{9,1... | collective-permute-start | bytes 786440 | tf_op jit(solution)/shard_map/ppermute | solution.py:515
  56.2 2.6 %collective-permute-start.17 = (f32[4,8,128]{2,1,0:T(8,128)S(1)}, f32[4,8,128]{2,1,0:T(8,128)S(1)}, u32[]{:S(2)}, u32[]{:S(2)}) collective-permute-start(f32[4,8,128]{2,1,0:T(8,128)S(1)} %get-tuple-element.120.a_ref), channel_id=1, source_target_pairs={{0,1},{1,0},{2,3},{3,2},{4,5},{5,4},{6,7},{7,6},{8,9},{9,8},{10,11... | collective-permute-start | bytes 49160 | tf_op jit(solution)/shard_map/ppermute | solution.py:367
  58.8 3.9 %collective-permute-start.18 = (f32[4,8,128]{2,1,0:T(8,128)S(1)}, f32[4,8,128]{2,1,0:T(8,128)S(1)}, u32[]{:S(2)}, u32[]{:S(2)}) collective-permute-start(f32[4,8,128]{2,1,0:T(8,128)S(1)} %add.2.a_ref), channel_id=1, source_target_pairs={{0,2},{1,3},{2,0},{3,1},{4,6},{5,7},{6,4},{7,5},{8,10},{9,11},{10,... | collective-permute-start | bytes 49160 | tf_op jit(solution)/shard_map/ppermute | solution.py:367
  62.7 3.0 %collective-permute-start.23 = (f32[4,8,128]{2,1,0:T(8,128)S(1)}, f32[4,8,128]{2,1,0:T(8,128)S(1)}, u32[]{:S(2)}, u32[]{:S(2)}) collective-permute-start(f32[4,8,128]{2,1,0:T(8,128)S(1)} %add.3.sums_ref), channel_id=1, source_target_pairs={{0,4},{4,0},{1,5},{5,1},{2,6},{6,2},{3,7},{7,3},{8,12},{12,8},{9,1... | collective-permute-start | bytes 49160 | tf_op jit(solution)/shard_map/ppermute | solution.py:530
